TPU v7x, 32 devices: a whole 2x2x4 slice. The times are simulated.
32 devices in a mesh: dp: 8 (over y, x, core), tensor: 4 (over z).
Axes of the slice: x: 2, y: 2, z: 4, core: 2. Of those that a mesh axis runs over, the one named last changes fastest.
Arguments:
- hidden_in: bfloat16 [8192, 1024], P(('dp', 'tensor')), may hold values from -6 to 6
- out_grad: bfloat16 [8192, 1024], P(('dp', 'tensor')), may hold values from -6 to 6
- positions: int32 [8192], P('dp'), may hold values from 0 to 1023, as said below
- query_weight: float32 [1024, 2048], P('dp', 'tensor'), may hold values from -0.1875 to 0.1875
- key_matrix: float32 [1024, 1024], P('dp', 'tensor'), may hold values from -0.1875 to 0.1875
- value_matrix: float32 [1024, 1024], P('dp', 'tensor'), may hold values from -0.1875 to 0.1875
- out_weight: float32 [2048, 1024], P('tensor', 'dp'), may hold values from -1 to 1
- gate_weight: float32 [1024, 3072], P('dp', 'tensor'), may hold values from -0.1875 to 0.1875
- up_weight: float32 [1024, 3072], P('dp', 'tensor'), may hold values from -0.1875 to 0.1875
- down_weight: float32 [3072, 1024], P('tensor', 'dp'), may hold values from -0.109375 to 0.109375
- query_moment: float32 [1024, 2048], P('dp', 'tensor'), may hold values from -814.58701 to 814.58701, as said below
- key_momentum: float32 [1024, 1024], P('dp', 'tensor'), may hold values from -814.58701 to 814.58701, as said below
- value_momentum: float32 [1024, 1024], P('dp', 'tensor'), may hold values from -1629.17402 to 1629.17402, as said below
- out_moment: float32 [2048, 1024], P('tensor', 'dp'), may hold values from -488.7522 to 488.7522, as said below
- gate_moment: float32 [1024, 3072], P('dp', 'tensor'), may hold values from -977.5044 to 977.5044, as said below
- up_moment: float32 [1024, 3072], P('dp', 'tensor'), may hold values from -977.5044 to 977.5044, as said below
- down_moment: float32 [3072, 1024], P('tensor', 'dp'), may hold values from -977.5044 to 977.5044, as said below
- gains: float32 [2304], replicated, may hold values from 0.5 to 1.5
- gain_first: float32 [2304], replicated, may hold values from -64 to 64
- gain_second: float32 [2304], replicated, may hold values from 212.992 to 3440.64
Outputs:
- block_out: float32 [8192, 1024], P(('dp', 'tensor'))
- input_grad: float32 [8192, 1024], P(('dp', 'tensor'))
- query_grad: float32 [1024, 2048], P('dp', 'tensor')
- key_grad: float32 [1024, 1024], P('dp', 'tensor')
- value_grad: float32 [1024, 1024], P('dp', 'tensor')
- out_weight_grad: float32 [2048, 1024], P('tensor', 'dp')
- gate_grad: float32 [1024, 3072], P('dp', 'tensor')
- up_grad: float32 [1024, 3072], P('dp', 'tensor')
- down_grad: float32 [3072, 1024], P('tensor', 'dp')
- query_new: float32 [1024, 2048], P('dp', 'tensor')
- key_new: float32 [1024, 1024], P('dp', 'tensor')
- value_new: float32 [1024, 1024], P('dp', 'tensor')
- out_weight_new: float32 [2048, 1024], P('tensor', 'dp')
- gate_new: float32 [1024, 3072], P('dp', 'tensor')
- up_new: float32 [1024, 3072], P('dp', 'tensor')
- down_new: float32 [3072, 1024], P('tensor', 'dp')
- query_moment_next: float32 [1024, 2048], P('dp', 'tensor')
- key_moment_next: float32 [1024, 1024], P('dp', 'tensor')
- value_moment_next: float32 [1024, 1024], P('dp', 'tensor')
- out_moment_next: float32 [2048, 1024], P('tensor', 'dp')
- gate_moment_next: float32 [1024, 3072], P('dp', 'tensor')
- up_moment_next: float32 [1024, 3072], P('dp', 'tensor')
- down_moment_next: float32 [3072, 1024], P('tensor', 'dp')
- gain_first_next: float32 [2304], replicated
- gain_second_next: float32 [2304], replicated
- gains_next: float32 [2304], replicated
Inputs may be any that keep to these rules, and one draw needn't show every extreme that they name: `positions`: the 1024 tokens of one index of dp form one packed sequence of documents; a token's value is its distance from the first token of its document, so it is 0 where a document begins (always at the group's first token) and rises by one from token to token otherwise. In every group the first document begins at the first token and ends within the last 256 tokens. `query_moment`: momentum entries, of both signs. `key_momentum`: momentum entries, of both signs. `value_momentum`: momentum entries, of both signs. `out_moment`: momentum entries, of both signs. `gate_moment`: momentum entries, of both signs. `up_moment`: momentum entries, of both signs. `down_moment`: momentum entries, of both signs.
All inputs are finite; a program needn't handle non-finite values.
Results may differ from a plain program's by a relative error of at most 0.02.
Values may be sent and summed in bfloat16 or wider, within the bound.
No kernel may reach another device: no remote copies, remote signals or barrier semaphores. Data moves between devices by JAX's collectives and lax.ppermute only.
A program may use at most 128 MiB of HBM per device.

v0:
```python
import math

import jax
import jax.numpy as jnp
from jax import lax
from jax.sharding import PartitionSpec as P

MODEL_WIDTH = 1024
QUERY_HEADS = 16
KEY_VALUE_HEADS = 8
HEAD_SIZE = 128
FF = 3072
NS_STEPS = 5
ADAM_STEP = 10


EPS_NORM = 1e-06
ROPE_BASE = 1000000.0
MASK_FILL = -1e30
MOMENTUM = 0.95
COEF_LINEAR = 3.4445
COEF_GRAM = -4.775
COEF_SQUARE = 2.0315
NS_EPS = 1e-07
DECAY_KEEP = 0.998
BETA_FIRST = 0.9
BETA_SECOND = 0.95
ADAM_EPS = 1e-08
GAIN_RATE = 0.6
HIGHEST = lax.Precision.HIGHEST


def for_sending(array):
    return jax.tree.map(lambda a: a.astype(jnp.bfloat16) if a.dtype == jnp.float32 else a, array)


def matmul(left, right):
    return jnp.dot(left, right, preferred_element_type=jnp.float32)


def contract_rows(left, right):
    return lax.dot_general(
        left, right, (((0,), (0,)), ((), ())), preferred_element_type=jnp.float32
    )


def contract_cols(left, right):
    return lax.dot_general(
        left, right, (((1,), (1,)), ((), ())), preferred_element_type=jnp.float32
    )


def rms_norm(values, gain):
    return values * lax.rsqrt(jnp.mean(values * values, axis=-1, keepdims=True) + EPS_NORM) * gain


def rotary(positions):
    half_width = HEAD_SIZE // 2
    inverse = jnp.power(
        jnp.float32(ROPE_BASE), -(jnp.arange(half_width, dtype=jnp.float32) * (2.0 / HEAD_SIZE))
    )
    angles = positions.astype(jnp.float32)[:, None] * inverse[None, :]
    cosine_part = jnp.cos(angles)
    sine_part = jnp.sin(angles)
    return (
        jnp.concatenate([cosine_part, cosine_part], axis=-1),
        jnp.concatenate([sine_part, sine_part], axis=-1),
    )


def rotate(values, cosine_part, sine_part):
    half_width = values.shape[-1] // 2
    turned = jnp.concatenate([-values[..., half_width:], values[..., :half_width]], axis=-1)
    return values * cosine_part[:, None, :] + turned * sine_part[:, None, :]


def on_device(
    hidden_in,
    out_grad,
    positions,
    query_weight,
    key_matrix,
    value_matrix,
    out_weight,
    gate_weight,
    up_weight,
    down_weight,
    query_moment,
    key_momentum,
    value_momentum,
    out_moment,
    gate_moment,
    up_moment,
    down_moment,
    gains,
    gain_first,
    gain_second,
):
    halves = (
        query_weight.astype(jnp.bfloat16),
        key_matrix.astype(jnp.bfloat16),
        value_matrix.astype(jnp.bfloat16),
        out_weight.astype(jnp.bfloat16),
        gate_weight.astype(jnp.bfloat16),
        up_weight.astype(jnp.bfloat16),
        down_weight.astype(jnp.bfloat16),
    )

    def fetch_weights():
        return (
            lax.all_gather(halves[0], "dp", axis=0, tiled=True),
            lax.all_gather(halves[1], "dp", axis=0, tiled=True),
            lax.all_gather(halves[2], "dp", axis=0, tiled=True),
            lax.all_gather(halves[3], "dp", axis=1, tiled=True),
            lax.all_gather(halves[4], "dp", axis=0, tiled=True),
            lax.all_gather(halves[5], "dp", axis=0, tiled=True),
            lax.all_gather(halves[6], "dp", axis=1, tiled=True),
        )

    query_full, key_full, value_full, out_full, gate_full, up_full, down_full = fetch_weights()
    gain_attn = gains[:MODEL_WIDTH]
    gain_mlp = gains[MODEL_WIDTH : 2 * MODEL_WIDTH]
    gain_query = gains[2 * MODEL_WIDTH : 2 * MODEL_WIDTH + HEAD_SIZE]
    gain_key = gains[2 * MODEL_WIDTH + HEAD_SIZE :]
    cosine_part, sine_part = rotary(positions)
    residual_in = hidden_in.astype(jnp.float32)
    normalized = rms_norm(residual_in, gain_attn).astype(jnp.bfloat16)

    def prepare_heads(pre_heads, gain):
        return rotate(rms_norm(pre_heads, gain), cosine_part, sine_part)

    attn_rows = lax.all_gather(normalized, "tensor", axis=0, tiled=True)
    all_rows = attn_rows.shape[0]
    heads_query = query_full.shape[1] // HEAD_SIZE
    heads_key = key_full.shape[1] // HEAD_SIZE
    group_size = heads_query // heads_key
    query_pre = matmul(attn_rows, query_full).reshape(all_rows, heads_query, HEAD_SIZE)
    key_before_rotary = matmul(attn_rows, key_full).reshape(all_rows, heads_key, HEAD_SIZE)
    value_heads = (
        matmul(attn_rows, value_full).reshape(all_rows, heads_key, HEAD_SIZE).astype(jnp.bfloat16)
    )
    query_head_rows = prepare_heads(query_pre, gain_query).astype(jnp.bfloat16)
    key_heads = prepare_heads(key_before_rotary, gain_key).astype(jnp.bfloat16)
    rows_per_block = min(512, all_rows)
    block_number = all_rows // rows_per_block
    score_scale = HEAD_SIZE ** (-0.5)
    query_block_list = query_head_rows.reshape(
        block_number, rows_per_block, heads_key, group_size, HEAD_SIZE
    )
    first_rows = jnp.arange(block_number, dtype=jnp.int32) * rows_per_block
    pos_blocks = positions.reshape(block_number, rows_per_block)

    def masked_scores(query_block, first_row, pos_block):
        scores = (
            jnp.einsum("qhgd,khd->hgqk", query_block, key_heads, preferred_element_type=jnp.float32)
            * score_scale
        )
        row_ids = first_row + jnp.arange(rows_per_block, dtype=jnp.int32)
        col_ids = jnp.arange(all_rows, dtype=jnp.int32)
        visible = (col_ids[None, :] <= row_ids[:, None]) & (
            row_ids[:, None] - col_ids[None, :] <= pos_block[:, None]
        )
        return jnp.where(visible[None, None], scores, MASK_FILL)

    def forward_block(inputs):
        query_block, first_row, pos_block = inputs
        masked = masked_scores(query_block, first_row, pos_block)
        row_max = jnp.max(masked, axis=-1, keepdims=True)
        log_total = row_max + jnp.log(jnp.sum(jnp.exp(masked - row_max), axis=-1, keepdims=True))
        weights = jnp.exp(masked - log_total).astype(jnp.bfloat16)
        return (
            jnp.einsum("hgqk,khd->qhgd", weights, value_heads, preferred_element_type=jnp.float32),
            log_total,
        )

    mixed_blocks, log_totals = lax.map(forward_block, (query_block_list, first_rows, pos_blocks))
    mixed_heads = mixed_blocks.reshape(all_rows, heads_query * HEAD_SIZE).astype(jnp.bfloat16)
    residual = residual_in + lax.psum_scatter(
        matmul(mixed_heads, out_full).astype(jnp.bfloat16),
        "tensor",
        scatter_dimension=0,
        tiled=True,
    ).astype(jnp.float32)
    normed_mlp = rms_norm(residual, gain_mlp).astype(jnp.bfloat16)
    mlp_rows = lax.all_gather(normed_mlp, "tensor", axis=0, tiled=True)
    gate_value = matmul(mlp_rows, gate_full)
    up_value = matmul(mlp_rows, up_full)
    activated = (jax.nn.silu(gate_value) * up_value).astype(jnp.bfloat16)
    block_out = residual + lax.psum_scatter(
        matmul(activated, down_full).astype(jnp.bfloat16), "tensor", scatter_dimension=0, tiled=True
    ).astype(jnp.float32)
    query_full, key_full, value_full, out_full, gate_full, up_full, down_full = fetch_weights()
    cot_rows = lax.all_gather(out_grad, "tensor", axis=0, tiled=True)
    d_activated = contract_cols(cot_rows, down_full)
    down_grad = contract_rows(activated, cot_rows)

    def swiglu(gate_in, up_in):
        return jax.nn.silu(gate_in) * up_in

    swiglu_out, swiglu_pull = jax.vjp(swiglu, gate_value, up_value)
    d_gate, d_up = swiglu_pull(d_activated)
    d_gate = d_gate.astype(jnp.bfloat16)
    d_up = d_up.astype(jnp.bfloat16)
    gate_grad = contract_rows(mlp_rows, d_gate)
    up_grad = contract_rows(mlp_rows, d_up)
    gate_part = contract_cols(d_gate, gate_full)
    d_normed_mlp = lax.psum_scatter(
        (gate_part + contract_cols(d_up, up_full)).astype(jnp.bfloat16),
        "tensor",
        scatter_dimension=0,
        tiled=True,
    ).astype(jnp.float32)
    norm_out, norm_pull = jax.vjp(rms_norm, residual, gain_mlp)
    d_residual_norm, d_gain_mlp = norm_pull(d_normed_mlp)
    d_residual = out_grad.astype(jnp.float32) + d_residual_norm
    state_rows = lax.all_gather(d_residual.astype(jnp.bfloat16), "tensor", axis=0, tiled=True)
    d_mixed = contract_cols(state_rows, out_full).astype(jnp.bfloat16)
    out_weight_grad = contract_rows(mixed_heads, state_rows)
    d_blocks = d_mixed.reshape(block_number, rows_per_block, heads_key, group_size, HEAD_SIZE)

    def backward_block(carry, inputs):
        query_block, first_row, pos_block, log_total, d_block = inputs
        probs = jnp.exp(masked_scores(query_block, first_row, pos_block) - log_total)
        d_probs = jnp.einsum(
            "qhgd,khd->hgqk", d_block, value_heads, preferred_element_type=jnp.float32
        )
        d_scores = (probs * (d_probs - jnp.sum(d_probs * probs, axis=-1, keepdims=True))).astype(
            jnp.bfloat16
        )
        d_query_block = (
            jnp.einsum("hgqk,khd->qhgd", d_scores, key_heads, preferred_element_type=jnp.float32)
            * score_scale
        )
        d_key_part = (
            jnp.einsum("hgqk,qhgd->khd", d_scores, query_block, preferred_element_type=jnp.float32)
            * score_scale
        )
        d_value_part = jnp.einsum(
            "hgqk,qhgd->khd",
            probs.astype(jnp.bfloat16),
            d_block,
            preferred_element_type=jnp.float32,
        )
        return ((carry[0] + d_key_part, carry[1] + d_value_part), d_query_block)

    zero_heads = jnp.zeros((all_rows, heads_key, HEAD_SIZE), jnp.float32)
    (d_key, d_value), d_query = lax.scan(
        backward_block,
        (zero_heads, zero_heads),
        (query_block_list, first_rows, pos_blocks, log_totals, d_blocks),
    )
    d_query = d_query.reshape(all_rows, heads_query, HEAD_SIZE)
    query_out, query_pull = jax.vjp(prepare_heads, query_pre, gain_query)
    d_query_pre, d_gain_query = query_pull(d_query)
    key_out, key_pull = jax.vjp(prepare_heads, key_before_rotary, gain_key)
    d_key_pre, d_gain_key = key_pull(d_key)
    d_query_pre = d_query_pre.reshape(all_rows, heads_query * HEAD_SIZE).astype(jnp.bfloat16)
    d_key_pre = d_key_pre.reshape(all_rows, heads_key * HEAD_SIZE).astype(jnp.bfloat16)
    d_value_pre = d_value.reshape(all_rows, heads_key * HEAD_SIZE).astype(jnp.bfloat16)
    query_grad = contract_rows(attn_rows, d_query_pre)
    key_grad = contract_rows(attn_rows, d_key_pre)
    value_grad = contract_rows(attn_rows, d_value_pre)
    query_part = contract_cols(d_query_pre, query_full)
    key_part = contract_cols(d_key_pre, key_full)
    d_normed = lax.psum_scatter(
        (query_part + key_part + contract_cols(d_value_pre, value_full)).astype(jnp.bfloat16),
        "tensor",
        scatter_dimension=0,
        tiled=True,
    ).astype(jnp.float32)
    input_out, input_pull = jax.vjp(rms_norm, residual_in, gain_attn)
    d_input_norm, d_gain_attn = input_pull(d_normed)
    input_grad = d_residual + d_input_norm
    gain_grad = lax.psum(
        jnp.concatenate([d_gain_attn, d_gain_mlp, d_gain_query, d_gain_key]), ("dp", "tensor")
    )
    reduced = (
        lax.psum_scatter(
            query_grad.astype(jnp.bfloat16), "dp", scatter_dimension=0, tiled=True
        ).astype(jnp.float32),
        lax.psum_scatter(
            key_grad.astype(jnp.bfloat16), "dp", scatter_dimension=0, tiled=True
        ).astype(jnp.float32),
        lax.psum_scatter(
            value_grad.astype(jnp.bfloat16), "dp", scatter_dimension=0, tiled=True
        ).astype(jnp.float32),
        lax.psum_scatter(
            out_weight_grad.astype(jnp.bfloat16), "dp", scatter_dimension=1, tiled=True
        ).astype(jnp.float32),
        lax.psum_scatter(
            gate_grad.astype(jnp.bfloat16), "dp", scatter_dimension=0, tiled=True
        ).astype(jnp.float32),
        lax.psum_scatter(
            up_grad.astype(jnp.bfloat16), "dp", scatter_dimension=0, tiled=True
        ).astype(jnp.float32),
        lax.psum_scatter(
            down_grad.astype(jnp.bfloat16), "dp", scatter_dimension=1, tiled=True
        ).astype(jnp.float32),
    )
    masters = (
        query_weight,
        key_matrix,
        value_matrix,
        out_weight,
        gate_weight,
        up_weight,
        down_weight,
    )
    moments = (
        query_moment,
        key_momentum,
        value_momentum,
        out_moment,
        gate_moment,
        up_moment,
        down_moment,
    )
    flipped = (False, False, False, True, False, False, True)
    fans = (
        MODEL_WIDTH,
        MODEL_WIDTH,
        MODEL_WIDTH,
        QUERY_HEADS * HEAD_SIZE // 64,
        MODEL_WIDTH,
        MODEL_WIDTH,
        FF,
    )
    full_shapes = (
        (MODEL_WIDTH, QUERY_HEADS * HEAD_SIZE),
        (MODEL_WIDTH, KEY_VALUE_HEADS * HEAD_SIZE),
        (MODEL_WIDTH, KEY_VALUE_HEADS * HEAD_SIZE),
        (QUERY_HEADS * HEAD_SIZE, MODEL_WIDTH),
        (MODEL_WIDTH, FF),
        (MODEL_WIDTH, FF),
        (FF, MODEL_WIDTH),
    )
    fresh = []
    oriented = []
    for number in range(7):
        moment_next = MOMENTUM * moments[number] + reduced[number]
        looked = reduced[number] + MOMENTUM * moment_next
        fresh.append(moment_next)
        oriented.append(looked.T if flipped[number] else looked)
    slot_rows = oriented[0].shape[0]
    slot_width = max((portion.shape[1] for portion in oriented))
    dp_count = lax.axis_size("dp")
    slots = jnp.zeros((dp_count, slot_rows, slot_width), jnp.float32)
    for number in range(7):
        padded = jnp.pad(oriented[number], ((0, 0), (0, slot_width - oriented[number].shape[1])))
        slots = slots.at[number * dp_count // 7].set(padded)
    owned = lax.all_to_all(
        slots.astype(jnp.bfloat16), "dp", split_axis=0, concat_axis=1, tiled=True
    ).astype(slots.dtype)[0]

    def gram_sum(matrix):
        local_gram = lax.dot_general(
            matrix,
            matrix,
            (((1,), (1,)), ((), ())),
            preferred_element_type=jnp.float32,
            precision=HIGHEST,
        )
        return lax.psum(local_gram.astype(jnp.bfloat16), "tensor").astype(jnp.float32)

    gram_matrix = gram_sum(owned)
    norm_size = jnp.sqrt(jnp.trace(gram_matrix)) + NS_EPS
    current = owned / norm_size
    gram_matrix = gram_matrix / (norm_size * norm_size)
    for sweep_number in range(NS_STEPS):
        if sweep_number > 0:
            gram_matrix = gram_sum(current)
        mixture = COEF_GRAM * gram_matrix + COEF_SQUARE * jnp.dot(
            gram_matrix, gram_matrix, preferred_element_type=jnp.float32, precision=HIGHEST
        )
        current = COEF_LINEAR * current + jnp.dot(
            mixture, current, preferred_element_type=jnp.float32, precision=HIGHEST
        )
    returned = lax.all_to_all(
        for_sending(current[None]), "dp", split_axis=1, concat_axis=0, tiled=True
    )
    updated = []
    for number in range(7):
        portion = returned[number * dp_count // 7][:, : oriented[number].shape[1]]
        if flipped[number]:
            portion = portion.T
        step_size = 0.5 * fans[number] ** (-0.5) * math.sqrt(max(full_shapes[number]))
        updated.append(DECAY_KEEP * masters[number] - step_size * portion)
    first_next = BETA_FIRST * gain_first + (1.0 - BETA_FIRST) * gain_grad
    second_next = BETA_SECOND * gain_second + (1.0 - BETA_SECOND) * gain_grad * gain_grad
    first_hat = first_next / (1.0 - BETA_FIRST**ADAM_STEP)
    second_hat = second_next / (1.0 - BETA_SECOND**ADAM_STEP)
    gains_next = gains - GAIN_RATE * first_hat / (jnp.sqrt(second_hat) + ADAM_EPS)
    return (
        block_out,
        input_grad,
        reduced[0],
        reduced[1],
        reduced[2],
        reduced[3],
        reduced[4],
        reduced[5],
        reduced[6],
        updated[0],
        updated[1],
        updated[2],
        updated[3],
        updated[4],
        updated[5],
        updated[6],
        fresh[0],
        fresh[1],
        fresh[2],
        fresh[3],
        fresh[4],
        fresh[5],
        fresh[6],
        first_next,
        second_next,
        gains_next,
    )


def solution(mesh):
    placed = (
        P(("dp", "tensor"), None),
        P(("dp", "tensor"), None),
        P("dp"),
        P("dp", "tensor"),
        P("dp", "tensor"),
        P("dp", "tensor"),
        P("tensor", "dp"),
        P("dp", "tensor"),
        P("dp", "tensor"),
        P("tensor", "dp"),
        P("dp", "tensor"),
        P("dp", "tensor"),
        P("dp", "tensor"),
        P("tensor", "dp"),
        P("dp", "tensor"),
        P("dp", "tensor"),
        P("tensor", "dp"),
        P(),
        P(),
        P(),
    )
    return jax.shard_map(
        on_device,
        mesh=mesh,
        in_specs=placed,
        out_specs=(
            P(("dp", "tensor"), None),
            P(("dp", "tensor"), None),
            P("dp", "tensor"),
            P("dp", "tensor"),
            P("dp", "tensor"),
            P("tensor", "dp"),
            P("dp", "tensor"),
            P("dp", "tensor"),
            P("tensor", "dp"),
            P("dp", "tensor"),
            P("dp", "tensor"),
            P("dp", "tensor"),
            P("tensor", "dp"),
            P("dp", "tensor"),
            P("dp", "tensor"),
            P("tensor", "dp"),
            P("dp", "tensor"),
            P("dp", "tensor"),
            P("dp", "tensor"),
            P("tensor", "dp"),
            P("dp", "tensor"),
            P("dp", "tensor"),
            P("tensor", "dp"),
            P(),
            P(),
            P(),
        ),
        check_vma=False,
    )
```

profile of v0, /device:TPU:0, one launch (start us, length us, event | category | flops | bytes accessed | tf_op | source)
XLA Modules:
  0.0 1491.2 jit_solution(10575486562067085032)
XLA Ops:
  14.5 11.3 all_gather.43
  25.8 9.8 all_gather.42
  36.6 4.0 multiply_cosine_fusion.1
  42.0 18.7 %all-gather.10.cloned.1.call-done = bf16[1024,1024]{1,0:T(8,128)(2,1)} async-done(((bf16[256,1024]{1,0:T(8,128)(2,1)}), bf16[1024,1024]{1,0:T(8,128)(2,1)}) %all-gather.10.cloned.1.call-update) | async-done | bytes 2097168 | tf_op jit(solution)/shard_map/all_gather | solution.py:132
  67.5 17.9 %all-gather.12.cloned.1.call-done = bf16[1024,512]{1,0:T(8,128)(2,1)} async-done(((bf16[128,512]{1,0:T(8,128)(2,1)}), bf16[1024,512]{1,0:T(8,128)(2,1)}) %all-gather.12.cloned.1.call-update) | async-done | bytes 1048592 | tf_op jit(solution)/shard_map/all_gather | solution.py:111
  94.0 3.3 concatenate.41
  100.3 4.2 fusion.89
  107.2 17.5 %while.34 = (s32[]{:T(128)}, bf16[2,512,2,2,128]{4,1,3,2,0:T(8,128)(2,1)S(1)}, f32[2,2,2,512,1]{3,2,1,4,0:T(2,128)S(1)}, s32[2]{0:T(128)S(1)}, s32[2,512]{1,0:T(...) while((s32[]{:T(128)}, ...), condition=%wide.region_6.7_spmd, body=%wide.region_3.6_spmd.sunk | while | flops 1098906112 | bytes 29960324 | solution.py:176
  129.2 4.1 convolution_convert_fusion.4
  135.1 42.3 %reduce-scatter.12.cloned.1.call-done = bf16[256,1024]{1,0:T(8,128)(2,1)} async-done(((bf16[1024,1024]{1,0:T(8,128)(2,1)}), bf16[256,1024]{1,0:T(8,128)(2,1)}) %reduce-scatter.12.cloned.1.call-update) | async-done | bytes 524304 | tf_op jit(solution)/shard_map/reduce_scatter | solution.py:178
  183.5 21.4 %all-gather.20.cloned.1.call-done = bf16[1024,768]{1,0:T(8,128)(2,1)} async-done(((bf16[128,768]{1,0:T(8,128)(2,1)}), bf16[1024,768]{1,0:T(8,128)(2,1)}) %all-gather.20.cloned.1.call-update) | async-done | bytes 1572880 | tf_op jit(solution)/shard_map/all_gather | solution.py:116
  204.9 48.0 %all-gather.16.cloned.1.call-done = bf16[1024,1024]{1,0:T(8,128)(2,1)} async-done(((bf16[256,1024]{1,0:T(8,128)(2,1)}), bf16[1024,1024]{1,0:T(8,128)(2,1)}) %all-gather.16.cloned.1.call-update) | async-done | bytes 2097168 | tf_op jit(solution)/shard_map/all_gather | solution.py:185
  252.9 5.5 fusion.154
  258.4 21.6 %all-gather.18.cloned.1.call-done = bf16[1024,768]{1,0:T(8,128)(2,1)} async-done(((bf16[128,768]{1,0:T(8,128)(2,1)}), bf16[1024,768]{1,0:T(8,128)(2,1)}) %all-gather.18.cloned.1.call-update) | async-done | bytes 1572880 | tf_op jit(solution)/shard_map/all_gather | solution.py:115
  280.0 5.5 fusion.153
  285.5 23.0 %all-gather.22.cloned.1.call-done = bf16[768,1024]{1,0:T(8,128)(2,1)} async-done(((bf16[768,128]{1,0:T(8,128)(2,1)}), bf16[768,1024]{1,0:T(8,128)(2,1)}) %all-gather.22.cloned.1.call-update) | async-done | bytes 1572880 | tf_op jit(solution)/shard_map/all_gather | solution.py:117
  308.5 47.6 %all-gather.24.cloned.1.call-done = bf16[1024,1024]{1,0:T(8,128)(2,1)} async-done(((bf16[256,1024]{1,0:T(8,128)(2,1)}), bf16[1024,1024]{1,0:T(8,128)(2,1)}) %all-gather.24.cloned.1.call-update) | async-done | bytes 2097168 | tf_op jit(solution)/shard_map/all_gather | solution.py:193
  356.1 8.0 multiply_convert_fusion
  369.9 42.7 %reduce-scatter.16.cloned.1.call-done = bf16[256,1024]{1,0:T(8,128)(2,1)} async-done(((bf16[1024,1024]{1,0:T(8,128)(2,1)}), bf16[256,1024]{1,0:T(8,128)(2,1)}) %reduce-scatter.16.cloned.1.call-update) | async-done | bytes 524304 | tf_op jit(solution)/shard_map/reduce_scatter | solution.py:207
  417.4 45.2 %all-gather.26.cloned.1.call-done = bf16[1024,1024]{1,0:T(8,128)(2,1)} async-done(((bf16[256,1024]{1,0:T(8,128)(2,1)}), bf16[1024,1024]{1,0:T(8,128)(2,1)}) %all-gather.26.cloned.1.call-update) | async-done | bytes 2097168 | tf_op jit(solution)/shard_map/all_gather | solution.py:216
  462.5 4.1 convolution_convert_fusion.12
  468.8 34.4 %while.35 = (s32[]{:T(128)}, f32[1024,2,128]{0,2,1:T(8,128)S(1)}, f32[1024,2,128]{0,2,1:T(8,128)}, f32[2,512,2,2,128]{4,1,0,3,2:T(8,128)}, bf16[2,512,2,2,128]{4...) while((s32[]{:T(128)}, f32[1024,2,128]{0,2,1:T(8,128)S(1)}, ...), condition=%wide.region_14.15_spmd.clone, body=%wide.region_12.14_spmd.clone.sunk | while | flops 2719480320 | bytes 100206888 | solution.py:247
  476.0 3.4 fusion.261
  493.2 3.4 fusion.261
  519.1 3.2 multiply_reduce_fusion
  526.3 3.9 convolution_convert_fusion.10
  530.3 5.2 convolution_convert_fusion.9
  535.5 4.4 convolution_convert_fusion.8
  540.1 5.1 convolution_convert_fusion.7
  548.0 33.7 %reduce-scatter.22.cloned.1.call-done = bf16[128,256]{1,0:T(8,128)(2,1)} async-done(((bf16[1024,256]{1,0:T(8,128)(2,1)}), bf16[128,256]{1,0:T(8,128)(2,1)}) %reduce-scatter.22.cloned.1.call-update) | async-done | bytes 65552 | tf_op jit(solution)/shard_map/reduce_scatter | solution.py:281
  583.3 38.1 %reduce-scatter.20.cloned.1.call-done = bf16[128,512]{1,0:T(8,128)(2,1)} async-done(((bf16[1024,512]{1,0:T(8,128)(2,1)}), bf16[128,512]{1,0:T(8,128)(2,1)}) %reduce-scatter.20.cloned.1.call-update) | async-done | bytes 131088 | tf_op jit(solution)/shard_map/reduce_scatter | solution.py:278
  623.3 37.6 %reduce-scatter.26.cloned.1.call-done = bf16[512,128]{0,1:T(8,128)(2,1)} async-done(((bf16[512,1024]{0,1:T(8,128)(2,1)}), bf16[512,128]{0,1:T(8,128)(2,1)}) %reduce-scatter.26.cloned.1.call-update) | async-done | bytes 131088 | tf_op jit(solution)/shard_map/reduce_scatter | solution.py:287
  661.9 40.7 %reduce-scatter.28.cloned.1.call-done = bf16[128,768]{1,0:T(8,128)(2,1)} async-done(((bf16[1024,768]{1,0:T(8,128)(2,1)}), bf16[128,768]{1,0:T(8,128)(2,1)}) %reduce-scatter.28.cloned.1.call-update) | async-done | bytes 196624 | tf_op jit(solution)/shard_map/reduce_scatter | solution.py:290
  704.6 39.6 %reduce-scatter.30.cloned.1.call-done = bf16[128,768]{1,0:T(8,128)(2,1)} async-done(((bf16[1024,768]{1,0:T(8,128)(2,1)}), bf16[128,768]{1,0:T(8,128)(2,1)}) %reduce-scatter.30.cloned.1.call-update) | async-done | bytes 196624 | tf_op jit(solution)/shard_map/reduce_scatter | solution.py:293
  746.2 39.6 %reduce-scatter.32.cloned.1.call-done = bf16[768,128]{0,1:T(8,128)(2,1)} async-done(((bf16[768,1024]{0,1:T(8,128)(2,1)}), bf16[768,128]{0,1:T(8,128)(2,1)}) %reduce-scatter.32.cloned.1.call-update) | async-done | bytes 196624 | tf_op jit(solution)/shard_map/reduce_scatter | solution.py:296
  786.9 23.5 %all_to_all.24 = bf16[8,128,768]{2,1,0:T(8,128)(2,1)S(1)} all-to-all(bf16[8,128,768]{2,1,0:T(8,128)(2,1)S(1)} %bitcast_dynamic-update-slice_fusion.1), channel_id=1, replica_groups=mesh['dp'=8,'tensor'=4] {'dp'}, dimensions={0} | all-to-all | bytes 3145728 | tf_op jit(solution)/shard_map/all_to_all | solution.py:351
  814.9 85.5 %all-reduce.15.cloned.1.call-done = bf16[1024,1024]{1,0:T(8,128)(2,1)} async-done(((bf16[1024,1024]{1,0:T(8,128)(2,1)}), bf16[1024,1024]{1,0:T(8,128)(2,1)}) %all-reduce.15.cloned.1.call-update) | async-done | bytes 2097168 | tf_op jit(solution)/shard_map/psum | solution.py:363
  903.7 13.5 fusion.84
  917.2 11.1 multiply_add_fusion.3
  930.0 11.2 convolution_convert_fusion.3
  941.4 85.4 %all-reduce.17.cloned.1.call-done = bf16[1024,1024]{1,0:T(8,128)(2,1)} async-done(((bf16[1024,1024]{1,0:T(8,128)(2,1)}), bf16[1024,1024]{1,0:T(8,128)(2,1)}) %all-reduce.17.cloned.1.call-update) | async-done | bytes 2097168 | tf_op jit(solution)/shard_map/psum | solution.py:363
  1026.8 4.7 fusion.158
  1031.6 10.8 multiply_add_fusion.2
  1044.0 11.7 convolution_convert_fusion.2
  1055.7 85.6 %all-reduce.19.cloned.1.call-done = bf16[1024,1024]{1,0:T(8,128)(2,1)} async-done(((bf16[1024,1024]{1,0:T(8,128)(2,1)}), bf16[1024,1024]{1,0:T(8,128)(2,1)}) %all-reduce.19.cloned.1.call-update) | async-done | bytes 2097168 | tf_op jit(solution)/shard_map/psum | solution.py:363
  1141.3 4.7 fusion.159
  1146.0 10.8 multiply_add_fusion.1
  1158.5 11.4 convolution_convert_fusion.1
  1170.0 85.6 %all-reduce.21.cloned.1.call-done = bf16[1024,1024]{1,0:T(8,128)(2,1)} async-done(((bf16[1024,1024]{1,0:T(8,128)(2,1)}), bf16[1024,1024]{1,0:T(8,128)(2,1)}) %all-reduce.21.cloned.1.call-update) | async-done | bytes 2097168 | tf_op jit(solution)/shard_map/psum | solution.py:363
  1255.6 4.7 fusion.160
  1260.3 10.8 multiply_add_fusion
  1272.7 11.6 convolution_convert_fusion
  1291.7 4.6 convolution_convert_fusion.6
  1299.0 71.0 %all-reduce.23.cloned.1.call-done = bf16[1024,1024]{1,0:T(8,128)(2,1)} async-done(((bf16[1024,1024]{1,0:T(8,128)(2,1)}), bf16[1024,1024]{1,0:T(8,128)(2,1)}) %all-reduce.23.cloned.1.call-update) | async-done | bytes 2097168 | tf_op jit(solution)/shard_map/psum | solution.py:363
  1370.0 4.7 fusion.161
  1374.7 10.6 fusion.111
  1388.3 11.7 reduce.14
  1400.0 3.7 reshape.631
  1403.7 4.4 all-to-all-start.1
  1411.8 3.2 reduce-scatter.18.cloned.1.call-done
  1416.6 47.4 %psum.47 = f32[2304]{0:T(1024)S(1)} all-reduce(f32[2304]{0:T(1024)S(1)} %pad_maximum_fusion.4), channel_id=1, replica_groups=mesh['dp'=8,'tensor'=4] {'dp','tensor'}, use_global_device_ids=true, to_apply=%region_36.37 | all-reduce | flops 2304 | bytes 18432 | tf_op jit(solution)/shard_map/psum | solution.py:274
  1464.8 3.3 fusion.124
  1468.0 4.7 reshape.632
  1474.1 3.4 fusion.129
  (444 shorter events, 172.5 us)
Async XLA Ops:
  7.2 7.1 copy-start.84
  7.2 7.2 copy-start.60
  7.2 7.2 copy-start.58
  7.3 53.5 %all-gather.10.cloned.1.call-start = ((), (), s32[]{:S(2)}) async-start(), calls=%async_computation.13 | async-start | bytes 2621440 | tf_op jit(solution)/shard_map/all_gather | solution.py:132
  9.9 404.8 %copy-start.72 = (f32[1024]{0:T(1024)}, f32[1024]{0:T(1024)S(1)}, u32[]{:S(2)}) copy-start(f32[1024]{0:T(1024)S(1)} %get-tuple-element.614) | copy-start | bytes 12292
  12.0 73.5 %all-gather.12.cloned.1.call-start = ((), (), s32[]{:S(2)}) async-start(), calls=%async_computation.14 | async-start | bytes 1179648 | tf_op jit(solution)/shard_map/all_gather | solution.py:111
  12.7 116.5 %all-gather.14.cloned.1.call-start = ((), (), s32[]{:S(2)}) async-start(), calls=%async_computation.15 | async-start | bytes 1179648 | tf_op jit(solution)/shard_map/all_gather | solution.py:114
  13.5 163.9 %reduce-scatter.12.cloned.1.call-start = ((), (), s32[]{:S(2)}) async-start(), calls=%async_computation.16 | async-start | bytes 2621440 | tf_op jit(solution)/shard_map/reduce_scatter | solution.py:178
  14.3 52.3 %copy-start.89 = (f32[128]{0:T(128)}, f32[128]{0:T(128)S(1)}, u32[]{:S(2)}) copy-start(f32[128]{0:T(128)S(1)} %get-tuple-element.616) | copy-start | bytes 1540
  14.3 86.0 %copy-start.87 = (f32[128]{0:T(128)}, f32[128]{0:T(128)S(1)}, u32[]{:S(2)}) copy-start(f32[128]{0:T(128)S(1)} %get-tuple-element.617) | copy-start | bytes 1540
  25.8 35.0 %copy-start.25 = (bf16[1024,256]{1,0:T(8,128)(2,1)}, bf16[1024,256]{1,0:T(8,128)(2,1)S(1)}, u32[]{:S(2)}) copy-start(bf16[1024,256]{1,0:T(8,128)(2,1)S(1)} %all_gather.43) | copy-start | bytes 1572868
  35.6 27.8 %copy-start.15 = (bf16[1024,256]{1,0:T(8,128)(2,1)}, bf16[1024,256]{1,0:T(8,128)(2,1)S(1)}, u32[]{:S(2)}) copy-start(bf16[1024,256]{1,0:T(8,128)(2,1)S(1)} %all_gather.42) | copy-start | bytes 1572868
  36.6 30.0 %copy-start.10 = (f32[1024,128]{0,1:T(8,128)}, f32[1024,128]{0,1:T(8,128)S(1)}, u32[]{:S(2)}) copy-start(f32[1024,128]{0,1:T(8,128)S(1)} %pad_maximum_fusion.2) | copy-start | bytes 1572868
  40.7 26.0 %copy-start.13 = (f32[1024,128]{0,1:T(8,128)}, f32[1024,128]{0,1:T(8,128)S(1)}, u32[]{:S(2)}) copy-start(f32[1024,128]{0,1:T(8,128)S(1)} %pad_maximum_fusion.3) | copy-start | bytes 1572868
  133.3 44.1 %copy-start.4 = (bf16[256,1024]{1,0:T(8,128)(2,1)S(1)}, bf16[256,1024]{1,0:T(8,128)(2,1)}, u32[]{:S(2)}) copy-start(bf16[256,1024]{1,0:T(8,128)(2,1)} %param.38) | copy-start | bytes 1572868
  133.3 47.5 %copy-start.43 = (f32[128,768]{1,0:T(8,128)S(1)}, f32[128,768]{1,0:T(8,128)}, u32[]{:S(2)}) copy-start(f32[128,768]{1,0:T(8,128)} %param.45) | copy-start | bytes 1179652
  133.3 71.5 %all-gather.20.cloned.1.call-start = ((), (), s32[]{:S(2)}) async-start(), calls=%async_computation.19 | async-start | bytes 1769472 | tf_op jit(solution)/shard_map/all_gather | solution.py:116
  135.0 46.6 %copy-start.35 = (f32[768,128]{1,0:T(8,128)S(1)}, f32[768,128]{1,0:T(8,128)}, u32[]{:S(2)}) copy-start(f32[768,128]{1,0:T(8,128)} %param.47) | copy-start | bytes 1179652
  135.0 117.9 %all-gather.16.cloned.1.call-start = ((), (), s32[]{:S(2)}) async-start(), calls=%async_computation.17 | async-start | bytes 2621440 | tf_op jit(solution)/shard_map/all_gather | solution.py:185
  178.7 236.0 %copy-start.81 = (f32[256]{0:T(256)}, f32[256]{0:T(256)S(1)}, u32[]{:S(2)}) copy-start(f32[256]{0:T(256)S(1)} %fusion.136) | copy-start | bytes 3076
  180.7 99.3 %all-gather.18.cloned.1.call-start = ((), (), s32[]{:S(2)}) async-start(), calls=%async_computation.18 | async-start | bytes 1769472 | tf_op jit(solution)/shard_map/all_gather | solution.py:115
  181.5 127.0 %all-gather.22.cloned.1.call-start = ((), (), s32[]{:S(2)}) async-start(), calls=%async_computation.20 | async-start | bytes 1769472 | tf_op jit(solution)/shard_map/all_gather | solution.py:117
  182.3 173.8 %all-gather.24.cloned.1.call-start = ((), (), s32[]{:S(2)}) async-start(), calls=%async_computation.22 | async-start | bytes 2621440 | tf_op jit(solution)/shard_map/all_gather | solution.py:193
  183.0 229.5 %reduce-scatter.16.cloned.1.call-start = ((), (), s32[]{:S(2)}) async-start(), calls=%async_computation.23 | async-start | bytes 2621440 | tf_op jit(solution)/shard_map/reduce_scatter | solution.py:207
  356.1 8.0 copy-start.104
  369.8 42.8 %copy-start.7 = (bf16[256,1024]{1,0:T(8,128)(2,1)S(1)}, bf16[256,1024]{1,0:T(8,128)(2,1)}, u32[]{:S(2)}) copy-start(bf16[256,1024]{1,0:T(8,128)(2,1)} %reduce-scatter.12.cloned.1.call-done) | copy-start | bytes 1572868
  369.8 92.7 %all-gather.26.cloned.1.call-start = ((), (), s32[]{:S(2)}) async-start(), calls=%async_computation.24 | async-start | bytes 2621440 | tf_op jit(solution)/shard_map/all_gather | solution.py:216
  414.7 52.0 %copy-start.93 = (f32[256]{0:T(256)}, f32[256]{0:T(256)S(1)}, u32[]{:S(2)}) copy-start(f32[256]{0:T(256)S(1)} %multiply_multiply_fusion.6) | copy-start | bytes 3076
  417.1 129.3 %reduce-scatter.24.cloned.1.call-start = ((), (), s32[]{:S(2)}) async-start(), calls=%async_computation.28 | async-start | bytes 589824 | tf_op jit(solution)/shard_map/reduce_scatter | solution.py:284
  505.1 8.7 copy-start.6
  511.2 70.5 %reduce-scatter.22.cloned.1.call-start = ((), (), s32[]{:S(2)}) async-start(), calls=%async_computation.27 | async-start | bytes 589824 | tf_op jit(solution)/shard_map/reduce_scatter | solution.py:281
  518.9 102.4 %reduce-scatter.20.cloned.1.call-start = ((), (), s32[]{:S(2)}) async-start(), calls=%async_computation.26 | async-start | bytes 1179648 | tf_op jit(solution)/shard_map/reduce_scatter | solution.py:278
  526.3 134.7 %reduce-scatter.26.cloned.1.call-start = ((), (), s32[]{:S(2)}) async-start(), calls=%async_computation.29 | async-start | bytes 1179648 | tf_op jit(solution)/shard_map/reduce_scatter | solution.py:287
  530.2 172.4 %reduce-scatter.28.cloned.1.call-start = ((), (), s32[]{:S(2)}) async-start(), calls=%async_computation.30 | async-start | bytes 1769472 | tf_op jit(solution)/shard_map/reduce_scatter | solution.py:290
  535.5 208.7 %reduce-scatter.30.cloned.1.call-start = ((), (), s32[]{:S(2)}) async-start(), calls=%async_computation.31 | async-start | bytes 1769472 | tf_op jit(solution)/shard_map/reduce_scatter | solution.py:293
  540.0 245.8 %reduce-scatter.32.cloned.1.call-start = ((), (), s32[]{:S(2)}) async-start(), calls=%async_computation.32 | async-start | bytes 1769472 | tf_op jit(solution)/shard_map/reduce_scatter | solution.py:296
  545.2 36.5 %copy-start.71 = (f32[128,256]{1,0:T(8,128)S(1)}, f32[128,256]{1,0:T(8,128)}, u32[]{:S(2)}) copy-start(f32[128,256]{1,0:T(8,128)} %param.49) | copy-start | bytes 393220
  545.2 76.1 %copy-start.66 = (f32[128,512]{1,0:T(8,128)S(1)}, f32[128,512]{1,0:T(8,128)}, u32[]{:S(2)}) copy-start(f32[128,512]{1,0:T(8,128)} %param.48) | copy-start | bytes 786436
  545.2 355.2 %all-reduce.15.cloned.1.call-start = ((), (), s32[]{:S(2)}) async-start(), calls=%async_computation.33 | async-start | bytes 4194304 | tf_op jit(solution)/shard_map/psum | solution.py:363
  546.2 114.8 %copy-start.19 = (f32[512,128]{0,1:T(8,128)}, f32[512,128]{0,1:T(8,128)S(1)}, u32[]{:S(2)}) copy-start(f32[512,128]{0,1:T(8,128)S(1)} %copy.214) | copy-start | bytes 786436
  814.7 212.1 %all-reduce.17.cloned.1.call-start = ((), (), s32[]{:S(2)}) async-start(), calls=%async_computation.34 | async-start | bytes 4194304 | tf_op jit(solution)/shard_map/psum | solution.py:363
  903.7 13.5 copy-start.34
  941.2 200.1 %all-reduce.19.cloned.1.call-start = ((), (), s32[]{:S(2)}) async-start(), calls=%async_computation.35 | async-start | bytes 4194304 | tf_op jit(solution)/shard_map/psum | solution.py:363
  1055.7 199.9 %all-reduce.21.cloned.1.call-start = ((), (), s32[]{:S(2)}) async-start(), calls=%async_computation.36 | async-start | bytes 4194304 | tf_op jit(solution)/shard_map/psum | solution.py:363
  1169.9 200.0 %all-reduce.23.cloned.1.call-start = ((), (), s32[]{:S(2)}) async-start(), calls=%async_computation.37 | async-start | bytes 4194304 | tf_op jit(solution)/shard_map/psum | solution.py:363
  1284.4 130.7 %reduce-scatter.18.cloned.1.call-start = ((), (), s32[]{:S(2)}) async-start(), calls=%async_computation.25 | async-start | bytes 2621440 | tf_op jit(solution)/shard_map/reduce_scatter | solution.py:265
  1290.3 174.4 %reduce-scatter.14.cloned.1.call-start = ((), (), s32[]{:S(2)}) async-start(), calls=%async_computation.21 | async-start | bytes 2621440 | tf_op jit(solution)/shard_map/reduce_scatter | solution.py:189
  1299.0 75.7 %copy-start.106 = (f32[1024,768]{1,0:T(8,128)S(1)}, f32[1024,768]{1,0:T(8,128)}, u32[]{:S(2)}) copy-start(f32[1024,768]{1,0:T(8,128)} %copy-done.105) | copy-start | bytes 9437188
  1403.7 6.5 copy-start.46
  1403.7 64.3 %all-to-all-start.1 = ((bf16[8,2,49152]{2,1,0:T(2,128)(2,1)}), bf16[8,2,49152]{2,1,0:T(2,128)(2,1)}, u32[]{:S(2)}, u32[]{:S(2)}) async-start(bf16[8,2,49152]{2,1,0:T(2,128)(2,1)} %reshape.631), calls=%async_computation.12 | async-start | bytes 3145728 | tf_op jit(solution)/shard_map/all_to_all | solution.py:378
  1408.1 6.9 copy-start.5
  1408.2 6.9 copy-start.79
  1408.2 6.9 copy-start.86
  1408.2 8.4 copy-start.83
  1408.2 55.8 %copy-start.96 = (f32[256]{0:T(256)S(1)}, f32[256]{0:T(256)}, u32[]{:S(2)}) copy-start(f32[256]{0:T(256)} %copy-done.95) | copy-start | bytes 3076
  1408.2 55.8 %copy-start.80 = (f32[2304]{0:T(1024)S(1)}, f32[2304]{0:T(1024)}, u32[]{:S(2)}) copy-start(f32[2304]{0:T(1024)} %param.55) | copy-start | bytes 27652
  1408.3 55.8 %copy-start.91 = (f32[2304]{0:T(1024)S(1)}, f32[2304]{0:T(1024)}, u32[]{:S(2)}) copy-start(f32[2304]{0:T(1024)} %param.57) | copy-start | bytes 27652
  1408.3 55.8 %copy-start.92 = (f32[2304]{0:T(1024)S(1)}, f32[2304]{0:T(1024)}, u32[]{:S(2)}) copy-start(f32[2304]{0:T(1024)} %param.56) | copy-start | bytes 27652
  1408.3 56.4 %copy-start.8 = (bf16[256,1024]{1,0:T(8,128)(2,1)S(1)}, bf16[256,1024]{1,0:T(8,128)(2,1)}, u32[]{:S(2)}) copy-start(bf16[256,1024]{1,0:T(8,128)(2,1)} %reduce-scatter.12.cloned.1.call-done) | copy-start | bytes 1572868
  1408.3 56.4 %copy-start.17 = (bf16[256,1024]{1,0:T(8,128)(2,1)S(1)}, bf16[256,1024]{1,0:T(8,128)(2,1)}, u32[]{:S(2)}) copy-start(bf16[256,1024]{1,0:T(8,128)(2,1)} %param.39) | copy-start | bytes 1572868
  1408.3 56.4 %copy-start.18 = (bf16[256,1024]{1,0:T(8,128)(2,1)S(1)}, bf16[256,1024]{1,0:T(8,128)(2,1)}, u32[]{:S(2)}) copy-start(bf16[256,1024]{1,0:T(8,128)(2,1)} %reduce-scatter.16.cloned.1.call-done) | copy-start | bytes 1572868
  1408.3 56.4 %copy-start.73 = (f32[1024]{0:T(1024)S(1)}, f32[1024]{0:T(1024)}, u32[]{:S(2)}) copy-start(f32[1024]{0:T(1024)} %copy-done.72) | copy-start | bytes 12292
  1408.3 56.4 %copy-start.82 = (f32[256]{0:T(256)S(1)}, f32[256]{0:T(256)}, u32[]{:S(2)}) copy-start(f32[256]{0:T(256)} %copy-done.81) | copy-start | bytes 3076
  1408.3 56.4 %copy-start.94 = (f32[256]{0:T(256)S(1)}, f32[256]{0:T(256)}, u32[]{:S(2)}) copy-start(f32[256]{0:T(256)} %copy-done.93) | copy-start | bytes 3076
  (81 other events, 206.0 us)
Sparse Core Ops, SparseCore 0:
  12.1 48.6 all-gather.9
  63.2 22.1 all-gather.11
  87.9 23.5 all-gather.13
  133.4 43.8 reduce-scatter.11
  179.8 25.0 all-gather.19
  207.0 45.9 all-gather.15
  255.5 24.4 all-gather.17
  282.6 25.8 all-gather.21
  310.2 45.9 all-gather.23
  369.9 42.5 reduce-scatter.15
  417.2 45.2 all-gather.25
  511.3 32.8 reduce-scatter.23
  547.5 34.0 reduce-scatter.21
  585.3 35.9 reduce-scatter.19
  624.9 35.9 reduce-scatter.25
  664.1 38.4 reduce-scatter.27
  705.7 38.4 reduce-scatter.29
  747.4 38.4 reduce-scatter.31
  814.8 85.5 all-reduce.14
  941.3 85.4 all-reduce.16
  1055.8 85.4 all-reduce.18
  1170.1 85.4 all-reduce.20
  1284.5 85.4 all-reduce.22
  1372.2 42.7 reduce-scatter.17
  1417.4 44.2 reduce-scatter.13
where the time goes:
time: 1500 us; the launch traced here: 1490 us
  waiting for transfers between devices  975 us (65%)
  matrix products  237 us (16%)
  blocking collectives  92.1 us (6%)
  other arithmetic  89.9 us (6%)
  local copies, waits for them, and re-layouts  72.3 us (5%)
  between operations  16.7 us (1%)
    psum x5, waiting for transfers between devices, gram_sum(): lax.psum(local_gram.astype(jnp.bfloat16), 'tensor').astype(jnp.float32)  413 us
    dot_general x5, matrix products, on_device(): jnp.dot(mixture, current, preferred_element_type=jnp.float32, precision=H...  54.1 us
    dot_general x5, matrix products, gram_sum(): lax.dot_general(matrix, matrix, (((1,), (1,)), ((), ())), preferred_eleme...  49.1 us
    all_gather x1, waiting for transfers between devices, on_device(): mlp_rows = lax.all_gather(normed_mlp, 'tensor', axis=0, tiled=True)  48 us
    all_gather x1, waiting for transfers between devices, on_device(): cot_rows = lax.all_gather(out_grad, 'tensor', axis=0, tiled=True)  47.6 us
    psum x1, blocking collectives, on_device(): lax.psum(jnp.concatenate([d_gain_attn, d_gain_mlp, d_gain_query, d_gain_k...  47.4 us
    all_gather x1, waiting for transfers between devices, on_device(): lax.all_gather(d_residual.astype(jnp.bfloat16), 'tensor', axis=0, tiled=T...  45.2 us
    reduce_scatter x1, waiting for transfers between devices, on_device(): lax.psum_scatter((gate_part + contract_cols(d_up, up_full)).astype(jnp.bf...  42.7 us
  transfers between devices with their start and end apart: 26, of which 22 were waited for; matrix products, arithmetic and copies ran while one was open for 11% of the time, Pallas kernels for 0%

commit v1 on v0

v1 whole, which is shorter than its diff:
```python
import functools
import math

import jax
import jax.numpy as jnp
from jax import lax
from jax.experimental import pallas as pl
from jax.experimental.pallas import tpu as pltpu
from jax.sharding import Mesh, PartitionSpec as P

MODEL_WIDTH = 1024
QUERY_HEADS = 16
KEY_VALUE_HEADS = 8
HEAD_SIZE = 128
FF = 3072
NS_STEPS = 5
ADAM_STEP = 10


EPS_NORM = 1e-06
ROPE_BASE = 1000000.0
MASK_FILL = -1e30
MOMENTUM = 0.95
COEF_LINEAR = 3.4445
COEF_GRAM = -4.775
COEF_SQUARE = 2.0315
NS_EPS = 1e-07
DECAY_KEEP = 0.998
BETA_FIRST = 0.9
BETA_SECOND = 0.95
ADAM_EPS = 1e-08
GAIN_RATE = 0.6
ROW_BLOCK = 256


DP = ("pl", "core")
TENSOR = ("hi", "lo")


def matmul(left, right):
    return jnp.dot(left, right, preferred_element_type=jnp.float32)


def contract_rows(left, right):
    return lax.dot_general(
        left, right, (((0,), (0,)), ((), ())), preferred_element_type=jnp.float32
    )


def contract_cols(left, right):
    return lax.dot_general(
        left, right, (((1,), (1,)), ((), ())), preferred_element_type=jnp.float32
    )


def orthogonalize_kernel(owner_ref, *refs):
    count = (len(refs) - 4) // 2

    @pl.when(owner_ref[0] != 0)
    def _():
        orthogonalize_owned(count, refs)

    @pl.when(owner_ref[0] == 0)
    def _():
        for result in refs[count : 2 * count]:
            result[...] = jnp.zeros_like(result)


def orthogonalize_owned(count, refs):
    pieces, results = refs[:count], refs[count : 2 * count]
    current, gram, gram_low, mixing = refs[2 * count :]
    size, width = pieces[0].shape
    block = 256
    blocks = size // block
    for number, piece in enumerate(pieces):
        current[:, number * width : (number + 1) * width] = piece[...]
    diagonal = lax.broadcasted_iota(jnp.int32, (block, block), 0) == lax.broadcasted_iota(
        jnp.int32, (block, block), 1
    )

    def mix(number):
        for col in range(blocks):
            at = col * block
            gram[at:, at : at + block] = contract_cols(current[at:, :], current[at : at + block, :])
        trace = jnp.float32(0.0)
        for col in range(blocks):
            at = col * block
            trace += jnp.sum(jnp.where(diagonal, gram[at : at + block, at : at + block], 0.0))
        scale = jnp.where(number == 0, 1.0 / (jnp.sqrt(trace) + NS_EPS), 1.0)
        scale_square = scale * scale
        for col in range(blocks):
            at = col * block
            for row in range(col, blocks):
                to = row * block
                tile = gram[to : to + block, at : at + block] * scale_square
                gram[to : to + block, at : at + block] = tile
                gram_low[to : to + block, at : at + block] = tile.astype(jnp.bfloat16)
                if row > col:
                    gram_low[at : at + block, to : to + block] = tile.T.astype(jnp.bfloat16)
        for col in range(blocks):
            at = col * block
            square = matmul(gram_low[at:, :], gram_low[:, at : at + block])
            for row in range(col, blocks):
                to = row * block
                tile = COEF_GRAM * gram[to : to + block, at : at + block]
                tile += COEF_SQUARE * square[to - at : to - at + block]
                if row == col:
                    tile += jnp.where(diagonal, COEF_LINEAR, 0.0)
                tile = tile * scale
                mixing[to : to + block, at : at + block] = tile.astype(jnp.bfloat16)
                if row > col:
                    mixing[at : at + block, to : to + block] = tile.T.astype(jnp.bfloat16)

    def sweep(number, carry):
        mix(number)

        def columns(step, inner):
            span = pl.ds(pl.multiple_of(step * width, width), width)
            current[:, span] = matmul(mixing[...], current[:, span]).astype(jnp.bfloat16)
            return inner

        lax.fori_loop(0, count, columns, 0)
        return carry

    lax.fori_loop(0, NS_STEPS, sweep, 0)
    for number, result in enumerate(results):
        result[...] = current[:, number * width : (number + 1) * width]


def orthogonalize(owner, pieces):
    size, width = pieces[0].shape
    total = width * len(pieces)
    flops = NS_STEPS * 2 * size * size * (total * 13 // 8 + size * 5 // 8)
    return pl.pallas_call(
        orthogonalize_kernel,
        out_shape=[jax.ShapeDtypeStruct(piece.shape, piece.dtype) for piece in pieces],
        in_specs=[pl.BlockSpec(memory_space=pltpu.SMEM)]
        + [pl.BlockSpec(memory_space=pltpu.VMEM)] * len(pieces),
        out_specs=[pl.BlockSpec(memory_space=pltpu.VMEM)] * len(pieces),
        scratch_shapes=[
            pltpu.VMEM((size, total), jnp.bfloat16),
            pltpu.VMEM((size, size), jnp.float32),
            pltpu.VMEM((size, size), jnp.bfloat16),
            pltpu.VMEM((size, size), jnp.bfloat16),
        ],
        compiler_params=pltpu.CompilerParams(vmem_limit_bytes=48 * 1024 * 1024),
        cost_estimate=pl.CostEstimate(
            flops=flops, bytes_accessed=4 * size * total, transcendentals=0
        ),
    )(owner.astype(jnp.int32).reshape(1), *pieces)


def tied(*values):
    return lax.optimization_barrier(values)


def swap(values):
    return lax.ppermute(values, ("core", "hi"), [(0, 0), (1, 2), (2, 1), (3, 3)])


def to_partner(values, name):
    return lax.ppermute(values, name, [(0, 1), (1, 0)])


def in_order(first, mine, theirs):
    return jnp.concatenate([jnp.where(first, mine, theirs), jnp.where(first, theirs, mine)], axis=0)


def half_of(values, which):
    rows = values.shape[0] // 2
    return lax.dynamic_slice_in_dim(values, which * rows, rows, 0)


def gather_near(values, ordered):
    if lax.axis_size("lo") == 2:
        other = to_partner(values, "lo")
        if ordered:
            return in_order(lax.axis_index("lo") == 0, values, other)
        return jnp.concatenate([values, other], axis=0)
    return lax.all_gather(values, "lo", axis=0, tiled=True)


def gather_across(pair, ordered):
    other = to_partner(pair, "core")
    if ordered:
        return in_order(lax.axis_index("core") == 0, pair, other)
    return jnp.concatenate([pair, other], axis=0)


def scatter_across(values, ordered):
    place = lax.axis_index("core") if ordered else 0
    received = to_partner(half_of(values, 1 - place), "core").astype(jnp.float32)
    return half_of(values, place).astype(jnp.float32) + received


def scatter_near(pair, ordered):
    if lax.axis_size("lo") == 2:
        place = lax.axis_index("lo") if ordered else 0
        received = to_partner(half_of(pair, 1 - place).astype(jnp.bfloat16), "lo")
        return half_of(pair, place) + received.astype(jnp.float32)
    return lax.psum_scatter(
        pair.astype(jnp.bfloat16), "lo", scatter_dimension=0, tiled=True
    ).astype(jnp.float32)


def scatter_tokens(values, ordered):
    return scatter_near(scatter_across(values, ordered), ordered)


def both_cores(shard):
    return in_order(lax.axis_index("core") == 0, shard, to_partner(shard, "core"))


def exchange(values, stride):
    count = lax.axis_size("pl")
    return lax.ppermute(values, "pl", [(index, index ^ stride) for index in range(count)])


def in_places(found, held):
    rows = held.shape[0] * lax.axis_size("pl")
    full = jnp.zeros((rows, held.shape[1]), held.dtype)
    for piece, at in found:
        full = lax.dynamic_update_slice_in_dim(full, piece, at, 0)
    return full


def gather_plane_direct(held):
    place = lax.axis_index("pl")
    rows = held.shape[0]
    found = [(held, place * rows)]
    for stride in range(1, lax.axis_size("pl")):
        found.append((exchange(held, stride), (place ^ stride) * rows))
    return in_places(found, held)


def gather_plane_near(held):
    if lax.axis_size("pl") != 4:
        return [held] + [exchange(held, stride) for stride in range(1, lax.axis_size("pl"))]
    return [held, exchange(held, 1), exchange(held, 2)]


def gather_plane_far(near):
    place = lax.axis_index("pl")
    rows = near[0].shape[0]
    half = rows // 2
    found = [(piece, (place ^ stride) * rows) for stride, piece in enumerate(near)]
    if lax.axis_size("pl") == 4:
        found.append((exchange(near[2][:half], 1), (place ^ 3) * rows))
        found.append((exchange(near[1][half:], 2), (place ^ 3) * rows + half))
    return in_places(found, near[0])


def gather_plane(held):
    return gather_plane_far(gather_plane_near(held))


def sum_far(values):
    count = lax.axis_size("pl")
    place = lax.axis_index("pl")
    rows = values.shape[0] // count
    half = rows // 2
    chunks = [
        lax.dynamic_slice_in_dim(values, (place ^ stride) * rows, rows, 0) for stride in range(count)
    ]
    if count != 4:
        return chunks
    return chunks[:3] + [exchange(chunks[3][half:], 2), exchange(chunks[3][:half], 1)]


def sum_near(chunks):
    count = lax.axis_size("pl")
    if count != 4:
        return chunks[:1] + [exchange(chunks[stride], stride) for stride in range(1, count)]
    mine, first, second, for_first, for_second = chunks
    half = mine.shape[0] // 2
    first = jnp.concatenate([first[:half], add(first[half:], for_first)], axis=0)
    second = jnp.concatenate([add(second[:half], for_second), second[half:]], axis=0)
    return [mine, exchange(first, 1), exchange(second, 2)]


def sum_plane(values):
    return sum_near(sum_far(values))


def add(left, right):
    return (left.astype(jnp.float32) + right.astype(jnp.float32)).astype(jnp.bfloat16)


def cross_sum(pieces):
    total = sum(piece.astype(jnp.float32) for piece in pieces)
    return swap(total.astype(jnp.bfloat16))


def finish_sum(held):
    place = lax.axis_index("core")
    received = to_partner(half_of(held, 1 - place), "core")
    return half_of(held, place).astype(jnp.float32) + received.astype(jnp.float32)


def sum_everywhere(values, sizes):
    for name, count in sizes:
        stride = 1
        while stride < count:
            pairs = [(index, index ^ stride) for index in range(count)]
            values = values + lax.ppermute(values, name, pairs)
            stride *= 2
    return values


def rms_norm(values, gain):
    return values * lax.rsqrt(jnp.mean(values * values, axis=-1, keepdims=True) + EPS_NORM) * gain


def rotary(positions):
    half_width = HEAD_SIZE // 2
    inverse = jnp.power(
        jnp.float32(ROPE_BASE), -(jnp.arange(half_width, dtype=jnp.float32) * (2.0 / HEAD_SIZE))
    )
    angles = positions.astype(jnp.float32)[:, None] * inverse[None, :]
    cosine_part = jnp.cos(angles)
    sine_part = jnp.sin(angles)
    return (
        jnp.concatenate([cosine_part, cosine_part], axis=-1),
        jnp.concatenate([-sine_part, sine_part], axis=-1),
    )


def visible_pairs(start_ref, block, extent, rows):
    query = block * rows + lax.broadcasted_iota(jnp.int32, (extent, rows), 1)
    key = lax.broadcasted_iota(jnp.int32, (extent, rows), 0)
    begin = start_ref[:, block * rows : (block + 1) * rows]
    return (key <= query) & (key >= begin)


def turn_half(values):
    return pltpu.roll(values, HEAD_SIZE // 2, 1)


def project_kernel(
    rows_ref,
    weight_ref,
    cosine_ref,
    sine_ref,
    gain_query_ref,
    gain_key_ref,
    query_ref,
    key_ref,
    value_ref,
    pre_ref,
):
    total_rows = rows_ref.shape[0]
    width_query, width_key = query_ref.shape[1], key_ref.shape[1]
    size = ROW_BLOCK
    low = jnp.bfloat16

    def project(block, carry):
        span = pl.ds(pl.multiple_of(block * size, size), size)
        pre = matmul(rows_ref[span, :], weight_ref[...])
        pre_ref[span, :] = pre[:, : width_query + width_key]
        cosine, sine = cosine_ref[span, :], sine_ref[span, :]
        for at in range(0, width_query + width_key, HEAD_SIZE):
            gain_ref = gain_query_ref if at < width_query else gain_key_ref
            normal = rms_norm(pre[:, at : at + HEAD_SIZE], gain_ref[...])
            turned = (normal * cosine + turn_half(normal) * sine).astype(low)
            if at < width_query:
                query_ref[span, at : at + HEAD_SIZE] = turned
            else:
                key_ref[span, at - width_query : at - width_query + HEAD_SIZE] = turned
        value_ref[span, :] = pre[:, width_query + width_key :].astype(low)
        return carry

    lax.fori_loop(0, total_rows // size, project, 0)


def attend_kernel(
    query_ref, key_ref, value_ref, start_ref, mixed_ref, log_total_ref, turned_value
):
    total_rows = query_ref.shape[0]
    width_query, width_key = query_ref.shape[1], key_ref.shape[1]
    size = ROW_BLOCK
    scale = HEAD_SIZE**-0.5
    low = jnp.bfloat16

    def prepare(block, carry):
        span = pl.ds(pl.multiple_of(block * size, size), size)
        for at in range(0, width_key, HEAD_SIZE):
            value = value_ref[span, at : at + HEAD_SIZE].astype(jnp.float32)
            turned_value[at : at + HEAD_SIZE, span] = value.T.astype(low)
        return carry

    lax.fori_loop(0, total_rows // size, prepare, 0)
    group = width_query // width_key
    for block in range(total_rows // size):
        extent = (block + 1) * size
        rows = slice(block * size, extent)
        visible = visible_pairs(start_ref, block, extent, size)
        for head in range(width_query // HEAD_SIZE):
            key_at = head // group * HEAD_SIZE
            lanes = slice(head * HEAD_SIZE, (head + 1) * HEAD_SIZE)
            key_lanes = slice(key_at, key_at + HEAD_SIZE)
            scores = contract_cols(key_ref[:extent, key_lanes], query_ref[rows, lanes])
            scores = jnp.where(visible, scores, MASK_FILL)
            row_max = jnp.max(scores, axis=0, keepdims=True)
            weights = jnp.exp((scores - row_max) * scale)
            total = jnp.sum(weights, axis=0, keepdims=True)
            log_total_ref[head : head + 1, rows] = row_max * scale + jnp.log(total)
            weights = (weights * (1.0 / total)).astype(low)
            mixed = matmul(turned_value[key_lanes, :extent], weights)
            mixed_ref[rows, lanes] = mixed.T.astype(low)


def attention_backward_kernel(
    state_ref,
    out_ref,
    query_ref,
    key_ref,
    value_ref,
    pre_ref,
    log_total_ref,
    cosine_ref,
    sine_ref,
    gain_query_ref,
    gain_key_ref,
    start_ref,
    d_heads_ref,
    d_gain_ref,
    d_mixed,
    turned_key,
    d_query,
    d_key,
    d_value,
):
    total_rows = state_ref.shape[0]
    width_query, width_key = query_ref.shape[1], key_ref.shape[1]
    size = ROW_BLOCK
    scale = HEAD_SIZE**-0.5
    low = jnp.bfloat16

    def prepare(block, carry):
        span = pl.ds(pl.multiple_of(block * size, size), size)
        d_mixed[span, :] = matmul(state_ref[span, :], out_ref[...]).astype(low)
        for at in range(0, width_key, HEAD_SIZE):
            key = key_ref[span, at : at + HEAD_SIZE].astype(jnp.float32)
            turned_key[at : at + HEAD_SIZE, span] = key.T.astype(low)
        return carry

    lax.fori_loop(0, total_rows // size, prepare, 0)
    d_key[...] = jnp.zeros_like(d_key)
    d_value[...] = jnp.zeros_like(d_value)
    group = width_query // width_key
    for block in range(total_rows // size):
        extent = (block + 1) * size
        rows = slice(block * size, extent)
        visible = visible_pairs(start_ref, block, extent, size)
        for head in range(width_query // HEAD_SIZE):
            key_at = head // group * HEAD_SIZE
            lanes = slice(head * HEAD_SIZE, (head + 1) * HEAD_SIZE)
            key_lanes = slice(key_at, key_at + HEAD_SIZE)
            query = query_ref[rows, lanes]
            cotangent = d_mixed[rows, lanes]
            scores = contract_cols(key_ref[:extent, key_lanes], query) * scale
            probs = jnp.exp(scores - log_total_ref[head : head + 1, rows])
            probs = jnp.where(visible, probs, 0.0)
            d_probs = contract_cols(value_ref[:extent, key_lanes], cotangent)
            shift = jnp.sum(d_probs * probs, axis=0, keepdims=True)
            d_scores = (probs * (d_probs - shift)).astype(low)
            d_value[:extent, key_lanes] += matmul(probs.astype(low), cotangent)
            d_key[:extent, key_lanes] += matmul(d_scores, query)
            d_query[rows, lanes] = matmul(turned_key[key_lanes, :extent], d_scores).T * scale

    def finish(block, carry):
        span = pl.ds(pl.multiple_of(block * size, size), size)
        cosine, sine = cosine_ref[span, :], sine_ref[span, :]
        sums = []
        for at in range(0, width_query + width_key, HEAD_SIZE):
            if at < width_query:
                gain, cotangent = gain_query_ref[...], d_query[span, at : at + HEAD_SIZE]
            else:
                begin = at - width_query
                gain = gain_key_ref[...]
                cotangent = d_key[span, begin : begin + HEAD_SIZE] * scale
            cotangent = cotangent * cosine - turn_half(cotangent) * sine
            pre = pre_ref[span, at : at + HEAD_SIZE]
            inverse = lax.rsqrt(jnp.mean(pre * pre, axis=-1, keepdims=True) + EPS_NORM)
            normal = pre * inverse
            sums.append(jnp.sum(cotangent * normal, axis=0, keepdims=True))
            pulled = cotangent * gain
            inner = jnp.mean(normal * pulled, axis=-1, keepdims=True)
            d_pre = inverse * (pulled - normal * inner)
            d_heads_ref[span, at : at + HEAD_SIZE] = d_pre.astype(low)
        d_heads_ref[span, width_query + width_key :] = d_value[span, :].astype(low)
        heads_query = width_query // HEAD_SIZE
        return carry[0] + sum(sums[:heads_query]), carry[1] + sum(sums[heads_query:])

    zero = jnp.zeros((1, HEAD_SIZE), jnp.float32)
    for_query, for_key = lax.fori_loop(0, total_rows // size, finish, (zero, zero))
    d_gain_ref[0:1, :] = for_query
    d_gain_ref[1:2, :] = for_key


def in_vmem(kernel, operands, results, scratch, flops):
    moved = sum(math.prod(item.shape) * item.dtype.itemsize for item in operands + results)
    return pl.pallas_call(
        kernel,
        out_shape=results,
        in_specs=[pl.BlockSpec(memory_space=pltpu.VMEM)] * len(operands),
        out_specs=[pl.BlockSpec(memory_space=pltpu.VMEM)] * len(results),
        scratch_shapes=scratch,
        compiler_params=pltpu.CompilerParams(vmem_limit_bytes=48 * 1024 * 1024),
        cost_estimate=pl.CostEstimate(flops=flops, bytes_accessed=moved, transcendentals=0),
    )(*operands)


def project(rows, weight, cosine, sine, gain_query, gain_key, width_query):
    total_rows, columns = rows.shape
    width_key = (weight.shape[1] - width_query) // 2
    low = jnp.bfloat16
    shape = jax.ShapeDtypeStruct
    return in_vmem(
        project_kernel,
        [rows, weight, cosine, sine, gain_query, gain_key],
        [
            shape((total_rows, width_query), low),
            shape((total_rows, width_key), low),
            shape((total_rows, width_key), low),
            shape((total_rows, width_query + width_key), jnp.float32),
        ],
        [],
        2 * total_rows * columns * weight.shape[1],
    )


def attend(query, key, value, start):
    total_rows, width_query = query.shape
    width_key = key.shape[1]
    shape = jax.ShapeDtypeStruct
    return in_vmem(
        attend_kernel,
        [query, key, value, start],
        [
            shape((total_rows, width_query), jnp.bfloat16),
            shape((width_query // HEAD_SIZE, total_rows), jnp.float32),
        ],
        [pltpu.VMEM((width_key, total_rows), jnp.bfloat16)],
        4 * total_rows * total_rows * width_query,
    )


def attention_backward(
    state, out_full, saved, cosine, sine, gain_query, gain_key, start
):
    query, key, value, pre, log_total = saved
    total_rows, columns = state.shape
    width_query, width_key = query.shape[1], key.shape[1]
    low = jnp.bfloat16
    shape = jax.ShapeDtypeStruct
    return in_vmem(
        attention_backward_kernel,
        [state, out_full, query, key, value, pre, log_total]
        + [cosine, sine, gain_query, gain_key, start],
        [
            shape((total_rows, width_query + 2 * width_key), low),
            shape((2, HEAD_SIZE), jnp.float32),
        ],
        [
            pltpu.VMEM((total_rows, width_query), low),
            pltpu.VMEM((width_key, total_rows), low),
            pltpu.VMEM((total_rows, width_query), jnp.float32),
            pltpu.VMEM((total_rows, width_key), jnp.float32),
            pltpu.VMEM((total_rows, width_key), jnp.float32),
        ],
        2 * total_rows * columns * width_query + 10 * total_rows * total_rows * width_query,
    )


def home_row(index):
    return lax.axis_size(TENSOR) // 2 - 1 + index % 2


def owns(group, homes):
    index, row = lax.axis_index(DP), lax.axis_index(TENSOR)
    mine = functools.reduce(jnp.logical_or, [index == homes[number] for number in group])
    return mine & (row == home_row(index))


def toward_home(group, homes, step):
    rows = lax.axis_size(TENSOR)
    return [
        (index * rows + (home_row(index) + step) % rows, index * rows + home_row(index))
        for index in sorted(homes[number] for number in group)
    ]


def to_columns(slots):
    owned = lax.all_to_all(slots, DP, split_axis=0, concat_axis=0, tiled=True)
    return owned.reshape(-1, slots.shape[2])


def to_homes(group, homes, owned):
    return [owned] + [
        lax.ppermute(owned, DP + TENSOR, toward_home(group, homes, step))
        for step in range(1, lax.axis_size(TENSOR))
    ]


def from_homes(group, homes, back):
    index, row = lax.axis_index(DP), lax.axis_index(TENSOR)
    received = jnp.where(row == home_row(index), back[0], jnp.zeros_like(back[0]))
    for step in range(1, lax.axis_size(TENSOR)):
        pairs = [(target, source) for source, target in toward_home(group, homes, step)]
        received = received + lax.ppermute(back[step], DP + TENSOR, pairs)
    return received


def from_columns(received):
    shape = (lax.axis_size(DP), -1, received.shape[1])
    return lax.all_to_all(received.reshape(shape), DP, split_axis=0, concat_axis=0, tiled=True)


FLIPPED = (False, False, False, True, False, False, True)
SHAPES = (
    (MODEL_WIDTH, QUERY_HEADS * HEAD_SIZE),
    (MODEL_WIDTH, KEY_VALUE_HEADS * HEAD_SIZE),
    (MODEL_WIDTH, KEY_VALUE_HEADS * HEAD_SIZE),
    (QUERY_HEADS * HEAD_SIZE, MODEL_WIDTH),
    (MODEL_WIDTH, FF),
    (MODEL_WIDTH, FF),
    (FF, MODEL_WIDTH),
)
FANS = (
    MODEL_WIDTH,
    MODEL_WIDTH,
    MODEL_WIDTH,
    QUERY_HEADS * HEAD_SIZE // 64,
    MODEL_WIDTH,
    MODEL_WIDTH,
    FF,
)


def advance_kernel(homes, *refs):
    late_ref, out_ref, gate_up_ref, down_ref = refs[:4]
    moment_refs, reduced_refs, fresh_refs = refs[4:11], refs[11:18], refs[18:25]
    slots_ref = refs[25]
    width_query, width_key = moment_refs[0].shape[1], moment_refs[1].shape[1]
    width_ff = moment_refs[4].shape[1]
    gradients = (
        late_ref[:, :width_query],
        late_ref[:, width_query : width_query + width_key],
        late_ref[:, width_query + width_key :],
        out_ref[...],
        gate_up_ref[:, :width_ff],
        gate_up_ref[:, width_ff:],
        down_ref[...],
    )
    slots_ref[...] = jnp.zeros_like(slots_ref)
    for number, gradient in enumerate(gradients):
        moment = moment_refs[number][...]
        if FLIPPED[number]:
            gradient_turned = gradient.T
            moment_next = MOMENTUM * moment + gradient_turned
            reduced_refs[number][...] = gradient_turned
            look = (gradient_turned + MOMENTUM * moment_next).T
        else:
            moment_next = MOMENTUM * moment + gradient
            reduced_refs[number][...] = gradient
            look = gradient + MOMENTUM * moment_next
        fresh_refs[number][...] = moment_next
        slots_ref[homes[number], :, : look.shape[1]] = look.astype(jnp.bfloat16)


def advance(sums, moments, homes, dp_count):
    rows = sums[0].shape[0]
    width = max(moment.shape[1] for moment in moments)
    shapes = [jax.ShapeDtypeStruct(moment.shape, jnp.float32) for moment in moments]
    results = in_vmem(
        functools.partial(advance_kernel, homes),
        list(sums) + list(moments),
        shapes + shapes + [jax.ShapeDtypeStruct((dp_count, rows, width), jnp.bfloat16)],
        [],
        0,
    )
    return results[:7], results[7:14], results[14]


def update_kernel(homes, returned_ref, *refs):
    for number in range(7):
        master_ref, result_ref = refs[number], refs[7 + number]
        width = master_ref.shape[0] if FLIPPED[number] else master_ref.shape[1]
        portion = returned_ref[homes[number], :, :width].astype(jnp.float32)
        if FLIPPED[number]:
            portion = portion.T
        step_size = 0.5 * FANS[number] ** (-0.5) * math.sqrt(max(SHAPES[number]))
        result_ref[...] = DECAY_KEEP * master_ref[...] - step_size * portion


def update(returned, masters, homes):
    return in_vmem(
        functools.partial(update_kernel, homes),
        [returned] + list(masters),
        [jax.ShapeDtypeStruct(master.shape, jnp.float32) for master in masters],
        [],
        0,
    )


def on_device(
    hidden_in,
    out_grad,
    positions,
    query_weight,
    key_matrix,
    value_matrix,
    out_weight,
    gate_weight,
    up_weight,
    down_weight,
    query_moment,
    key_momentum,
    value_momentum,
    out_moment,
    gate_moment,
    up_moment,
    down_moment,
    gains,
    gain_first,
    gain_second,
):
    bf16 = jnp.bfloat16
    heads_local = jnp.concatenate(
        [query_weight.astype(bf16), key_matrix.astype(bf16), value_matrix.astype(bf16)], axis=1
    )
    out_local = out_weight.astype(bf16).T
    mlp_local = jnp.concatenate(
        [gate_weight.astype(bf16), up_weight.astype(bf16), down_weight.astype(bf16).T], axis=1
    )
    width_query = query_weight.shape[1]
    width_key = key_matrix.shape[1]
    width_ff = gate_weight.shape[1]
    heads_held = swap(both_cores(heads_local))
    hidden_in, positions, heads_held = tied(hidden_in, positions, heads_held)
    positions = swap(positions)
    hidden_in = swap(hidden_in)
    heads_near = gather_plane_near(heads_held)
    out_pair = both_cores(out_local)
    mlp_pair = both_cores(mlp_local)
    hidden_in, out_pair, heads_near = tied(hidden_in, out_pair, heads_near)
    heads_full = gather_plane_far(heads_near)
    out_held = swap(out_pair)
    gain_attn = gains[:MODEL_WIDTH]
    gain_mlp = gains[MODEL_WIDTH : 2 * MODEL_WIDTH]
    gain_query = gains[2 * MODEL_WIDTH : 2 * MODEL_WIDTH + HEAD_SIZE][None, :]
    gain_key = gains[2 * MODEL_WIDTH + HEAD_SIZE :][None, :]
    start = (jnp.arange(positions.shape[0], dtype=jnp.int32) - positions)[None, :]
    cosine_part, sine_part = rotary(positions)
    residual_in = hidden_in.astype(jnp.float32)
    normalized = rms_norm(residual_in, gain_attn).astype(jnp.bfloat16)

    attn_pair = gather_near(normalized, True)
    attn_pair, mlp_pair = tied(attn_pair, mlp_pair)
    mlp_held = swap(mlp_pair)
    attn_rows = gather_across(attn_pair, True)
    query, key, value, pre = project(
        attn_rows, heads_full, cosine_part, sine_part, gain_query, gain_key, width_query
    )
    query, out_held = tied(query, out_held)
    out_full = gather_plane_direct(out_held)
    mixed_heads, log_total = attend(query, key, value, start)
    mixed_heads, mlp_held = tied(mixed_heads, mlp_held)
    gate_up_near = gather_plane_near(mlp_held[:, : 2 * width_ff])
    down_held = mlp_held[:, 2 * width_ff :]
    saved = (query, key, value, pre, log_total)
    residual = residual_in + scatter_tokens(
        contract_cols(mixed_heads, out_full).astype(bf16), True
    )
    residual, down_held, out_grad = tied(residual, down_held, out_grad)
    out_grad = swap(out_grad)
    normed_mlp = rms_norm(residual, gain_mlp).astype(jnp.bfloat16)
    mlp_pair = gather_near(normed_mlp, False)
    mlp_pair, down_held, gate_up_near = tied(mlp_pair, down_held, gate_up_near)
    gate_up_full = gather_plane_far(gate_up_near)
    down_full = gather_plane(down_held)
    mlp_rows = gather_across(mlp_pair, False)
    cot_rows = gather_across(gather_near(out_grad, False), False)
    gate_up = matmul(mlp_rows, gate_up_full)
    gate_value = gate_up[:, :width_ff]
    up_value = gate_up[:, width_ff:]
    activated = (jax.nn.silu(gate_value) * up_value).astype(jnp.bfloat16)
    block_part = contract_cols(activated, down_full).astype(bf16)
    down_grad = contract_rows(cot_rows, activated).astype(bf16)
    cot_rows, down_grad = tied(cot_rows, down_grad)
    down_pieces = sum_plane(down_grad)
    d_activated = matmul(cot_rows, down_full)

    def swiglu(gate_in, up_in):
        return jax.nn.silu(gate_in) * up_in

    swiglu_out, swiglu_pull = jax.vjp(swiglu, gate_value, up_value)
    d_gate, d_up = swiglu_pull(d_activated)
    d_gate = d_gate.astype(jnp.bfloat16)
    d_up = d_up.astype(jnp.bfloat16)
    d_gate_up = jnp.concatenate([d_gate, d_up], axis=1)
    gate_up_grad = contract_rows(mlp_rows, d_gate_up)
    gate_up_pieces = sum_plane(gate_up_grad.astype(bf16))
    d_normed_mlp = scatter_tokens(contract_cols(d_gate_up, gate_up_full).astype(bf16), False)
    norm_out, norm_pull = jax.vjp(rms_norm, residual, gain_mlp)
    d_residual_norm, d_gain_mlp = norm_pull(d_normed_mlp)
    d_residual = out_grad.astype(jnp.float32) + d_residual_norm
    state_pair = gather_near(d_residual.astype(bf16), True)
    state_rows = gather_across(state_pair, True)
    out_chunks = sum_far(contract_rows(state_rows, mixed_heads).astype(bf16))
    d_heads, d_gain_heads = attention_backward(
        state_rows, out_full, saved, cosine_part, sine_part, gain_query, gain_key, start
    )
    d_heads, gate_up_pieces, down_pieces, block_part, out_chunks = tied(
        d_heads, gate_up_pieces, down_pieces, block_part, out_chunks
    )
    gate_up_held = cross_sum(gate_up_pieces)
    down_held = cross_sum(down_pieces)
    out_pieces = sum_near(out_chunks)
    heads_grad = contract_rows(attn_rows, d_heads)
    late_chunks = sum_far(heads_grad.astype(bf16))
    late_chunks, out_pieces = tied(late_chunks, out_pieces)
    late_pieces = sum_near(late_chunks)
    out_held = cross_sum(out_pieces)
    late_pieces, gate_up_held, down_held, out_held = tied(
        late_pieces, gate_up_held, down_held, out_held
    )
    late_held = cross_sum(late_pieces)
    gate_up_sum = finish_sum(gate_up_held)
    down_sum = finish_sum(down_held)
    d_normed_pair = scatter_across(contract_cols(d_heads, heads_full).astype(bf16), True)
    block_pair = scatter_across(block_part, False)
    late_held, d_normed_pair, block_pair = tied(late_held, d_normed_pair, block_pair)
    late_sum = finish_sum(late_held)
    out_sum = finish_sum(out_held)
    d_normed = scatter_near(d_normed_pair, True)
    block_out = (residual + scatter_near(block_pair, False)).astype(bf16)
    masters = (
        query_weight,
        key_matrix,
        value_matrix,
        out_weight,
        gate_weight,
        up_weight,
        down_weight,
    )
    moments = (
        query_moment,
        key_momentum,
        value_momentum,
        out_moment,
        gate_moment,
        up_moment,
        down_moment,
    )
    homes = {4: 0, 5: 3, 6: 4, 0: 7, 3: 5, 1: 1, 2: 2}
    group = tuple(range(7))
    reduced, fresh, slots = advance(
        (late_sum, out_sum, gate_up_sum, down_sum), moments, homes, lax.axis_size(DP)
    )
    owned = to_columns(slots)
    owned, d_normed = tied(owned, d_normed)
    pieces = to_homes(group, homes, owned)
    input_out, input_pull = jax.vjp(rms_norm, residual_in, gain_attn)
    d_input_norm, d_gain_attn = input_pull(d_normed)
    input_grad = (d_residual + d_input_norm).astype(bf16)
    gain_grad = jnp.concatenate([d_gain_attn, d_gain_mlp, d_gain_heads.reshape(-1)])
    gain_grad = sum_everywhere(gain_grad, [(name, lax.axis_size(name)) for name in ("core", "pl")])
    pieces, input_grad, block_out, gain_grad = tied(pieces, input_grad, block_out, gain_grad)
    back = orthogonalize(owns(group, homes), pieces)
    input_grad = swap(input_grad)
    block_out = swap(block_out)
    gain_grad = sum_everywhere(gain_grad, [("lo", lax.axis_size("lo"))])
    back, input_grad, block_out, gain_grad = tied(back, input_grad, block_out, gain_grad)
    input_grad = input_grad.astype(jnp.float32)
    block_out = block_out.astype(jnp.float32)
    gain_grad = sum_everywhere(gain_grad, [("hi", 2)])
    updated = update(from_columns(from_homes(group, homes, back)), masters, homes)
    first_next = BETA_FIRST * gain_first + (1.0 - BETA_FIRST) * gain_grad
    second_next = BETA_SECOND * gain_second + (1.0 - BETA_SECOND) * gain_grad * gain_grad
    first_hat = first_next / (1.0 - BETA_FIRST**ADAM_STEP)
    second_hat = second_next / (1.0 - BETA_SECOND**ADAM_STEP)
    gains_next = gains - GAIN_RATE * first_hat / (jnp.sqrt(second_hat) + ADAM_EPS)
    return (
        block_out,
        input_grad,
        reduced[0],
        reduced[1],
        reduced[2],
        reduced[3],
        reduced[4],
        reduced[5],
        reduced[6],
        updated[0],
        updated[1],
        updated[2],
        updated[3],
        updated[4],
        updated[5],
        updated[6],
        fresh[0],
        fresh[1],
        fresh[2],
        fresh[3],
        fresh[4],
        fresh[5],
        fresh[6],
        first_next,
        second_next,
        gains_next,
    )


def solution(mesh):
    dp_count, tensor_count = mesh.shape["dp"], mesh.shape["tensor"]
    split = Mesh(
        mesh.devices.reshape(dp_count // 2, 2, 2, tensor_count // 2), ("pl", "core", "hi", "lo")
    )
    tokens = P(("pl", "core", "hi", "lo"), None)
    rows = P(DP, TENSOR)
    columns = P(TENSOR, DP)
    matrices = (rows, rows, rows, columns, rows, rows, columns)
    whole = (P(), P(), P())
    return jax.shard_map(
        on_device,
        mesh=split,
        in_specs=(tokens, tokens, P(DP)) + matrices + matrices + whole,
        out_specs=(tokens, tokens) + matrices + matrices + matrices + whole,
        check_vma=False,
    )
```

time: 1500 us -> 544 us (0.36)
  waiting for transfers between devices: 975 us -> 255 us
  matrix products: 237 us -> 30.5 us
  starting transfers between devices: 6.98 us -> 146 us
  blocking collectives: 92.1 us -> 0 us
  other arithmetic: 89.9 us -> 35.7 us
  local copies, waits for them, and re-layouts: 72.3 us -> 21.7 us
  Pallas kernels: 0 us -> 46.2 us
    psum x5 -> x0, waiting for transfers between devices: 413 us -> none  [gram_sum(): lax.psum(local_gram.astype(jnp.bfloat16), 'tensor').astype(jnp.float32)]
    reduce_scatter x11 -> x0, waiting for transfers between devices: 318 us -> none  [the longest x1 42.7 us: on_device(): lax.psum_scatter((gate_part + contract_cols(d_up, up_full)).astype(jnp.bf...]
    all_gather x9 -> x0, waiting for transfers between devices: 244 us -> none  [the longest x1 48 us: on_device(): mlp_rows = lax.all_gather(normed_mlp, 'tensor', axis=0, tiled=True)]
    ppermute x0 -> x77, waiting for transfers between devices: none -> 235 us  [the longest x3 101 us: from_homes(): received = received + lax.ppermute(back[step], DP + TENSOR, pairs)]
    dot_general x29 -> x0, matrix products: 163 us -> none  [the longest x5 54.1 us: on_device(): jnp.dot(mixture, current, preferred_element_type=jnp.float32, precision=H...]
    ppermute x0 -> x77, starting transfers between devices: none -> 129 us  [the longest x23 68.3 us: to_partner(): return lax.ppermute(values, name, [(0, 1), (1, 0)])]
    psum x1 -> x0, blocking collectives: 47.4 us -> none  [on_device(): lax.psum(jnp.concatenate([d_gain_attn, d_gain_mlp, d_gain_query, d_gain_k...]
    pallas_call x0 -> x6, Pallas kernels: none -> 46.2 us  [the longest x5 41.6 us: in_vmem(): pl.pallas_call(kernel, out_shape=results, in_specs=[pl.BlockSpec(memory_s...]
  transfers between devices with their start and end apart: 26 -> 79, of which waited for: 22 -> 30; matrix products, arithmetic and copies ran while one was open for 11% -> 10% of each run, Pallas kernels for 0% -> 8%
where the time goes in v1:
time: 544 us; the launch traced here: 538 us
  waiting for transfers between devices  255 us (47%)
  starting transfers between devices  146 us (27%)
  Pallas kernels  46.2 us (8%)
  other arithmetic  35.7 us (7%)
  matrix products  30.5 us (6%)
  local copies, waits for them, and re-layouts  21.7 us (4%)
    ppermute x3, waiting for transfers between devices, from_homes(): received = received + lax.ppermute(back[step], DP + TENSOR, pairs)  101 us
    ppermute x23, waiting for transfers between devices, to_partner(): return lax.ppermute(values, name, [(0, 1), (1, 0)])  68.7 us
    ppermute x23, starting transfers between devices, to_partner(): return lax.ppermute(values, name, [(0, 1), (1, 0)])  68.3 us
    pallas_call x5, Pallas kernels, in_vmem(): pl.pallas_call(kernel, out_shape=results, in_specs=[pl.BlockSpec(memory_s...  41.6 us
    ppermute x31, waiting for transfers between devices, exchange(): lax.ppermute(values, 'pl', [(index, index ^ stride) for index in range(co...  38 us
    ppermute x31, starting transfers between devices, exchange(): lax.ppermute(values, 'pl', [(index, index ^ stride) for index in range(co...  36 us
    ppermute x3, waiting for transfers between devices, to_homes(): lax.ppermute(owned, DP + TENSOR, toward_home(group, homes, step))  21.8 us
    all_to_all x1, waiting for transfers between devices, from_columns(): lax.all_to_all(received.reshape(shape), DP, split_axis=0, concat_axis=0,...  15.4 us
  transfers between devices with their start and end apart: 79, of which 30 were waited for; matrix products, arithmetic and copies ran while one was open for 10% of the time, Pallas kernels for 8%

profile of v1, /device:TPU:0, one launch (start us, length us, event | category | flops | bytes accessed | tf_op | source)
XLA Modules:
  0.0 537.9 jit_solution(7019165464933701138)
XLA Ops:
  9.0 4.6 collective-permute-start.7
  16.7 1.7 collective-permute-start.2
  18.5 4.6 collective-permute-done.4
  25.0 1.6 collective-permute-start.6
  27.6 8.4 %collective-permute-done.6 = bf16[256,1024]{1,0:T(8,128)(2,1)S(1)} collective-permute-done((bf16[256,1024]{1,0:T(8,128)(2,1)S(1)}, bf16[256,1024]{1,0:T(8,128)(2,1)S(1)}, u32[]{:S(2)}, u32[]{:S(2)}) %collective-permute-start.6) | collective-permute-done | bytes 524320 | tf_op jit(solution)/shard_map/ppermute | solution.py:162
  36.4 17.7 %collective-permute-start.8 = (bf16[512,1024]{1,0:T(8,128)(2,1)S(1)}, bf16[512,1024]{1,0:T(8,128)(2,1)S(1)}, u32[]{:S(2)}, u32[]{:S(2)}) collective-permute-start(bf16[512,1024]{1,0:T(8,128)(2,1)S(1)} %pad_maximum_fusion.8), channel_id=1, source_target_pairs={{0,4},{4,0},{1,5},{5,1},{2,6},{6,2},{3,7},{7,3},{8,12},{12,8},{9,1... | collective-permute-start | bytes 3145736 | tf_op jit(solution)/shard_map/ppermute | solution.py:162
  54.1 1.9 fusion.15
  60.6 4.0 collective-permute-done.9
  67.7 7.0 %shard_map.395 = (bf16[1024,512]{1,0:T(8,128)(2,1)S(1)}, bf16[1024,256]{1,0:T(8,128)(2,1)S(1)}, bf16[1024,256]{1,0:T(8,128)(2,1)S(1)}, f32[1024,768]{1,0:T(8,128)}) custom-call(bf16[1024,1024]{1,0:T(8,128)(2,1)S(1)} %pad_maximum_fusion.1.rows_ref, bf16[1024,1024]{1,0:T(8,128)(2,1)} %copy-done.39, f32[1024,128]{1,0:T(8,128)S(1)} %get-tuple-element.290.cosine_ref, ...), custom_call_target="tpu_custom_call" | custom-call | flops 2147483648 | bytes 10486784 | tf_op jit(solution)/shard_map/pallas_call | solution.py:503
  78.3 9.9 %shard_map.396 = (bf16[1024,512]{1,0:T(8,128)(2,1)S(1)}, f32[4,1024]{1,0:T(4,128)S(1)}) custom-call(bf16[1024,512]{1,0:T(8,128)(2,1)S(1)} %get-tuple-element.140.query_ref, bf16[1024,256]{1,0:T(8,128)(2,1)S(1)} %get-tuple-element.141.key_ref, bf16[1024,256]{1,0:T(8,128)(2,1)S(1)} %get-tuple-element.142.value_ref, s32[1,1024]{1,0:T(1,128)S(1)} %bitcast.32), custom_call_target="tpu_custom_call" | custom-call | flops 2147483648 | bytes 3166208 | tf_op jit(solution)/shard_map/pallas_call | solution.py:503
  88.4 1.9 collective-permute-done.15
  93.4 4.1 collective-permute-start.17
  97.5 2.6 collective-permute-done.17
  100.1 1.9 convert_add_fusion.3
  107.0 1.6 collective-permute-start.23
  110.1 8.7 %collective-permute-done.18 = bf16[256,1024]{1,0:T(8,128)(2,1)} collective-permute-done((bf16[256,1024]{1,0:T(8,128)(2,1)}, bf16[256,1024]{1,0:T(8,128)(2,1)}, u32[]{:S(2)}, u32[]{:S(2)}) %collective-permute-start.18) | collective-permute-done | bytes 524320 | tf_op jit(solution)/shard_map/ppermute | solution.py:162
  118.9 1.6 convert_add_fusion.4
  123.0 17.7 %collective-permute-done.22 = bf16[256,1024]{1,0:T(8,128)(2,1)S(1)} collective-permute-done((bf16[256,1024]{1,0:T(8,128)(2,1)S(1)}, bf16[256,1024]{1,0:T(8,128)(2,1)S(1)}, u32[]{:S(2)}, u32[]{:S(2)}) %collective-permute-start.22) | collective-permute-done | bytes 524320 | tf_op jit(solution)/shard_map/ppermute | solution.py:162
  140.8 1.6 collective-permute-start.28
  145.7 8.7 %collective-permute-done.29 = bf16[256,768]{1,0:T(8,128)(2,1)S(1)} collective-permute-done((bf16[256,768]{1,0:T(8,128)(2,1)S(1)}, bf16[256,768]{1,0:T(8,128)(2,1)S(1)}, u32[]{:S(2)}, u32[]{:S(2)}) %collective-permute-start.29) | collective-permute-done | bytes 393248 | tf_op jit(solution)/shard_map/ppermute | solution.py:216
  155.1 5.9 %collective-permute-done.26 = bf16[128,1536]{1,0:T(8,128)(2,1)S(1)} collective-permute-done((bf16[128,1536]{1,0:T(8,128)(2,1)S(1)}, bf16[128,1536]{1,0:T(8,128)(2,1)S(1)}, u32[]{:S(2)}, u32[]{:S(2)}) %collective-permute-start.26) | collective-permute-done | bytes 393248 | tf_op jit(solution)/shard_map/ppermute | solution.py:216
  163.8 2.9 collective-permute-done.31
  168.3 3.4 fusion.26
  172.7 3.2 convolution_convert_fusion.5
  175.9 3.4 fusion.2
  179.3 3.7 fusion.5
  185.3 3.8 convolution_convert_fusion.4
  189.2 1.8 convert_add_fusion.2
  192.0 4.1 convolution_convert_fusion
  196.2 1.6 collective-permute-start.42
  199.4 6.1 %collective-permute-done.33 = bf16[256,1024]{1,0:T(8,128)(2,1)S(1)} collective-permute-done((bf16[256,1024]{1,0:T(8,128)(2,1)S(1)}, bf16[256,1024]{1,0:T(8,128)(2,1)S(1)}, u32[]{:S(2)}, u32[]{:S(2)}) %collective-permute-start.33) | collective-permute-done | bytes 524320 | tf_op jit(solution)/shard_map/ppermute | solution.py:162
  207.6 1.6 collective-permute-start.38
  212.1 8.7 %collective-permute-done.34 = bf16[256,1024]{1,0:T(8,128)(2,1)S(1)} collective-permute-done((bf16[256,1024]{1,0:T(8,128)(2,1)S(1)}, bf16[256,1024]{1,0:T(8,128)(2,1)S(1)}, u32[]{:S(2)}, u32[]{:S(2)}) %collective-permute-start.34) | collective-permute-done | bytes 524320 | tf_op jit(solution)/shard_map/ppermute | solution.py:162
  223.6 1.6 collective-permute-start.37
  229.2 1.6 collective-permute-start.44
  230.8 20.4 %shard_map.397 = (bf16[1024,1024]{1,0:T(8,128)(2,1)}, f32[2,128]{1,0:T(2,128)S(1)}) custom-call(bf16[1024,1024]{1,0:T(8,128)(2,1)} %pad_maximum_fusion.2.state_ref, bf16[1024,512]{1,0:T(8,128)(2,1)S(1)} %constant_dynamic-update-slice_fusion.10.out_ref, bf16[1024,512]{1,0:T(8,128)(2,1)S(1)} %get-tuple-element.140.query_ref, bf16[1024,256]{1,0:T(8,128)(2,1)S(1)} %copy-done.17, ...), custom_call_target="tpu_custom_call" | custom-call | flops 6442450944 | bytes 11556864 | tf_op jit(solution)/shard_map/pallas_call | solution.py:503
  253.2 3.0 collective-permute-done.45
  256.2 4.0 convolution_convert_fusion.2
  261.6 1.6 collective-permute-start.48
  270.5 2.3 collective-permute-done.48
  276.1 2.4 convolution_convert_fusion.1
  278.7 21.5 %collective-permute-start.56 = (bf16[512,1024]{1,0:T(8,128)(2,1)S(1)}, bf16[512,1024]{1,0:T(8,128)(2,1)S(1)}, u32[]{:S(2)}, u32[]{:S(2)}) collective-permute-start(bf16[512,1024]{1,0:T(8,128)(2,1)S(1)} %constant_dynamic-slice_fusion.10), channel_id=1, source_target_pairs={{0,4},{4,0},{1,5},{5,1},{2,6},{6,2},{3,7},{7,3},{8,12},{12,8},{9,1... | collective-permute-start | bytes 3145736 | tf_op jit(solution)/shard_map/ppermute | solution.py:162
  300.2 2.8 collective-permute-start.57
  308.2 2.0 convert_add_fusion.1
  310.3 10.1 %collective-permute-start.58 = (bf16[128,1024]{1,0:T(8,128)(2,1)S(1)}, bf16[128,1024]{1,0:T(8,128)(2,1)S(1)}, u32[]{:S(2)}, u32[]{:S(2)}) collective-permute-start(bf16[128,1024]{1,0:T(8,128)(2,1)S(1)} %constant_dynamic-slice_fusion.9), channel_id=1, source_target_pairs={{0,4},{4,0},{1,5},{5,1},{2,6},{6,2},{3,7},{7,3},{8,12},{12,8},{9,1... | collective-permute-start | bytes 786440 | tf_op jit(solution)/shard_map/ppermute | solution.py:162
  321.7 2.9 shard_map.398
  324.6 4.3 all-to-all-start
  330.5 2.1 collective-permute-start.66
  332.6 12.6 %collective-permute-done.62 = bf16[256,1024]{1,0:T(8,128)(2,1)S(1)} collective-permute-done((bf16[256,1024]{1,0:T(8,128)(2,1)S(1)}, bf16[256,1024]{1,0:T(8,128)(2,1)S(1)}, u32[]{:S(2)}, u32[]{:S(2)}) %collective-permute-start.62) | collective-permute-done | bytes 524320 | tf_op jit(solution)/shard_map/ppermute | solution.py:162
  345.4 4.6 all-to-all-done
  349.9 1.8 collective-permute-start.63
  351.7 1.9 collective-permute-start.64
  353.7 2.4 collective-permute-start.65
  356.6 1.7 add_convert_fusion.1
  359.4 2.6 collective-permute-done.68
  363.4 2.3 collective-permute-done.69
  365.7 21.8 %collective-permute-done.65.refs_3_ = bf16[1024,768]{1,0:T(8,128)(2,1)} collective-permute-done((bf16[1024,768]{1,0:T(8,128)(2,1)}, bf16[1024,768]{1,0:T(8,128)(2,1)}, u32[]{:S(2)}, u32[]{:S(2)}) %collective-permute-start.65) | collective-permute-done | bytes 1572896 | tf_op jit(solution)/shard_map/ppermute | solution.py:601
  388.9 2.5 collective-permute-start.72
  391.5 4.6 shard_map.399
  399.5 101.5 %collective-permute-done.75 = bf16[1024,768]{1,0:T(8,128)(2,1)S(1)} collective-permute-done((bf16[1024,768]{1,0:T(8,128)(2,1)}, bf16[1024,768]{1,0:T(8,128)(2,1)S(1)}, u32[]{:S(2)}, u32[]{:S(2)}) %collective-permute-start.75) | collective-permute-done | bytes 1572896 | tf_op jit(solution)/shard_map/ppermute | solution.py:611
  502.4 12.5 %all-to-all-start.1 = ((bf16[8,128,768]{2,1,0:T(8,128)(2,1)}), bf16[8,128,768]{2,1,0:T(8,128)(2,1)S(1)}, u32[]{:S(2)}, u32[]{:S(2)}) async-start(bf16[8,128,768]{2,1,0:T(8,128)(2,1)} %bitcast.8), calls=%async_computation.1 | async-start | bytes 3145728 | tf_op jit(solution)/shard_map/all_to_all | solution.py:617
  515.1 2.2 convert_element_type.361
  517.4 2.1 convert_element_type.362
  520.6 15.4 %all-to-all-done.1.returned_ref = bf16[8,128,768]{2,1,0:T(8,128)(2,1)S(1)} async-done(((bf16[8,128,768]{2,1,0:T(8,128)(2,1)}), bf16[8,128,768]{2,1,0:T(8,128)(2,1)S(1)}, u32[]{:S(2)}, u32[]{:S(2)}) %all-to-all-start.1) | async-done | bytes 1572896 | tf_op jit(solution)/shard_map/all_to_all | solution.py:617
  (378 shorter events, 98.0 us)
Async XLA Ops:
  5.2 13.2 %collective-permute-start.3 = (bf16[128,512]{1,0:T(8,128)(2,1)S(1)}, bf16[128,512]{1,0:T(8,128)(2,1)S(1)}, u32[]{:S(2)}, u32[]{:S(2)}) collective-permute-start(bf16[128,512]{1,0:T(8,128)(2,1)S(1)} %bitcast.38), channel_id=1, source_target_pairs={{0,4},{4,0},{1,5},{5,1},{2,6},{6,2},{3,7},{7,3},{8,12},{12,8},{9,1... | collective-permute-start | bytes 393224 | tf_op jit(solution)/shard_map/ppermute | solution.py:162
  9.0 17.6 %collective-permute-start.7 = (bf16[128,2304]{1,0:T(8,128)(2,1)}, bf16[128,2304]{1,0:T(8,128)(2,1)S(1)}, u32[]{:S(2)}, u32[]{:S(2)}) collective-permute-start(bf16[128,2304]{1,0:T(8,128)(2,1)} %pad_maximum_fusion.14), channel_id=1, source_target_pairs={{0,4},{4,0},{1,5},{5,1},{2,6},{6,2},{3,7},{7,3},{8,12},{12,8},{9,1... | collective-permute-start | bytes 1769480 | tf_op jit(solution)/shard_map/ppermute | solution.py:162
  13.6 9.5 %collective-permute-start.4 = (bf16[256,1024]{1,0:T(8,128)(2,1)}, bf16[256,1024]{1,0:T(8,128)(2,1)S(1)}, u32[]{:S(2)}, u32[]{:S(2)}) collective-permute-start(bf16[256,1024]{1,0:T(8,128)(2,1)} %collective-permute-done.1), channel_id=1, source_target_pairs={{0,8},{8,0},{16,24},{24,16},{1,9},{9,1},{17,25},{25,17},{2,10},{10... | collective-permute-start | bytes 1572872 | tf_op jit(solution)/shard_map/ppermute | solution.py:216
  15.2 9.4 %collective-permute-start.5 = (bf16[256,1024]{1,0:T(8,128)(2,1)}, bf16[256,1024]{1,0:T(8,128)(2,1)S(1)}, u32[]{:S(2)}, u32[]{:S(2)}) collective-permute-start(bf16[256,1024]{1,0:T(8,128)(2,1)} %collective-permute-done.1), channel_id=1, source_target_pairs={{0,16},{8,24},{16,0},{24,8},{1,17},{9,25},{17,1},{25,9},{2,18},{10... | collective-permute-start | bytes 1572872 | tf_op jit(solution)/shard_map/ppermute | solution.py:216
  25.0 11.0 %collective-permute-start.6 = (bf16[256,1024]{1,0:T(8,128)(2,1)S(1)}, bf16[256,1024]{1,0:T(8,128)(2,1)S(1)}, u32[]{:S(2)}, u32[]{:S(2)}) collective-permute-start(bf16[256,1024]{1,0:T(8,128)(2,1)S(1)} %fusion.8), channel_id=1, source_target_pairs={{0,1},{1,0},{2,3},{3,2},{4,5},{5,4},{6,7},{7,6},{8,9},{9,8},{10,11... | collective-permute-start | bytes 1572872 | tf_op jit(solution)/shard_map/ppermute | solution.py:162
  26.9 27.2 %collective-permute-start.11 = (s32[1024]{0:T(1024)S(1)}, s32[1024]{0:T(1024)S(1)}, u32[]{:S(2)}, u32[]{:S(2)}) collective-permute-start(s32[1024]{0:T(1024)S(1)} %copy-done.57), channel_id=1, source_target_pairs={{0,0},{2,4},{4,2},{6,6},{1,1},{3,5},{5,3},{7,7},{8,8},{10,12},{12,... | collective-permute-start | bytes 12296 | tf_op jit(solution)/shard_map/ppermute | solution.py:158
  36.4 28.6 %collective-permute-start.8 = (bf16[512,1024]{1,0:T(8,128)(2,1)S(1)}, bf16[512,1024]{1,0:T(8,128)(2,1)S(1)}, u32[]{:S(2)}, u32[]{:S(2)}) collective-permute-start(bf16[512,1024]{1,0:T(8,128)(2,1)S(1)} %pad_maximum_fusion.8), channel_id=1, source_target_pairs={{0,4},{4,0},{1,5},{5,1},{2,6},{6,2},{3,7},{7,3},{8,12},{12,8},{9,1... | collective-permute-start | bytes 3145736 | tf_op jit(solution)/shard_map/ppermute | solution.py:162
  56.4 8.3 %collective-permute-start.9 = (bf16[128,1024]{1,0:T(8,128)(2,1)S(1)}, bf16[128,1024]{1,0:T(8,128)(2,1)S(1)}, u32[]{:S(2)}, u32[]{:S(2)}) collective-permute-start(bf16[128,1024]{1,0:T(8,128)(2,1)S(1)} %slice.115), channel_id=1, source_target_pairs={{0,8},{8,0},{16,24},{24,16},{1,9},{9,1},{17,25},{25,17},{2,10},{10... | collective-permute-start | bytes 786440 | tf_op jit(solution)/shard_map/ppermute | solution.py:216
  57.0 8.0 %collective-permute-start.10 = (bf16[128,1024]{1,0:T(8,128)(2,1)S(1)}, bf16[128,1024]{1,0:T(8,128)(2,1)S(1)}, u32[]{:S(2)}, u32[]{:S(2)}) collective-permute-start(bf16[128,1024]{1,0:T(8,128)(2,1)S(1)} %slice.116), channel_id=1, source_target_pairs={{0,16},{8,24},{16,0},{24,8},{1,17},{9,25},{17,1},{25,9},{2,18},{10... | collective-permute-start | bytes 786440 | tf_op jit(solution)/shard_map/ppermute | solution.py:216
  57.6 17.2 %collective-permute-start.12 = (bf16[256,512]{1,0:T(8,128)(2,1)S(1)}, bf16[256,512]{1,0:T(8,128)(2,1)S(1)}, u32[]{:S(2)}, u32[]{:S(2)}) collective-permute-start(bf16[256,512]{1,0:T(8,128)(2,1)S(1)} %pad_maximum_fusion.23), channel_id=1, source_target_pairs={{0,0},{2,4},{4,2},{6,6},{1,1},{3,5},{5,3},{7,7},{8,8},{10,12},{12,... | collective-permute-start | bytes 786440 | tf_op jit(solution)/shard_map/ppermute | solution.py:158
  59.7 28.6 %collective-permute-start.13 = (bf16[256,2304]{1,0:T(8,128)(2,1)S(1)}, bf16[256,2304]{1,0:T(8,128)(2,1)S(1)}, u32[]{:S(2)}, u32[]{:S(2)}) collective-permute-start(bf16[256,2304]{1,0:T(8,128)(2,1)S(1)} %pad_maximum_fusion.7), channel_id=1, source_target_pairs={{0,0},{2,4},{4,2},{6,6},{1,1},{3,5},{5,3},{7,7},{8,8},{10,12},{12,... | collective-permute-start | bytes 3538952 | tf_op jit(solution)/shard_map/ppermute | solution.py:158
  74.7 13.6 %collective-permute-start.14 = (bf16[256,512]{1,0:T(8,128)(2,1)S(1)}, bf16[256,512]{1,0:T(8,128)(2,1)S(1)}, u32[]{:S(2)}, u32[]{:S(2)}) collective-permute-start(bf16[256,512]{1,0:T(8,128)(2,1)S(1)} %collective-permute-done.12), channel_id=1, source_target_pairs={{0,8},{8,0},{16,24},{24,16},{1,9},{9,1},{17,25},{25,17},{2,10},{10... | collective-permute-start | bytes 786440 | tf_op jit(solution)/shard_map/ppermute | solution.py:216
  76.3 14.0 %collective-permute-start.15 = (bf16[256,512]{1,0:T(8,128)(2,1)S(1)}, bf16[256,512]{1,0:T(8,128)(2,1)S(1)}, u32[]{:S(2)}, u32[]{:S(2)}) collective-permute-start(bf16[256,512]{1,0:T(8,128)(2,1)S(1)} %collective-permute-done.12), channel_id=1, source_target_pairs={{0,16},{8,24},{16,0},{24,8},{1,17},{9,25},{17,1},{25,9},{2,18},{10... | collective-permute-start | bytes 786440 | tf_op jit(solution)/shard_map/ppermute | solution.py:216
  76.8 13.5 %collective-permute-start.16 = (bf16[256,512]{1,0:T(8,128)(2,1)S(1)}, bf16[256,512]{1,0:T(8,128)(2,1)S(1)}, u32[]{:S(2)}, u32[]{:S(2)}) collective-permute-start(bf16[256,512]{1,0:T(8,128)(2,1)S(1)} %collective-permute-done.12), channel_id=1, source_target_pairs={{0,24},{8,16},{16,8},{24,0},{1,25},{9,17},{17,9},{25,1},{2,26},{10... | collective-permute-start | bytes 786440 | tf_op jit(solution)/shard_map/ppermute | solution.py:216
  104.3 14.5 %collective-permute-start.18 = (bf16[256,1024]{1,0:T(8,128)(2,1)}, bf16[256,1024]{1,0:T(8,128)(2,1)}, u32[]{:S(2)}, u32[]{:S(2)}) collective-permute-start(bf16[256,1024]{1,0:T(8,128)(2,1)} %dynamic-slice_convert_fusion.1), channel_id=1, source_target_pairs={{0,1},{1,0},{2,3},{3,2},{4,5},{5,4},{6,7},{7,6},{8,9},{9,8},{10,11... | collective-permute-start | bytes 1572872 | tf_op jit(solution)/shard_map/ppermute | solution.py:162
  107.0 33.7 %collective-permute-start.23 = (bf16[256,1536]{1,0:T(8,128)(2,1)S(1)}, bf16[256,1536]{1,0:T(8,128)(2,1)S(1)}, u32[]{:S(2)}, u32[]{:S(2)}) collective-permute-start(bf16[256,1536]{1,0:T(8,128)(2,1)S(1)} %slice.121), channel_id=1, source_target_pairs={{0,8},{8,0},{16,24},{24,16},{1,9},{9,1},{17,25},{25,17},{2,10},{10... | collective-permute-start | bytes 2359304 | tf_op jit(solution)/shard_map/ppermute | solution.py:216
  108.6 32.2 %collective-permute-start.24 = (bf16[256,1536]{1,0:T(8,128)(2,1)S(1)}, bf16[256,1536]{1,0:T(8,128)(2,1)S(1)}, u32[]{:S(2)}, u32[]{:S(2)}) collective-permute-start(bf16[256,1536]{1,0:T(8,128)(2,1)S(1)} %slice.121), channel_id=1, source_target_pairs={{0,16},{8,24},{16,0},{24,8},{1,17},{9,25},{17,1},{25,9},{2,18},{10... | collective-permute-start | bytes 2359304 | tf_op jit(solution)/shard_map/ppermute | solution.py:216
  121.6 19.1 %collective-permute-start.22 = (bf16[256,1024]{1,0:T(8,128)(2,1)S(1)}, bf16[256,1024]{1,0:T(8,128)(2,1)S(1)}, u32[]{:S(2)}, u32[]{:S(2)}) collective-permute-start(bf16[256,1024]{1,0:T(8,128)(2,1)S(1)} %multiply_convert_fusion.2), channel_id=1, source_target_pairs={{0,1},{1,0},{2,3},{3,2},{4,5},{5,4},{6,7},{7,6},{8,9},{9,8},{10,11... | collective-permute-start | bytes 1572872 | tf_op jit(solution)/shard_map/ppermute | solution.py:162
  122.1 23.4 %collective-permute-start.19 = (bf16[256,1024]{1,0:T(8,128)(2,1)S(1)}, bf16[256,1024]{1,0:T(8,128)(2,1)S(1)}, u32[]{:S(2)}, u32[]{:S(2)}) collective-permute-start(bf16[256,1024]{1,0:T(8,128)(2,1)S(1)} %copy-done.56), channel_id=1, source_target_pairs={{0,0},{2,4},{4,2},{6,6},{1,1},{3,5},{5,3},{7,7},{8,8},{10,12},{12,... | collective-permute-start | bytes 1572872 | tf_op jit(solution)/shard_map/ppermute | solution.py:158
  140.8 13.6 %collective-permute-start.28 = (bf16[256,768]{1,0:T(8,128)(2,1)S(1)}, bf16[256,768]{1,0:T(8,128)(2,1)S(1)}, u32[]{:S(2)}, u32[]{:S(2)}) collective-permute-start(bf16[256,768]{1,0:T(8,128)(2,1)S(1)} %slice.119), channel_id=1, source_target_pairs={{0,8},{8,0},{16,24},{24,16},{1,9},{9,1},{17,25},{25,17},{2,10},{10... | collective-permute-start | bytes 1179656 | tf_op jit(solution)/shard_map/ppermute | solution.py:216
  142.4 12.1 %collective-permute-start.29 = (bf16[256,768]{1,0:T(8,128)(2,1)S(1)}, bf16[256,768]{1,0:T(8,128)(2,1)S(1)}, u32[]{:S(2)}, u32[]{:S(2)}) collective-permute-start(bf16[256,768]{1,0:T(8,128)(2,1)S(1)} %slice.119), channel_id=1, source_target_pairs={{0,16},{8,24},{16,0},{24,8},{1,17},{9,25},{17,1},{25,9},{2,18},{10... | collective-permute-start | bytes 1179656 | tf_op jit(solution)/shard_map/ppermute | solution.py:216
  144.4 16.7 %collective-permute-start.26 = (bf16[128,1536]{1,0:T(8,128)(2,1)S(1)}, bf16[128,1536]{1,0:T(8,128)(2,1)S(1)}, u32[]{:S(2)}, u32[]{:S(2)}) collective-permute-start(bf16[128,1536]{1,0:T(8,128)(2,1)S(1)} %slice.122), channel_id=1, source_target_pairs={{0,8},{8,0},{16,24},{24,16},{1,9},{9,1},{17,25},{25,17},{2,10},{10... | collective-permute-start | bytes 1179656 | tf_op jit(solution)/shard_map/ppermute | solution.py:216
  145.0 17.6 %collective-permute-start.27 = (bf16[128,1536]{1,0:T(8,128)(2,1)S(1)}, bf16[128,1536]{1,0:T(8,128)(2,1)S(1)}, u32[]{:S(2)}, u32[]{:S(2)}) collective-permute-start(bf16[128,1536]{1,0:T(8,128)(2,1)S(1)} %slice.123), channel_id=1, source_target_pairs={{0,16},{8,24},{16,0},{24,8},{1,17},{9,25},{17,1},{25,9},{2,18},{10... | collective-permute-start | bytes 1179656 | tf_op jit(solution)/shard_map/ppermute | solution.py:216
  145.5 21.3 %collective-permute-start.25 = (bf16[512,1024]{1,0:T(8,128)(2,1)S(1)}, bf16[512,1024]{1,0:T(8,128)(2,1)S(1)}, u32[]{:S(2)}, u32[]{:S(2)}) collective-permute-start(bf16[512,1024]{1,0:T(8,128)(2,1)S(1)} %pad_maximum_fusion.10), channel_id=1, source_target_pairs={{0,4},{4,0},{1,5},{5,1},{2,6},{6,2},{3,7},{7,3},{8,12},{12,8},{9,1... | collective-permute-start | bytes 3145736 | tf_op jit(solution)/shard_map/ppermute | solution.py:162
  154.4 9.2 %collective-permute-start.20 = (bf16[256,1024]{1,0:T(8,128)(2,1)S(1)}, bf16[256,1024]{1,0:T(8,128)(2,1)S(1)}, u32[]{:S(2)}, u32[]{:S(2)}) collective-permute-start(bf16[256,1024]{1,0:T(8,128)(2,1)S(1)} %collective-permute-done.19), channel_id=1, source_target_pairs={{0,1},{1,0},{2,3},{3,2},{4,5},{5,4},{6,7},{7,6},{8,9},{9,8},{10,11... | collective-permute-start | bytes 1572872 | tf_op jit(solution)/shard_map/ppermute | solution.py:162
  154.4 9.4 %collective-permute-start.30 = (bf16[128,768]{1,0:T(8,128)(2,1)S(1)}, bf16[128,768]{1,0:T(8,128)(2,1)S(1)}, u32[]{:S(2)}, u32[]{:S(2)}) collective-permute-start(bf16[128,768]{1,0:T(8,128)(2,1)S(1)} %slice.154), channel_id=1, source_target_pairs={{0,8},{8,0},{16,24},{24,16},{1,9},{9,1},{17,25},{25,17},{2,10},{10... | collective-permute-start | bytes 589832 | tf_op jit(solution)/shard_map/ppermute | solution.py:216
  163.7 9.0 %collective-permute-start.21 = (bf16[512,1024]{1,0:T(8,128)(2,1)S(1)}, bf16[512,1024]{1,0:T(8,128)(2,1)S(1)}, u32[]{:S(2)}, u32[]{:S(2)}) collective-permute-start(bf16[512,1024]{1,0:T(8,128)(2,1)S(1)} %pad_maximum_fusion.9), channel_id=1, source_target_pairs={{0,4},{4,0},{1,5},{5,1},{2,6},{6,2},{3,7},{7,3},{8,12},{12,8},{9,1... | collective-permute-start | bytes 3145736 | tf_op jit(solution)/shard_map/ppermute | solution.py:162
  191.1 14.4 %collective-permute-start.33 = (bf16[256,1024]{1,0:T(8,128)(2,1)S(1)}, bf16[256,1024]{1,0:T(8,128)(2,1)S(1)}, u32[]{:S(2)}, u32[]{:S(2)}) collective-permute-start(bf16[256,1024]{1,0:T(8,128)(2,1)S(1)} %dynamic_slice.204), channel_id=1, source_target_pairs={{0,1},{1,0},{2,3},{3,2},{4,5},{5,4},{6,7},{7,6},{8,9},{9,8},{10,11... | collective-permute-start | bytes 1572872 | tf_op jit(solution)/shard_map/ppermute | solution.py:162
  196.2 14.5 %collective-permute-start.42 = (bf16[128,768]{1,0:T(8,128)(2,1)S(1)}, bf16[128,768]{1,0:T(8,128)(2,1)S(1)}, u32[]{:S(2)}, u32[]{:S(2)}) collective-permute-start(bf16[128,768]{1,0:T(8,128)(2,1)S(1)} %get-tuple-element.262), channel_id=1, source_target_pairs={{0,8},{8,0},{16,24},{24,16},{1,9},{9,1},{17,25},{25,17},{2,10},{10... | collective-permute-start | bytes 589832 | tf_op jit(solution)/shard_map/ppermute | solution.py:216
  197.7 12.9 %collective-permute-start.40 = (bf16[128,768]{1,0:T(8,128)(2,1)S(1)}, bf16[128,768]{1,0:T(8,128)(2,1)S(1)}, u32[]{:S(2)}, u32[]{:S(2)}) collective-permute-start(bf16[128,768]{1,0:T(8,128)(2,1)S(1)} %get-tuple-element.263), channel_id=1, source_target_pairs={{0,16},{8,24},{16,0},{24,8},{1,17},{9,25},{17,1},{25,9},{2,18},{10... | collective-permute-start | bytes 589832 | tf_op jit(solution)/shard_map/ppermute | solution.py:216
  207.2 13.6 %collective-permute-start.34 = (bf16[256,1024]{1,0:T(8,128)(2,1)S(1)}, bf16[256,1024]{1,0:T(8,128)(2,1)S(1)}, u32[]{:S(2)}, u32[]{:S(2)}) collective-permute-start(bf16[256,1024]{1,0:T(8,128)(2,1)S(1)} %get-tuple-element.241), channel_id=1, source_target_pairs={{0,1},{1,0},{2,3},{3,2},{4,5},{5,4},{6,7},{7,6},{8,9},{9,8},{10,11... | collective-permute-start | bytes 1572872 | tf_op jit(solution)/shard_map/ppermute | solution.py:162
  207.6 15.7 %collective-permute-start.38 = (bf16[128,1536]{1,0:T(8,128)(2,1)S(1)}, bf16[128,1536]{1,0:T(8,128)(2,1)S(1)}, u32[]{:S(2)}, u32[]{:S(2)}) collective-permute-start(bf16[128,1536]{1,0:T(8,128)(2,1)S(1)} %get-tuple-element.247), channel_id=1, source_target_pairs={{0,8},{8,0},{16,24},{24,16},{1,9},{9,1},{17,25},{25,17},{2,10},{10... | collective-permute-start | bytes 1179656 | tf_op jit(solution)/shard_map/ppermute | solution.py:216
  209.1 14.2 %collective-permute-start.36 = (bf16[128,1536]{1,0:T(8,128)(2,1)S(1)}, bf16[128,1536]{1,0:T(8,128)(2,1)S(1)}, u32[]{:S(2)}, u32[]{:S(2)}) collective-permute-start(bf16[128,1536]{1,0:T(8,128)(2,1)S(1)} %get-tuple-element.248), channel_id=1, source_target_pairs={{0,16},{8,24},{16,0},{24,8},{1,17},{9,25},{17,1},{25,9},{2,18},{10... | collective-permute-start | bytes 1179656 | tf_op jit(solution)/shard_map/ppermute | solution.py:216
  211.6 39.7 %collective-permute-start.41 = (bf16[256,768]{1,0:T(8,128)(2,1)}, bf16[256,768]{1,0:T(8,128)(2,1)}, u32[]{:S(2)}, u32[]{:S(2)}) collective-permute-start(bf16[256,768]{1,0:T(8,128)(2,1)} %pad_maximum_fusion.20), channel_id=1, source_target_pairs={{0,8},{8,0},{16,24},{24,16},{1,9},{9,1},{17,25},{25,17},{2,10},{10... | collective-permute-start | bytes 1179656 | tf_op jit(solution)/shard_map/ppermute | solution.py:216
  221.8 30.1 %collective-permute-start.43 = (bf16[256,768]{1,0:T(8,128)(2,1)}, bf16[256,768]{1,0:T(8,128)(2,1)}, u32[]{:S(2)}, u32[]{:S(2)}) collective-permute-start(bf16[256,768]{1,0:T(8,128)(2,1)} %pad_maximum_fusion.21), channel_id=1, source_target_pairs={{0,16},{8,24},{16,0},{24,8},{1,17},{9,25},{17,1},{25,9},{2,18},{10... | collective-permute-start | bytes 1179656 | tf_op jit(solution)/shard_map/ppermute | solution.py:216
  223.6 28.3 %collective-permute-start.37 = (bf16[256,1536]{1,0:T(8,128)(2,1)S(1)}, bf16[256,1536]{1,0:T(8,128)(2,1)}, u32[]{:S(2)}, u32[]{:S(2)}) collective-permute-start(bf16[256,1536]{1,0:T(8,128)(2,1)S(1)} %pad_maximum_fusion.12), channel_id=1, source_target_pairs={{0,8},{8,0},{16,24},{24,16},{1,9},{9,1},{17,25},{25,17},{2,10},{10... | collective-permute-start | bytes 2359304 | tf_op jit(solution)/shard_map/ppermute | solution.py:216
  225.2 26.7 %collective-permute-start.39 = (bf16[256,1536]{1,0:T(8,128)(2,1)S(1)}, bf16[256,1536]{1,0:T(8,128)(2,1)S(1)}, u32[]{:S(2)}, u32[]{:S(2)}) collective-permute-start(bf16[256,1536]{1,0:T(8,128)(2,1)S(1)} %pad_maximum_fusion.13), channel_id=1, source_target_pairs={{0,16},{8,24},{16,0},{24,8},{1,17},{9,25},{17,1},{25,9},{2,18},{10... | collective-permute-start | bytes 2359304 | tf_op jit(solution)/shard_map/ppermute | solution.py:216
  229.2 24.0 %collective-permute-start.44 = (bf16[128,512]{1,0:T(8,128)(2,1)S(1)}, bf16[128,512]{1,0:T(8,128)(2,1)S(1)}, u32[]{:S(2)}, u32[]{:S(2)}) collective-permute-start(bf16[128,512]{1,0:T(8,128)(2,1)S(1)} %get-tuple-element.269), channel_id=1, source_target_pairs={{0,16},{8,24},{16,0},{24,8},{1,17},{9,25},{17,1},{25,9},{2,18},{10... | collective-permute-start | bytes 393224 | tf_op jit(solution)/shard_map/ppermute | solution.py:216
  260.5 9.3 %collective-permute-start.46 = (bf16[128,1024]{1,0:T(8,128)(2,1)S(1)}, bf16[128,1024]{1,0:T(8,128)(2,1)S(1)}, u32[]{:S(2)}, u32[]{:S(2)}) collective-permute-start(bf16[128,1024]{1,0:T(8,128)(2,1)S(1)} %get-tuple-element.252), channel_id=1, source_target_pairs={{0,16},{8,24},{16,0},{24,8},{1,17},{9,25},{17,1},{25,9},{2,18},{10... | collective-permute-start | bytes 786440 | tf_op jit(solution)/shard_map/ppermute | solution.py:216
  261.0 9.4 %collective-permute-start.47 = (bf16[128,1024]{1,0:T(8,128)(2,1)S(1)}, bf16[128,1024]{1,0:T(8,128)(2,1)S(1)}, u32[]{:S(2)}, u32[]{:S(2)}) collective-permute-start(bf16[128,1024]{1,0:T(8,128)(2,1)S(1)} %get-tuple-element.251), channel_id=1, source_target_pairs={{0,8},{8,0},{16,24},{24,16},{1,9},{9,1},{17,25},{25,17},{2,10},{10... | collective-permute-start | bytes 786440 | tf_op jit(solution)/shard_map/ppermute | solution.py:216
  261.6 11.2 %collective-permute-start.48 = (bf16[256,512]{1,0:T(8,128)(2,1)S(1)}, bf16[256,512]{1,0:T(8,128)(2,1)S(1)}, u32[]{:S(2)}, u32[]{:S(2)}) collective-permute-start(bf16[256,512]{1,0:T(8,128)(2,1)S(1)} %pad_maximum_fusion.24), channel_id=1, source_target_pairs={{0,8},{8,0},{16,24},{24,16},{1,9},{9,1},{17,25},{25,17},{2,10},{10... | collective-permute-start | bytes 786440 | tf_op jit(solution)/shard_map/ppermute | solution.py:216
  263.3 9.5 %collective-permute-start.49 = (bf16[256,512]{1,0:T(8,128)(2,1)S(1)}, bf16[256,512]{1,0:T(8,128)(2,1)S(1)}, u32[]{:S(2)}, u32[]{:S(2)}) collective-permute-start(bf16[256,512]{1,0:T(8,128)(2,1)S(1)} %pad_maximum_fusion.25), channel_id=1, source_target_pairs={{0,16},{8,24},{16,0},{24,8},{1,17},{9,25},{17,1},{25,9},{2,18},{10... | collective-permute-start | bytes 786440 | tf_op jit(solution)/shard_map/ppermute | solution.py:216
  266.3 36.7 %collective-permute-start.52 = (bf16[256,1536]{1,0:T(8,128)(2,1)S(1)}, bf16[256,1536]{1,0:T(8,128)(2,1)S(1)}, u32[]{:S(2)}, u32[]{:S(2)}) collective-permute-start(bf16[256,1536]{1,0:T(8,128)(2,1)S(1)} %add_convert_fusion), channel_id=1, source_target_pairs={{0,0},{2,4},{4,2},{6,6},{1,1},{3,5},{5,3},{7,7},{8,8},{10,12},{12,... | collective-permute-start | bytes 2359304 | tf_op jit(solution)/shard_map/ppermute | solution.py:158
  269.8 8.9 %collective-permute-start.53 = (bf16[256,768]{1,0:T(8,128)(2,1)S(1)}, bf16[256,768]{1,0:T(8,128)(2,1)S(1)}, u32[]{:S(2)}, u32[]{:S(2)}) collective-permute-start(bf16[256,768]{1,0:T(8,128)(2,1)S(1)} %add_convert_fusion.3), channel_id=1, source_target_pairs={{0,0},{2,4},{4,2},{6,6},{1,1},{3,5},{5,3},{7,7},{8,8},{10,12},{12,... | collective-permute-start | bytes 1179656 | tf_op jit(solution)/shard_map/ppermute | solution.py:158
  273.0 30.0 %collective-permute-start.50 = (bf16[256,1024]{1,0:T(8,128)(2,1)S(1)}, bf16[256,1024]{1,0:T(8,128)(2,1)S(1)}, u32[]{:S(2)}, u32[]{:S(2)}) collective-permute-start(bf16[256,1024]{1,0:T(8,128)(2,1)S(1)} %pad_maximum_fusion.18), channel_id=1, source_target_pairs={{0,8},{8,0},{16,24},{24,16},{1,9},{9,1},{17,25},{25,17},{2,10},{10... | collective-permute-start | bytes 1572872 | tf_op jit(solution)/shard_map/ppermute | solution.py:216
  274.1 28.8 %collective-permute-start.51 = (bf16[256,1024]{1,0:T(8,128)(2,1)S(1)}, bf16[256,1024]{1,0:T(8,128)(2,1)S(1)}, u32[]{:S(2)}, u32[]{:S(2)}) collective-permute-start(bf16[256,1024]{1,0:T(8,128)(2,1)S(1)} %pad_maximum_fusion.19), channel_id=1, source_target_pairs={{0,16},{8,24},{16,0},{24,8},{1,17},{9,25},{17,1},{25,9},{2,18},{10... | collective-permute-start | bytes 1572872 | tf_op jit(solution)/shard_map/ppermute | solution.py:216
  275.4 24.8 %collective-permute-start.54 = (bf16[256,512]{1,0:T(8,128)(2,1)S(1)}, bf16[256,512]{1,0:T(8,128)(2,1)S(1)}, u32[]{:S(2)}, u32[]{:S(2)}) collective-permute-start(bf16[256,512]{1,0:T(8,128)(2,1)S(1)} %add_convert_fusion.6), channel_id=1, source_target_pairs={{0,0},{2,4},{4,2},{6,6},{1,1},{3,5},{5,3},{7,7},{8,8},{10,12},{12,... | collective-permute-start | bytes 786440 | tf_op jit(solution)/shard_map/ppermute | solution.py:158
  278.7 29.5 %collective-permute-start.56 = (bf16[512,1024]{1,0:T(8,128)(2,1)S(1)}, bf16[512,1024]{1,0:T(8,128)(2,1)S(1)}, u32[]{:S(2)}, u32[]{:S(2)}) collective-permute-start(bf16[512,1024]{1,0:T(8,128)(2,1)S(1)} %constant_dynamic-slice_fusion.10), channel_id=1, source_target_pairs={{0,4},{4,0},{1,5},{5,1},{2,6},{6,2},{3,7},{7,3},{8,12},{12,8},{9,1... | collective-permute-start | bytes 3145736 | tf_op jit(solution)/shard_map/ppermute | solution.py:162
  300.2 7.6 %collective-permute-start.57 = (bf16[512,1024]{1,0:T(8,128)(2,1)S(1)}, bf16[512,1024]{1,0:T(8,128)(2,1)S(1)}, u32[]{:S(2)}, u32[]{:S(2)}) collective-permute-start(bf16[512,1024]{1,0:T(8,128)(2,1)S(1)} %dynamic_slice.149), channel_id=1, source_target_pairs={{0,4},{4,0},{1,5},{5,1},{2,6},{6,2},{3,7},{7,3},{8,12},{12,8},{9,1... | collective-permute-start | bytes 3145736 | tf_op jit(solution)/shard_map/ppermute | solution.py:162
  305.3 15.1 %collective-permute-start.60 = (bf16[128,1536]{1,0:T(8,128)(2,1)S(1)}, bf16[128,1536]{1,0:T(8,128)(2,1)S(1)}, u32[]{:S(2)}, u32[]{:S(2)}) collective-permute-start(bf16[128,1536]{1,0:T(8,128)(2,1)S(1)} %constant_dynamic-slice_fusion.7), channel_id=1, source_target_pairs={{0,4},{4,0},{1,5},{5,1},{2,6},{6,2},{3,7},{7,3},{8,12},{12,8},{9,1... | collective-permute-start | bytes 1179656 | tf_op jit(solution)/shard_map/ppermute | solution.py:162
  310.3 11.3 %collective-permute-start.58 = (bf16[128,1024]{1,0:T(8,128)(2,1)S(1)}, bf16[128,1024]{1,0:T(8,128)(2,1)S(1)}, u32[]{:S(2)}, u32[]{:S(2)}) collective-permute-start(bf16[128,1024]{1,0:T(8,128)(2,1)S(1)} %constant_dynamic-slice_fusion.9), channel_id=1, source_target_pairs={{0,4},{4,0},{1,5},{5,1},{2,6},{6,2},{3,7},{7,3},{8,12},{12,8},{9,1... | collective-permute-start | bytes 786440 | tf_op jit(solution)/shard_map/ppermute | solution.py:162
  324.6 25.3 %all-to-all-start = ((bf16[8,128,768]{2,1,0:T(8,128)(2,1)}), bf16[8,128,768]{2,1,0:T(8,128)(2,1)}, u32[]{:S(2)}, u32[]{:S(2)}) async-start(bf16[8,128,768]{2,1,0:T(8,128)(2,1)} %get-tuple-element.189), calls=%async_computation | async-start | bytes 3145728 | tf_op jit(solution)/shard_map/all_to_all | solution.py:595
  330.4 14.8 %collective-permute-start.62 = (bf16[256,1024]{1,0:T(8,128)(2,1)S(1)}, bf16[256,1024]{1,0:T(8,128)(2,1)S(1)}, u32[]{:S(2)}, u32[]{:S(2)}) collective-permute-start(bf16[256,1024]{1,0:T(8,128)(2,1)S(1)} %dynamic-slice_convert_fusion), channel_id=1, source_target_pairs={{0,1},{1,0},{2,3},{3,2},{4,5},{5,4},{6,7},{7,6},{8,9},{9,8},{10,11... | collective-permute-start | bytes 1572872 | tf_op jit(solution)/shard_map/ppermute | solution.py:162
  330.5 26.0 %collective-permute-start.66 = (bf16[256,1024]{1,0:T(8,128)(2,1)S(1)}, bf16[256,1024]{1,0:T(8,128)(2,1)}, u32[]{:S(2)}, u32[]{:S(2)}) collective-permute-start(bf16[256,1024]{1,0:T(8,128)(2,1)S(1)} %dynamic_slice.203), channel_id=1, source_target_pairs={{0,1},{1,0},{2,3},{3,2},{4,5},{5,4},{6,7},{7,6},{8,9},{9,8},{10,11... | collective-permute-start | bytes 1572872 | tf_op jit(solution)/shard_map/ppermute | solution.py:162
  349.9 15.8 %collective-permute-start.63 = (bf16[1024,768]{1,0:T(8,128)(2,1)}, bf16[1024,768]{1,0:T(8,128)(2,1)}, u32[]{:S(2)}, u32[]{:S(2)}) collective-permute-start(bf16[1024,768]{1,0:T(8,128)(2,1)} %bitcast.6.refs_0_), channel_id=1, source_target_pairs={{2,1},{7,6},{10,9},{15,14},{18,17},{23,22},{31,30}} | collective-permute-start | bytes 4718600 | tf_op jit(solution)/shard_map/ppermute | solution.py:601
  351.7 14.0 %collective-permute-start.64 = (bf16[1024,768]{1,0:T(8,128)(2,1)}, bf16[1024,768]{1,0:T(8,128)(2,1)}, u32[]{:S(2)}, u32[]{:S(2)}) collective-permute-start(bf16[1024,768]{1,0:T(8,128)(2,1)} %bitcast.6.refs_0_), channel_id=1, source_target_pairs={{3,1},{4,6},{11,9},{12,14},{19,17},{20,22},{28,30}} | collective-permute-start | bytes 4718600 | tf_op jit(solution)/shard_map/ppermute | solution.py:601
  353.7 33.9 %collective-permute-start.65 = (bf16[1024,768]{1,0:T(8,128)(2,1)}, bf16[1024,768]{1,0:T(8,128)(2,1)}, u32[]{:S(2)}, u32[]{:S(2)}) collective-permute-start(bf16[1024,768]{1,0:T(8,128)(2,1)} %bitcast.6.refs_0_), channel_id=1, source_target_pairs={{0,1},{5,6},{8,9},{13,14},{16,17},{21,22},{29,30}} | collective-permute-start | bytes 4718600 | tf_op jit(solution)/shard_map/ppermute | solution.py:601
  387.5 9.2 %collective-permute-start.70 = (bf16[256,1024]{1,0:T(8,128)(2,1)S(1)}, bf16[256,1024]{1,0:T(8,128)(2,1)S(1)}, u32[]{:S(2)}, u32[]{:S(2)}) collective-permute-start(bf16[256,1024]{1,0:T(8,128)(2,1)S(1)} %fusion.12), channel_id=1, source_target_pairs={{0,0},{2,4},{4,2},{6,6},{1,1},{3,5},{5,3},{7,7},{8,8},{10,12},{12,... | collective-permute-start | bytes 1572872 | tf_op jit(solution)/shard_map/ppermute | solution.py:158
  388.2 8.5 %collective-permute-start.71 = (bf16[256,1024]{1,0:T(8,128)(2,1)S(1)}, bf16[256,1024]{1,0:T(8,128)(2,1)S(1)}, u32[]{:S(2)}, u32[]{:S(2)}) collective-permute-start(bf16[256,1024]{1,0:T(8,128)(2,1)S(1)} %add_convert_fusion.1), channel_id=1, source_target_pairs={{0,0},{2,4},{4,2},{6,6},{1,1},{3,5},{5,3},{7,7},{8,8},{10,12},{12,... | collective-permute-start | bytes 1572872 | tf_op jit(solution)/shard_map/ppermute | solution.py:158
  388.9 7.2 %collective-permute-start.72 = (f32[2304]{0:T(1024)S(1)}, f32[2304]{0:T(1024)S(1)}, u32[]{:S(2)}, u32[]{:S(2)}) collective-permute-start(f32[2304]{0:T(1024)S(1)} %add.310), channel_id=1, source_target_pairs={{0,1},{1,0},{2,3},{3,2},{4,5},{5,4},{6,7},{7,6},{8,9},{9,8},{10,11... | collective-permute-start | bytes 27656 | tf_op jit(solution)/shard_map/ppermute | solution.py:305
  396.7 104.3 %collective-permute-start.75 = (bf16[1024,768]{1,0:T(8,128)(2,1)}, bf16[1024,768]{1,0:T(8,128)(2,1)S(1)}, u32[]{:S(2)}, u32[]{:S(2)}) collective-permute-start(bf16[1024,768]{1,0:T(8,128)(2,1)} %get-tuple-element.218), channel_id=1, source_target_pairs={{1,0},{6,5},{9,8},{14,13},{17,16},{22,21},{30,29}} | collective-permute-start | bytes 4718600 | tf_op jit(solution)/shard_map/ppermute | solution.py:611
  398.0 103.0 %collective-permute-start.74 = (bf16[1024,768]{1,0:T(8,128)(2,1)S(1)}, bf16[1024,768]{1,0:T(8,128)(2,1)S(1)}, u32[]{:S(2)}, u32[]{:S(2)}) collective-permute-start(bf16[1024,768]{1,0:T(8,128)(2,1)S(1)} %get-tuple-element.217), channel_id=1, source_target_pairs={{1,3},{6,4},{9,11},{14,12},{17,19},{22,20},{30,28}} | collective-permute-start | bytes 4718600 | tf_op jit(solution)/shard_map/ppermute | solution.py:611
  398.8 102.2 %collective-permute-start.73 = (bf16[1024,768]{1,0:T(8,128)(2,1)S(1)}, bf16[1024,768]{1,0:T(8,128)(2,1)S(1)}, u32[]{:S(2)}, u32[]{:S(2)}) collective-permute-start(bf16[1024,768]{1,0:T(8,128)(2,1)S(1)} %get-tuple-element.216), channel_id=1, source_target_pairs={{1,2},{6,7},{9,10},{14,15},{17,18},{22,23},{30,31}} | collective-permute-start | bytes 4718600 | tf_op jit(solution)/shard_map/ppermute | solution.py:611
  502.4 33.6 %all-to-all-start.1 = ((bf16[8,128,768]{2,1,0:T(8,128)(2,1)}), bf16[8,128,768]{2,1,0:T(8,128)(2,1)S(1)}, u32[]{:S(2)}, u32[]{:S(2)}) async-start(bf16[8,128,768]{2,1,0:T(8,128)(2,1)} %bitcast.8), calls=%async_computation.1 | async-start | bytes 3145728 | tf_op jit(solution)/shard_map/all_to_all | solution.py:617
  (78 other events, 850.8 us)

commit v2 on v1

--- a/solution.py
+++ b/solution.py
@@ -54,7 +54,7 @@
 
 
 def orthogonalize_kernel(owner_ref, *refs):
-    count = (len(refs) - 4) // 2
+    count = (len(refs) - 4) // 3
 
     @pl.when(owner_ref[0] != 0)
     def _():
@@ -62,13 +62,13 @@
 
     @pl.when(owner_ref[0] == 0)
     def _():
-        for result in refs[count : 2 * count]:
+        for result in refs[count : 3 * count]:
             result[...] = jnp.zeros_like(result)
 
 
 def orthogonalize_owned(count, refs):
-    pieces, results = refs[:count], refs[count : 2 * count]
-    current, gram, gram_low, mixing = refs[2 * count :]
+    pieces, results = refs[:count], refs[count : 3 * count]
+    current, gram, gram_low, mixing = refs[3 * count :]
     size, width = pieces[0].shape
     block = 256
     blocks = size // block
@@ -124,19 +124,28 @@
 
     lax.fori_loop(0, NS_STEPS, sweep, 0)
     for number, result in enumerate(results):
-        result[...] = current[:, number * width : (number + 1) * width]
+        at = number % count * width
+        if number < count:
+            result[...] = current[:, at : at + result.shape[1]]
+        else:
+            result[...] = current[:, at + width - result.shape[1] : at + width]
 
 
 def orthogonalize(owner, pieces):
     size, width = pieces[0].shape
+    first = (width // 2 + 127) // 128 * 128
     total = width * len(pieces)
     flops = NS_STEPS * 2 * size * size * (total * 13 // 8 + size * 5 // 8)
     return pl.pallas_call(
         orthogonalize_kernel,
-        out_shape=[jax.ShapeDtypeStruct(piece.shape, piece.dtype) for piece in pieces],
+        out_shape=[
+            jax.ShapeDtypeStruct((size, part), piece.dtype)
+            for part in (first, width - first)
+            for piece in pieces
+        ],
         in_specs=[pl.BlockSpec(memory_space=pltpu.SMEM)]
         + [pl.BlockSpec(memory_space=pltpu.VMEM)] * len(pieces),
-        out_specs=[pl.BlockSpec(memory_space=pltpu.VMEM)] * len(pieces),
+        out_specs=[pl.BlockSpec(memory_space=pltpu.VMEM)] * (2 * len(pieces)),
         scratch_shapes=[
             pltpu.VMEM((size, total), jnp.bfloat16),
             pltpu.VMEM((size, size), jnp.float32),
@@ -683,11 +692,17 @@
     return results[:7], results[7:14], results[14]
 
 
-def update_kernel(homes, returned_ref, *refs):
+def update_kernel(homes, *refs):
+    returned_refs, refs = refs[:2], refs[2:]
+    first = returned_refs[0].shape[2]
     for number in range(7):
         master_ref, result_ref = refs[number], refs[7 + number]
         width = master_ref.shape[0] if FLIPPED[number] else master_ref.shape[1]
-        portion = returned_ref[homes[number], :, :width].astype(jnp.float32)
+        portion = returned_refs[0][homes[number], :, : min(width, first)]
+        if width > first:
+            rest = returned_refs[1][homes[number], :, : width - first]
+            portion = jnp.concatenate([portion, rest], axis=1)
+        portion = portion.astype(jnp.float32)
         if FLIPPED[number]:
             portion = portion.T
         step_size = 0.5 * FANS[number] ** (-0.5) * math.sqrt(max(SHAPES[number]))
@@ -697,7 +712,7 @@
 def update(returned, masters, homes):
     return in_vmem(
         functools.partial(update_kernel, homes),
-        [returned] + list(masters),
+        list(returned) + list(masters),
         [jax.ShapeDtypeStruct(master.shape, jnp.float32) for master in masters],
         [],
         0,
@@ -786,7 +801,6 @@
     gate_value = gate_up[:, :width_ff]
     up_value = gate_up[:, width_ff:]
     activated = (jax.nn.silu(gate_value) * up_value).astype(jnp.bfloat16)
-    block_part = contract_cols(activated, down_full).astype(bf16)
     down_grad = contract_rows(cot_rows, activated).astype(bf16)
     cot_rows, down_grad = tied(cot_rows, down_grad)
     down_pieces = sum_plane(down_grad)
@@ -807,20 +821,22 @@
     d_residual_norm, d_gain_mlp = norm_pull(d_normed_mlp)
     d_residual = out_grad.astype(jnp.float32) + d_residual_norm
     state_pair = gather_near(d_residual.astype(bf16), True)
+    state_pair, down_pieces = tied(state_pair, down_pieces)
     state_rows = gather_across(state_pair, True)
+    down_held = cross_sum(down_pieces)
     out_chunks = sum_far(contract_rows(state_rows, mixed_heads).astype(bf16))
     d_heads, d_gain_heads = attention_backward(
         state_rows, out_full, saved, cosine_part, sine_part, gain_query, gain_key, start
     )
-    d_heads, gate_up_pieces, down_pieces, block_part, out_chunks = tied(
-        d_heads, gate_up_pieces, down_pieces, block_part, out_chunks
-    )
+    d_heads, gate_up_pieces, down_held, activated, out_chunks = tied(
+        d_heads, gate_up_pieces, down_held, activated, out_chunks
+    )
+    block_part = contract_cols(activated, down_full).astype(bf16)
     gate_up_held = cross_sum(gate_up_pieces)
-    down_held = cross_sum(down_pieces)
     out_pieces = sum_near(out_chunks)
     heads_grad = contract_rows(attn_rows, d_heads)
     late_chunks = sum_far(heads_grad.astype(bf16))
-    late_chunks, out_pieces = tied(late_chunks, out_pieces)
+    late_chunks, out_pieces, d_heads = tied(late_chunks, out_pieces, d_heads)
     late_pieces = sum_near(late_chunks)
     out_held = cross_sum(out_pieces)
     late_pieces, gate_up_held, down_held, out_held = tied(
@@ -869,14 +885,15 @@
     gain_grad = sum_everywhere(gain_grad, [(name, lax.axis_size(name)) for name in ("core", "pl")])
     pieces, input_grad, block_out, gain_grad = tied(pieces, input_grad, block_out, gain_grad)
     back = orthogonalize(owns(group, homes), pieces)
-    input_grad = swap(input_grad)
-    block_out = swap(block_out)
     gain_grad = sum_everywhere(gain_grad, [("lo", lax.axis_size("lo"))])
     back, input_grad, block_out, gain_grad = tied(back, input_grad, block_out, gain_grad)
-    input_grad = input_grad.astype(jnp.float32)
-    block_out = block_out.astype(jnp.float32)
+    half = len(back) // 2
+    received = [from_homes(group, homes, part) for part in (back[:half], back[half:])]
+    input_grad = swap(input_grad).astype(jnp.float32)
+    block_out = swap(block_out).astype(jnp.float32)
+    received[1], gain_grad = tied(received[1], gain_grad)
     gain_grad = sum_everywhere(gain_grad, [("hi", 2)])
-    updated = update(from_columns(from_homes(group, homes, back)), masters, homes)
+    updated = update([from_columns(part) for part in received], masters, homes)
     first_next = BETA_FIRST * gain_first + (1.0 - BETA_FIRST) * gain_grad
     second_next = BETA_SECOND * gain_second + (1.0 - BETA_SECOND) * gain_grad * gain_grad
     first_hat = first_next / (1.0 - BETA_FIRST**ADAM_STEP)

time: 544 us -> 541 us (level)
  waiting for transfers between devices: 255 us -> 219 us
  starting transfers between devices: 146 us -> 174 us
    ppermute x3 -> x6, waiting for transfers between devices: 101 us -> 81.6 us  [from_homes(): received = received + lax.ppermute(back[step], DP + TENSOR, pairs)]
    all_to_all x1 -> x2, waiting for transfers between devices: 15.4 us -> 0.01 us  [from_columns(): lax.all_to_all(received.reshape(shape), DP, split_axis=0, concat_axis=0,...]
    ppermute x12, starting transfers between devices: 10.5 us -> 19.8 us  [swap(): lax.ppermute(values, ('core', 'hi'), [(0, 0), (1, 2), (2, 1), (3, 3)])]
    all_to_all x1 -> x2, starting transfers between devices: 12.5 us -> 21.1 us  [from_columns(): lax.all_to_all(received.reshape(shape), DP, split_axis=0, concat_axis=0,...]
    ppermute x5, starting transfers between devices: 4.9 us -> 12.1 us  [sum_everywhere(): values = values + lax.ppermute(values, name, pairs)]
    unnamed x131 -> x124, local copies, waits for them, and re-layouts: 11.4 us -> 8.79 us
  transfers between devices with their start and end apart: 79 -> 83, of which waited for: 30 -> 26; matrix products, arithmetic and copies ran while one was open for 10% -> 11% of each run, Pallas kernels for 8% -> 8%
where the time goes in v2:
time: 541 us; the launch traced here: 531 us
  waiting for transfers between devices  219 us (40%)
  starting transfers between devices  174 us (32%)
  Pallas kernels  45.4 us (8%)
  other arithmetic  37.2 us (7%)
  matrix products  30.5 us (6%)
  local copies, waits for them, and re-layouts  22.2 us (4%)
    ppermute x6, waiting for transfers between devices, from_homes(): received = received + lax.ppermute(back[step], DP + TENSOR, pairs)  81.6 us
    ppermute x23, waiting for transfers between devices, to_partner(): return lax.ppermute(values, name, [(0, 1), (1, 0)])  72.4 us
    ppermute x23, starting transfers between devices, to_partner(): return lax.ppermute(values, name, [(0, 1), (1, 0)])  67.5 us
    pallas_call x5, Pallas kernels, in_vmem(): pl.pallas_call(kernel, out_shape=results, in_specs=[pl.BlockSpec(memory_s...  41.1 us
    ppermute x31, waiting for transfers between devices, exchange(): lax.ppermute(values, 'pl', [(index, index ^ stride) for index in range(co...  35.5 us
    ppermute x31, starting transfers between devices, exchange(): lax.ppermute(values, 'pl', [(index, index ^ stride) for index in range(co...  35.3 us
    all_to_all x2, starting transfers between devices, from_columns(): lax.all_to_all(received.reshape(shape), DP, split_axis=0, concat_axis=0,...  21.1 us
    ppermute x12, starting transfers between devices, swap(): lax.ppermute(values, ('core', 'hi'), [(0, 0), (1, 2), (2, 1), (3, 3)])  19.8 us
  transfers between devices with their start and end apart: 83, of which 26 were waited for; matrix products, arithmetic and copies ran while one was open for 11% of the time, Pallas kernels for 8%

profile of v2, /device:TPU:0, one launch (start us, length us, event | category | flops | bytes accessed | tf_op | source)
XLA Modules:
  0.0 530.8 jit_solution(8207374684003062587)
XLA Ops:
  8.3 4.7 collective-permute-start.7
  16.1 1.7 collective-permute-start.2
  17.9 4.6 collective-permute-done.4
  24.4 1.6 collective-permute-start.6
  28.1 6.5 %collective-permute-done.6 = bf16[256,1024]{1,0:T(8,128)(2,1)S(1)} collective-permute-done((bf16[256,1024]{1,0:T(8,128)(2,1)S(1)}, bf16[256,1024]{1,0:T(8,128)(2,1)S(1)}, u32[]{:S(2)}, u32[]{:S(2)}) %collective-permute-start.6) | collective-permute-done | bytes 524320 | tf_op jit(solution)/shard_map/ppermute | solution.py:171
  35.1 19.1 %collective-permute-start.8 = (bf16[512,1024]{1,0:T(8,128)(2,1)S(1)}, bf16[512,1024]{1,0:T(8,128)(2,1)S(1)}, u32[]{:S(2)}, u32[]{:S(2)}) collective-permute-start(bf16[512,1024]{1,0:T(8,128)(2,1)S(1)} %pad_maximum_fusion.8), channel_id=1, source_target_pairs={{0,4},{4,0},{1,5},{5,1},{2,6},{6,2},{3,7},{7,3},{8,12},{12,8},{9,1... | collective-permute-start | bytes 3145736 | tf_op jit(solution)/shard_map/ppermute | solution.py:171
  54.2 1.9 fusion.15
  60.8 4.0 collective-permute-done.9
  67.9 6.9 %shard_map.395 = (bf16[1024,512]{1,0:T(8,128)(2,1)S(1)}, bf16[1024,256]{1,0:T(8,128)(2,1)S(1)}, bf16[1024,256]{1,0:T(8,128)(2,1)S(1)}, f32[1024,768]{1,0:T(8,128)}) custom-call(bf16[1024,1024]{1,0:T(8,128)(2,1)S(1)} %pad_maximum_fusion.1.rows_ref, bf16[1024,1024]{1,0:T(8,128)(2,1)} %copy-done.37, f32[1024,128]{1,0:T(8,128)S(1)} %get-tuple-element.316.cosine_ref, ...), custom_call_target="tpu_custom_call" | custom-call | flops 2147483648 | bytes 10486784 | tf_op jit(solution)/shard_map/pallas_call | solution.py:512
  78.3 9.9 %shard_map.396 = (bf16[1024,512]{1,0:T(8,128)(2,1)S(1)}, f32[4,1024]{1,0:T(4,128)S(1)}) custom-call(bf16[1024,512]{1,0:T(8,128)(2,1)S(1)} %get-tuple-element.153.query_ref, bf16[1024,256]{1,0:T(8,128)(2,1)S(1)} %get-tuple-element.154.key_ref, bf16[1024,256]{1,0:T(8,128)(2,1)S(1)} %get-tuple-element.155.value_ref, s32[1,1024]{1,0:T(1,128)S(1)} %bitcast.32), custom_call_target="tpu_custom_call" | custom-call | flops 2147483648 | bytes 3166208 | tf_op jit(solution)/shard_map/pallas_call | solution.py:512
  88.4 2.0 collective-permute-done.15
  93.3 4.2 collective-permute-start.17
  97.6 2.6 collective-permute-done.17
  100.2 3.3 convert_add_fusion.3
  103.5 2.1 dynamic-slice_convert_fusion.1
  108.3 1.6 collective-permute-start.23
  111.3 8.8 %collective-permute-done.18 = bf16[256,1024]{1,0:T(8,128)(2,1)} collective-permute-done((bf16[256,1024]{1,0:T(8,128)(2,1)}, bf16[256,1024]{1,0:T(8,128)(2,1)}, u32[]{:S(2)}, u32[]{:S(2)}) %collective-permute-start.18) | collective-permute-done | bytes 524320 | tf_op jit(solution)/shard_map/ppermute | solution.py:171
  120.1 1.6 convert_add_fusion.4
  124.2 17.7 %collective-permute-done.22 = bf16[256,1024]{1,0:T(8,128)(2,1)S(1)} collective-permute-done((bf16[256,1024]{1,0:T(8,128)(2,1)S(1)}, bf16[256,1024]{1,0:T(8,128)(2,1)S(1)}, u32[]{:S(2)}, u32[]{:S(2)}) %collective-permute-start.22) | collective-permute-done | bytes 524320 | tf_op jit(solution)/shard_map/ppermute | solution.py:171
  147.4 8.2 %collective-permute-done.29 = bf16[256,768]{0,1:T(8,128)(2,1)S(1)} collective-permute-done((bf16[256,768]{0,1:T(8,128)(2,1)S(1)}, bf16[256,768]{0,1:T(8,128)(2,1)S(1)}, u32[]{:S(2)}, u32[]{:S(2)}) %collective-permute-start.29) | collective-permute-done | bytes 393248 | tf_op jit(solution)/shard_map/ppermute | solution.py:225
  156.4 5.9 %collective-permute-done.26 = bf16[128,1536]{0,1:T(8,128)(2,1)S(1)} collective-permute-done((bf16[128,1536]{0,1:T(8,128)(2,1)S(1)}, bf16[128,1536]{0,1:T(8,128)(2,1)S(1)}, u32[]{:S(2)}, u32[]{:S(2)}) %collective-permute-start.26) | collective-permute-done | bytes 393248 | tf_op jit(solution)/shard_map/ppermute | solution.py:225
  165.1 2.9 collective-permute-done.31
  168.1 3.5 fusion.26
  173.7 3.1 convolution_convert_fusion.5
  176.8 3.5 fusion.2
  180.3 3.6 fusion.5
  187.6 1.6 collective-permute-start.37
  190.7 6.0 %convolution_convert_fusion = bf16[1024,1536]{1,0:T(8,128)(2,1)S(1)} fusion(bf16[1024,1024]{1,0:T(8,128)(2,1)} %copy-done.47, bf16[1024,768]{1,0:T(8,128)(2,1)} %copy-done.57, bf16[1024,768]{1,0:T(8,128)(2,1)} %copy-done.56), kind=kOutput, calls=%fused_computation.1 | convolution fusion | flops 3229089792 | bytes 8388608 | tf_op jit(solution)/shard_map/dot_general | solution.py:45
  196.7 1.6 convert_add_fusion.2
  198.7 13.6 %collective-permute-done.33 = bf16[256,1024]{1,0:T(8,128)(2,1)S(1)} collective-permute-done((bf16[256,1024]{1,0:T(8,128)(2,1)S(1)}, bf16[256,1024]{1,0:T(8,128)(2,1)S(1)}, u32[]{:S(2)}, u32[]{:S(2)}) %collective-permute-start.33) | collective-permute-done | bytes 524320 | tf_op jit(solution)/shard_map/ppermute | solution.py:171
  218.8 8.2 %collective-permute-done.34 = bf16[256,1024]{1,0:T(8,128)(2,1)S(1)} collective-permute-done((bf16[256,1024]{1,0:T(8,128)(2,1)S(1)}, bf16[256,1024]{1,0:T(8,128)(2,1)S(1)}, u32[]{:S(2)}, u32[]{:S(2)}) %collective-permute-start.34) | collective-permute-done | bytes 524320 | tf_op jit(solution)/shard_map/ppermute | solution.py:171
  227.1 5.9 %collective-permute-done.36 = bf16[256,768]{1,0:T(8,128)(2,1)S(1)} collective-permute-done((bf16[256,768]{1,0:T(8,128)(2,1)S(1)}, bf16[256,768]{1,0:T(8,128)(2,1)S(1)}, u32[]{:S(2)}, u32[]{:S(2)}) %collective-permute-start.36) | collective-permute-done | bytes 393248 | tf_op jit(solution)/shard_map/ppermute | solution.py:225
  241.7 20.1 %shard_map.397 = (bf16[1024,1024]{1,0:T(8,128)(2,1)}, f32[2,128]{1,0:T(2,128)S(1)}) custom-call(bf16[1024,1024]{1,0:T(8,128)(2,1)} %pad_maximum_fusion.2.state_ref, bf16[1024,512]{1,0:T(8,128)(2,1)S(1)} %constant_dynamic-update-slice_fusion.10.out_ref, bf16[1024,512]{1,0:T(8,128)(2,1)S(1)} %get-tuple-element.153.query_ref, bf16[1024,256]{1,0:T(8,128)(2,1)S(1)} %copy-done.17, ...), custom_call_target="tpu_custom_call" | custom-call | flops 6442450944 | bytes 11556864 | tf_op jit(solution)/shard_map/pallas_call | solution.py:512
  262.0 4.1 convolution_convert_fusion.2
  271.6 1.8 convolution_convert_fusion.4
  273.6 6.0 %collective-permute-start.57 = (bf16[512,1024]{1,0:T(8,128)(2,1)S(1)}, bf16[512,1024]{1,0:T(8,128)(2,1)S(1)}, u32[]{:S(2)}, u32[]{:S(2)}) collective-permute-start(bf16[512,1024]{1,0:T(8,128)(2,1)S(1)} %dynamic_slice.167), channel_id=1, source_target_pairs={{0,4},{4,0},{1,5},{5,1},{2,6},{6,2},{3,7},{7,3},{8,12},{12,8},{9,1... | collective-permute-start | bytes 3145736 | tf_op jit(solution)/shard_map/ppermute | solution.py:171
  283.0 2.4 convolution_convert_fusion.1
  285.6 16.6 %collective-permute-start.56 = (bf16[512,1024]{1,0:T(8,128)(2,1)S(1)}, bf16[512,1024]{1,0:T(8,128)(2,1)S(1)}, u32[]{:S(2)}, u32[]{:S(2)}) collective-permute-start(bf16[512,1024]{1,0:T(8,128)(2,1)S(1)} %constant_dynamic-slice_fusion.10), channel_id=1, source_target_pairs={{0,4},{4,0},{1,5},{5,1},{2,6},{6,2},{3,7},{7,3},{8,12},{12,8},{9,1... | collective-permute-start | bytes 3145736 | tf_op jit(solution)/shard_map/ppermute | solution.py:171
  307.0 1.7 convert_add_fusion
  309.2 9.5 %collective-permute-start.58 = (bf16[128,1024]{1,0:T(8,128)(2,1)S(1)}, bf16[128,1024]{1,0:T(8,128)(2,1)S(1)}, u32[]{:S(2)}, u32[]{:S(2)}) collective-permute-start(bf16[128,1024]{1,0:T(8,128)(2,1)S(1)} %constant_dynamic-slice_fusion.9), channel_id=1, source_target_pairs={{0,4},{4,0},{1,5},{5,1},{2,6},{6,2},{3,7},{7,3},{8,12},{12,8},{9,1... | collective-permute-start | bytes 786440 | tf_op jit(solution)/shard_map/ppermute | solution.py:171
  320.0 2.9 shard_map.398
  322.8 4.3 all-to-all-start
  328.7 2.0 collective-permute-start.66
  330.7 11.3 %collective-permute-done.62 = bf16[256,1024]{1,0:T(8,128)(2,1)S(1)} collective-permute-done((bf16[256,1024]{1,0:T(8,128)(2,1)S(1)}, bf16[256,1024]{1,0:T(8,128)(2,1)S(1)}, u32[]{:S(2)}, u32[]{:S(2)}) %collective-permute-start.62) | collective-permute-done | bytes 524320 | tf_op jit(solution)/shard_map/ppermute | solution.py:171
  343.4 4.7 all-to-all-done
  348.2 1.8 collective-permute-start.63
  350.0 1.9 collective-permute-start.64
  351.9 2.7 collective-permute-start.65
  355.1 2.4 add_convert_fusion.1
  358.2 3.1 collective-permute-done.68
  363.0 2.0 collective-permute-done.69
  365.1 19.3 %collective-permute-done.65.refs_3_ = bf16[1024,768]{1,0:T(8,128)(2,1)} collective-permute-done((bf16[1024,768]{1,0:T(8,128)(2,1)}, bf16[1024,768]{1,0:T(8,128)(2,1)}, u32[]{:S(2)}, u32[]{:S(2)}) %collective-permute-start.65) | collective-permute-done | bytes 1572896 | tf_op jit(solution)/shard_map/ppermute | solution.py:610
  384.4 3.1 collective-permute-start.70
  387.5 4.3 shard_map.399
  397.3 81.6 %collective-permute-done.75 = bf16[1024,384]{1,0:T(8,128)(2,1)S(1)} collective-permute-done((bf16[1024,384]{1,0:T(8,128)(2,1)S(1)}, bf16[1024,384]{1,0:T(8,128)(2,1)S(1)}, u32[]{:S(2)}, u32[]{:S(2)}) %collective-permute-start.75) | collective-permute-done | bytes 786464 | tf_op jit(solution)/shard_map/ppermute | solution.py:620
  478.9 1.6 collective-permute-start.76
  481.5 3.5 all-to-all-start.1
  485.0 5.4 %collective-permute-start.71 = (bf16[256,1024]{1,0:T(8,128)(2,1)}, bf16[256,1024]{1,0:T(8,128)(2,1)}, u32[]{:S(2)}, u32[]{:S(2)}) collective-permute-start(bf16[256,1024]{1,0:T(8,128)(2,1)} %add_convert_fusion.1), channel_id=1, source_target_pairs={{0,0},{2,4},{4,2},{6,6},{1,1},{3,5},{5,3},{7,7},{8,8},{10,12},{12,... | collective-permute-start | bytes 1572872 | tf_op jit(solution)/shard_map/ppermute | solution.py:167
  490.4 5.4 %collective-permute-start.72 = (bf16[256,1024]{1,0:T(8,128)(2,1)}, bf16[256,1024]{1,0:T(8,128)(2,1)}, u32[]{:S(2)}, u32[]{:S(2)}) collective-permute-start(bf16[256,1024]{1,0:T(8,128)(2,1)} %fusion.12), channel_id=1, source_target_pairs={{0,0},{2,4},{4,2},{6,6},{1,1},{3,5},{5,3},{7,7},{8,8},{10,12},{12,... | collective-permute-start | bytes 1572872 | tf_op jit(solution)/shard_map/ppermute | solution.py:167
  495.8 2.7 add_add_fusion.2
  498.5 17.6 %all-to-all-start.2 = ((bf16[8,128,384]{2,1,0:T(8,128)(2,1)}), bf16[8,128,384]{2,1,0:T(8,128)(2,1)S(1)}, u32[]{:S(2)}, u32[]{:S(2)}) async-start(bf16[8,128,384]{2,1,0:T(8,128)(2,1)} %bitcast.36), calls=%async_computation.2 | async-start | bytes 1572864 | tf_op jit(solution)/shard_map/all_to_all | solution.py:626
  516.2 7.8 %collective-permute-start.79 = (f32[2304]{0:T(1024)S(1)}, f32[2304]{0:T(1024)S(1)}, u32[]{:S(2)}, u32[]{:S(2)}) collective-permute-start(f32[2304]{0:T(1024)S(1)} %add.324), channel_id=1, source_target_pairs={{0,2},{2,0},{1,3},{3,1},{4,6},{6,4},{5,7},{7,5},{8,10},{10,8},{9,1... | collective-permute-start | bytes 27656 | tf_op jit(solution)/shard_map/ppermute | solution.py:314
  524.0 2.1 convert_element_type.361
  526.1 2.1 convert_element_type.362
  (379 shorter events, 97.7 us)
Async XLA Ops:
  5.2 12.6 %collective-permute-start.3 = (bf16[128,512]{1,0:T(8,128)(2,1)S(1)}, bf16[128,512]{1,0:T(8,128)(2,1)S(1)}, u32[]{:S(2)}, u32[]{:S(2)}) collective-permute-start(bf16[128,512]{1,0:T(8,128)(2,1)S(1)} %bitcast.38), channel_id=1, source_target_pairs={{0,4},{4,0},{1,5},{5,1},{2,6},{6,2},{3,7},{7,3},{8,12},{12,8},{9,1... | collective-permute-start | bytes 393224 | tf_op jit(solution)/shard_map/ppermute | solution.py:171
  8.3 17.7 %collective-permute-start.7 = (bf16[128,2304]{0,1:T(8,128)(2,1)S(1)}, bf16[128,2304]{0,1:T(8,128)(2,1)}, u32[]{:S(2)}, u32[]{:S(2)}) collective-permute-start(bf16[128,2304]{0,1:T(8,128)(2,1)S(1)} %pad_maximum_fusion.14), channel_id=1, source_target_pairs={{0,4},{4,0},{1,5},{5,1},{2,6},{6,2},{3,7},{7,3},{8,12},{12,8},{9,1... | collective-permute-start | bytes 1769480 | tf_op jit(solution)/shard_map/ppermute | solution.py:171
  13.0 9.5 %collective-permute-start.4 = (bf16[256,1024]{1,0:T(8,128)(2,1)}, bf16[256,1024]{1,0:T(8,128)(2,1)S(1)}, u32[]{:S(2)}, u32[]{:S(2)}) collective-permute-start(bf16[256,1024]{1,0:T(8,128)(2,1)} %collective-permute-done.1), channel_id=1, source_target_pairs={{0,8},{8,0},{16,24},{24,16},{1,9},{9,1},{17,25},{25,17},{2,10},{10... | collective-permute-start | bytes 1572872 | tf_op jit(solution)/shard_map/ppermute | solution.py:225
  14.6 9.4 %collective-permute-start.5 = (bf16[256,1024]{1,0:T(8,128)(2,1)}, bf16[256,1024]{1,0:T(8,128)(2,1)S(1)}, u32[]{:S(2)}, u32[]{:S(2)}) collective-permute-start(bf16[256,1024]{1,0:T(8,128)(2,1)} %collective-permute-done.1), channel_id=1, source_target_pairs={{0,16},{8,24},{16,0},{24,8},{1,17},{9,25},{17,1},{25,9},{2,18},{10... | collective-permute-start | bytes 1572872 | tf_op jit(solution)/shard_map/ppermute | solution.py:225
  24.4 10.3 %collective-permute-start.6 = (bf16[256,1024]{1,0:T(8,128)(2,1)S(1)}, bf16[256,1024]{1,0:T(8,128)(2,1)S(1)}, u32[]{:S(2)}, u32[]{:S(2)}) collective-permute-start(bf16[256,1024]{1,0:T(8,128)(2,1)S(1)} %fusion.8), channel_id=1, source_target_pairs={{0,1},{1,0},{2,3},{3,2},{4,5},{5,4},{6,7},{7,6},{8,9},{9,8},{10,11... | collective-permute-start | bytes 1572872 | tf_op jit(solution)/shard_map/ppermute | solution.py:171
  27.5 26.7 %collective-permute-start.11 = (s32[1024]{0:T(1024)S(1)}, s32[1024]{0:T(1024)S(1)}, u32[]{:S(2)}, u32[]{:S(2)}) collective-permute-start(s32[1024]{0:T(1024)S(1)} %copy-done.55), channel_id=1, source_target_pairs={{0,0},{2,4},{4,2},{6,6},{1,1},{3,5},{5,3},{7,7},{8,8},{10,12},{12,... | collective-permute-start | bytes 12296 | tf_op jit(solution)/shard_map/ppermute | solution.py:167
  35.1 30.1 %collective-permute-start.8 = (bf16[512,1024]{1,0:T(8,128)(2,1)S(1)}, bf16[512,1024]{1,0:T(8,128)(2,1)S(1)}, u32[]{:S(2)}, u32[]{:S(2)}) collective-permute-start(bf16[512,1024]{1,0:T(8,128)(2,1)S(1)} %pad_maximum_fusion.8), channel_id=1, source_target_pairs={{0,4},{4,0},{1,5},{5,1},{2,6},{6,2},{3,7},{7,3},{8,12},{12,8},{9,1... | collective-permute-start | bytes 3145736 | tf_op jit(solution)/shard_map/ppermute | solution.py:171
  57.7 17.0 %collective-permute-start.12 = (bf16[256,512]{1,0:T(8,128)(2,1)S(1)}, bf16[256,512]{1,0:T(8,128)(2,1)S(1)}, u32[]{:S(2)}, u32[]{:S(2)}) collective-permute-start(bf16[256,512]{1,0:T(8,128)(2,1)S(1)} %pad_maximum_fusion.23), channel_id=1, source_target_pairs={{0,0},{2,4},{4,2},{6,6},{1,1},{3,5},{5,3},{7,7},{8,8},{10,12},{12,... | collective-permute-start | bytes 786440 | tf_op jit(solution)/shard_map/ppermute | solution.py:167
  59.8 28.5 %collective-permute-start.13 = (bf16[256,2304]{0,1:T(8,128)(2,1)S(1)}, bf16[256,2304]{0,1:T(8,128)(2,1)S(1)}, u32[]{:S(2)}, u32[]{:S(2)}) collective-permute-start(bf16[256,2304]{0,1:T(8,128)(2,1)S(1)} %pad_maximum_fusion.7), channel_id=1, source_target_pairs={{0,0},{2,4},{4,2},{6,6},{1,1},{3,5},{5,3},{7,7},{8,8},{10,12},{12,... | collective-permute-start | bytes 3538952 | tf_op jit(solution)/shard_map/ppermute | solution.py:167
  74.7 13.6 %collective-permute-start.14 = (bf16[256,512]{1,0:T(8,128)(2,1)S(1)}, bf16[256,512]{1,0:T(8,128)(2,1)S(1)}, u32[]{:S(2)}, u32[]{:S(2)}) collective-permute-start(bf16[256,512]{1,0:T(8,128)(2,1)S(1)} %collective-permute-done.12), channel_id=1, source_target_pairs={{0,8},{8,0},{16,24},{24,16},{1,9},{9,1},{17,25},{25,17},{2,10},{10... | collective-permute-start | bytes 786440 | tf_op jit(solution)/shard_map/ppermute | solution.py:225
  76.3 14.0 %collective-permute-start.15 = (bf16[256,512]{1,0:T(8,128)(2,1)S(1)}, bf16[256,512]{1,0:T(8,128)(2,1)S(1)}, u32[]{:S(2)}, u32[]{:S(2)}) collective-permute-start(bf16[256,512]{1,0:T(8,128)(2,1)S(1)} %collective-permute-done.12), channel_id=1, source_target_pairs={{0,16},{8,24},{16,0},{24,8},{1,17},{9,25},{17,1},{25,9},{2,18},{10... | collective-permute-start | bytes 786440 | tf_op jit(solution)/shard_map/ppermute | solution.py:225
  76.8 13.5 %collective-permute-start.16 = (bf16[256,512]{1,0:T(8,128)(2,1)S(1)}, bf16[256,512]{1,0:T(8,128)(2,1)S(1)}, u32[]{:S(2)}, u32[]{:S(2)}) collective-permute-start(bf16[256,512]{1,0:T(8,128)(2,1)S(1)} %collective-permute-done.12), channel_id=1, source_target_pairs={{0,24},{8,16},{16,8},{24,0},{1,25},{9,17},{17,9},{25,1},{2,26},{10... | collective-permute-start | bytes 786440 | tf_op jit(solution)/shard_map/ppermute | solution.py:225
  105.6 14.5 %collective-permute-start.18 = (bf16[256,1024]{1,0:T(8,128)(2,1)}, bf16[256,1024]{1,0:T(8,128)(2,1)}, u32[]{:S(2)}, u32[]{:S(2)}) collective-permute-start(bf16[256,1024]{1,0:T(8,128)(2,1)} %dynamic-slice_convert_fusion.1), channel_id=1, source_target_pairs={{0,1},{1,0},{2,3},{3,2},{4,5},{5,4},{6,7},{7,6},{8,9},{9,8},{10,11... | collective-permute-start | bytes 1572872 | tf_op jit(solution)/shard_map/ppermute | solution.py:171
  108.3 33.7 %collective-permute-start.23 = (bf16[256,1536]{0,1:T(8,128)(2,1)S(1)}, bf16[256,1536]{0,1:T(8,128)(2,1)S(1)}, u32[]{:S(2)}, u32[]{:S(2)}) collective-permute-start(bf16[256,1536]{0,1:T(8,128)(2,1)S(1)} %slice.121), channel_id=1, source_target_pairs={{0,8},{8,0},{16,24},{24,16},{1,9},{9,1},{17,25},{25,17},{2,10},{10... | collective-permute-start | bytes 2359304 | tf_op jit(solution)/shard_map/ppermute | solution.py:225
  109.8 32.2 %collective-permute-start.24 = (bf16[256,1536]{0,1:T(8,128)(2,1)S(1)}, bf16[256,1536]{0,1:T(8,128)(2,1)S(1)}, u32[]{:S(2)}, u32[]{:S(2)}) collective-permute-start(bf16[256,1536]{0,1:T(8,128)(2,1)S(1)} %slice.121), channel_id=1, source_target_pairs={{0,16},{8,24},{16,0},{24,8},{1,17},{9,25},{17,1},{25,9},{2,18},{10... | collective-permute-start | bytes 2359304 | tf_op jit(solution)/shard_map/ppermute | solution.py:225
  122.9 19.1 %collective-permute-start.22 = (bf16[256,1024]{1,0:T(8,128)(2,1)S(1)}, bf16[256,1024]{1,0:T(8,128)(2,1)S(1)}, u32[]{:S(2)}, u32[]{:S(2)}) collective-permute-start(bf16[256,1024]{1,0:T(8,128)(2,1)S(1)} %multiply_convert_fusion.2), channel_id=1, source_target_pairs={{0,1},{1,0},{2,3},{3,2},{4,5},{5,4},{6,7},{7,6},{8,9},{9,8},{10,11... | collective-permute-start | bytes 1572872 | tf_op jit(solution)/shard_map/ppermute | solution.py:171
  123.3 23.7 %collective-permute-start.19 = (bf16[256,1024]{1,0:T(8,128)(2,1)S(1)}, bf16[256,1024]{1,0:T(8,128)(2,1)S(1)}, u32[]{:S(2)}, u32[]{:S(2)}) collective-permute-start(bf16[256,1024]{1,0:T(8,128)(2,1)S(1)} %copy-done.54), channel_id=1, source_target_pairs={{0,0},{2,4},{4,2},{6,6},{1,1},{3,5},{5,3},{7,7},{8,8},{10,12},{12,... | collective-permute-start | bytes 1572872 | tf_op jit(solution)/shard_map/ppermute | solution.py:167
  142.0 13.6 %collective-permute-start.28 = (bf16[256,768]{0,1:T(8,128)(2,1)S(1)}, bf16[256,768]{0,1:T(8,128)(2,1)S(1)}, u32[]{:S(2)}, u32[]{:S(2)}) collective-permute-start(bf16[256,768]{0,1:T(8,128)(2,1)S(1)} %slice.119), channel_id=1, source_target_pairs={{0,8},{8,0},{16,24},{24,16},{1,9},{9,1},{17,25},{25,17},{2,10},{10... | collective-permute-start | bytes 1179656 | tf_op jit(solution)/shard_map/ppermute | solution.py:225
  143.6 12.1 %collective-permute-start.29 = (bf16[256,768]{0,1:T(8,128)(2,1)S(1)}, bf16[256,768]{0,1:T(8,128)(2,1)S(1)}, u32[]{:S(2)}, u32[]{:S(2)}) collective-permute-start(bf16[256,768]{0,1:T(8,128)(2,1)S(1)} %slice.119), channel_id=1, source_target_pairs={{0,16},{8,24},{16,0},{24,8},{1,17},{9,25},{17,1},{25,9},{2,18},{10... | collective-permute-start | bytes 1179656 | tf_op jit(solution)/shard_map/ppermute | solution.py:225
  145.9 16.4 %collective-permute-start.26 = (bf16[128,1536]{0,1:T(8,128)(2,1)S(1)}, bf16[128,1536]{0,1:T(8,128)(2,1)S(1)}, u32[]{:S(2)}, u32[]{:S(2)}) collective-permute-start(bf16[128,1536]{0,1:T(8,128)(2,1)S(1)} %slice.122), channel_id=1, source_target_pairs={{0,8},{8,0},{16,24},{24,16},{1,9},{9,1},{17,25},{25,17},{2,10},{10... | collective-permute-start | bytes 1179656 | tf_op jit(solution)/shard_map/ppermute | solution.py:225
  146.5 17.4 %collective-permute-start.27 = (bf16[128,1536]{0,1:T(8,128)(2,1)S(1)}, bf16[128,1536]{0,1:T(8,128)(2,1)S(1)}, u32[]{:S(2)}, u32[]{:S(2)}) collective-permute-start(bf16[128,1536]{0,1:T(8,128)(2,1)S(1)} %slice.123), channel_id=1, source_target_pairs={{0,16},{8,24},{16,0},{24,8},{1,17},{9,25},{17,1},{25,9},{2,18},{10... | collective-permute-start | bytes 1179656 | tf_op jit(solution)/shard_map/ppermute | solution.py:225
  147.0 21.0 %collective-permute-start.25 = (bf16[512,1024]{1,0:T(8,128)(2,1)S(1)}, bf16[512,1024]{1,0:T(8,128)(2,1)S(1)}, u32[]{:S(2)}, u32[]{:S(2)}) collective-permute-start(bf16[512,1024]{1,0:T(8,128)(2,1)S(1)} %pad_maximum_fusion.10), channel_id=1, source_target_pairs={{0,4},{4,0},{1,5},{5,1},{2,6},{6,2},{3,7},{7,3},{8,12},{12,8},{9,1... | collective-permute-start | bytes 3145736 | tf_op jit(solution)/shard_map/ppermute | solution.py:171
  155.7 9.4 %collective-permute-start.30 = (bf16[128,768]{0,1:T(8,128)(2,1)S(1)}, bf16[128,768]{0,1:T(8,128)(2,1)S(1)}, u32[]{:S(2)}, u32[]{:S(2)}) collective-permute-start(bf16[128,768]{0,1:T(8,128)(2,1)S(1)} %slice.154), channel_id=1, source_target_pairs={{0,8},{8,0},{16,24},{24,16},{1,9},{9,1},{17,25},{25,17},{2,10},{10... | collective-permute-start | bytes 589832 | tf_op jit(solution)/shard_map/ppermute | solution.py:225
  186.3 10.3 %collective-permute-start.32 = (bf16[512,1024]{1,0:T(8,128)(2,1)}, bf16[512,1024]{1,0:T(8,128)(2,1)}, u32[]{:S(2)}, u32[]{:S(2)}) collective-permute-start(bf16[512,1024]{1,0:T(8,128)(2,1)} %dynamic_slice.163), channel_id=1, source_target_pairs={{0,4},{4,0},{1,5},{5,1},{2,6},{6,2},{3,7},{7,3},{8,12},{12,8},{9,1... | collective-permute-start | bytes 3145736 | tf_op jit(solution)/shard_map/ppermute | solution.py:171
  187.6 28.0 %collective-permute-start.37 = (bf16[128,768]{1,0:T(8,128)(2,1)S(1)}, bf16[128,768]{1,0:T(8,128)(2,1)S(1)}, u32[]{:S(2)}, u32[]{:S(2)}) collective-permute-start(bf16[128,768]{1,0:T(8,128)(2,1)S(1)} %get-tuple-element.288), channel_id=1, source_target_pairs={{0,8},{8,0},{16,24},{24,16},{1,9},{9,1},{17,25},{25,17},{2,10},{10... | collective-permute-start | bytes 589832 | tf_op jit(solution)/shard_map/ppermute | solution.py:225
  189.2 26.4 %collective-permute-start.35 = (bf16[128,768]{1,0:T(8,128)(2,1)S(1)}, bf16[128,768]{1,0:T(8,128)(2,1)S(1)}, u32[]{:S(2)}, u32[]{:S(2)}) collective-permute-start(bf16[128,768]{1,0:T(8,128)(2,1)S(1)} %get-tuple-element.289), channel_id=1, source_target_pairs={{0,16},{8,24},{16,0},{24,8},{1,17},{9,25},{17,1},{25,9},{2,18},{10... | collective-permute-start | bytes 589832 | tf_op jit(solution)/shard_map/ppermute | solution.py:225
  198.4 13.8 %collective-permute-start.33 = (bf16[256,1024]{1,0:T(8,128)(2,1)S(1)}, bf16[256,1024]{1,0:T(8,128)(2,1)S(1)}, u32[]{:S(2)}, u32[]{:S(2)}) collective-permute-start(bf16[256,1024]{1,0:T(8,128)(2,1)S(1)} %dynamic_slice.206), channel_id=1, source_target_pairs={{0,1},{1,0},{2,3},{3,2},{4,5},{5,4},{6,7},{7,6},{8,9},{9,8},{10,11... | collective-permute-start | bytes 1572872 | tf_op jit(solution)/shard_map/ppermute | solution.py:171
  214.1 12.9 %collective-permute-start.34 = (bf16[256,1024]{1,0:T(8,128)(2,1)S(1)}, bf16[256,1024]{1,0:T(8,128)(2,1)S(1)}, u32[]{:S(2)}, u32[]{:S(2)}) collective-permute-start(bf16[256,1024]{1,0:T(8,128)(2,1)S(1)} %get-tuple-element.267), channel_id=1, source_target_pairs={{0,1},{1,0},{2,3},{3,2},{4,5},{5,4},{6,7},{7,6},{8,9},{9,8},{10,11... | collective-permute-start | bytes 1572872 | tf_op jit(solution)/shard_map/ppermute | solution.py:171
  214.4 18.9 %collective-permute-start.42 = (bf16[128,1536]{1,0:T(8,128)(2,1)S(1)}, bf16[128,1536]{1,0:T(8,128)(2,1)S(1)}, u32[]{:S(2)}, u32[]{:S(2)}) collective-permute-start(bf16[128,1536]{1,0:T(8,128)(2,1)S(1)} %get-tuple-element.273), channel_id=1, source_target_pairs={{0,8},{8,0},{16,24},{24,16},{1,9},{9,1},{17,25},{25,17},{2,10},{10... | collective-permute-start | bytes 1179656 | tf_op jit(solution)/shard_map/ppermute | solution.py:225
  215.0 18.3 %collective-permute-start.40 = (bf16[128,1536]{1,0:T(8,128)(2,1)S(1)}, bf16[128,1536]{1,0:T(8,128)(2,1)S(1)}, u32[]{:S(2)}, u32[]{:S(2)}) collective-permute-start(bf16[128,1536]{1,0:T(8,128)(2,1)S(1)} %get-tuple-element.274), channel_id=1, source_target_pairs={{0,16},{8,24},{16,0},{24,8},{1,17},{9,25},{17,1},{25,9},{2,18},{10... | collective-permute-start | bytes 1179656 | tf_op jit(solution)/shard_map/ppermute | solution.py:225
  215.8 17.3 %collective-permute-start.36 = (bf16[256,768]{1,0:T(8,128)(2,1)S(1)}, bf16[256,768]{1,0:T(8,128)(2,1)S(1)}, u32[]{:S(2)}, u32[]{:S(2)}) collective-permute-start(bf16[256,768]{1,0:T(8,128)(2,1)S(1)} %pad_maximum_fusion.20), channel_id=1, source_target_pairs={{0,8},{8,0},{16,24},{24,16},{1,9},{9,1},{17,25},{25,17},{2,10},{10... | collective-permute-start | bytes 1179656 | tf_op jit(solution)/shard_map/ppermute | solution.py:225
  217.3 15.9 %collective-permute-start.38 = (bf16[256,768]{1,0:T(8,128)(2,1)S(1)}, bf16[256,768]{1,0:T(8,128)(2,1)S(1)}, u32[]{:S(2)}, u32[]{:S(2)}) collective-permute-start(bf16[256,768]{1,0:T(8,128)(2,1)S(1)} %pad_maximum_fusion.21), channel_id=1, source_target_pairs={{0,16},{8,24},{16,0},{24,8},{1,17},{9,25},{17,1},{25,9},{2,18},{10... | collective-permute-start | bytes 1179656 | tf_op jit(solution)/shard_map/ppermute | solution.py:225
  233.6 28.3 %collective-permute-start.41 = (bf16[256,1536]{1,0:T(8,128)(2,1)S(1)}, bf16[256,1536]{1,0:T(8,128)(2,1)S(1)}, u32[]{:S(2)}, u32[]{:S(2)}) collective-permute-start(bf16[256,1536]{1,0:T(8,128)(2,1)S(1)} %pad_maximum_fusion.12), channel_id=1, source_target_pairs={{0,8},{8,0},{16,24},{24,16},{1,9},{9,1},{17,25},{25,17},{2,10},{10... | collective-permute-start | bytes 2359304 | tf_op jit(solution)/shard_map/ppermute | solution.py:225
  235.2 26.7 %collective-permute-start.43 = (bf16[256,1536]{1,0:T(8,128)(2,1)S(1)}, bf16[256,1536]{1,0:T(8,128)(2,1)S(1)}, u32[]{:S(2)}, u32[]{:S(2)}) collective-permute-start(bf16[256,1536]{1,0:T(8,128)(2,1)S(1)} %pad_maximum_fusion.13), channel_id=1, source_target_pairs={{0,16},{8,24},{16,0},{24,8},{1,17},{9,25},{17,1},{25,9},{2,18},{10... | collective-permute-start | bytes 2359304 | tf_op jit(solution)/shard_map/ppermute | solution.py:225
  236.0 25.9 %collective-permute-start.44 = (bf16[256,768]{1,0:T(8,128)(2,1)S(1)}, bf16[256,768]{1,0:T(8,128)(2,1)S(1)}, u32[]{:S(2)}, u32[]{:S(2)}) collective-permute-start(bf16[256,768]{1,0:T(8,128)(2,1)S(1)} %add_convert_fusion.3), channel_id=1, source_target_pairs={{0,0},{2,4},{4,2},{6,6},{1,1},{3,5},{5,3},{7,7},{8,8},{10,12},{12,... | collective-permute-start | bytes 1179656 | tf_op jit(solution)/shard_map/ppermute | solution.py:167
  239.7 22.2 %collective-permute-start.45 = (bf16[128,512]{1,0:T(8,128)(2,1)S(1)}, bf16[128,512]{1,0:T(8,128)(2,1)S(1)}, u32[]{:S(2)}, u32[]{:S(2)}) collective-permute-start(bf16[128,512]{1,0:T(8,128)(2,1)S(1)} %get-tuple-element.295), channel_id=1, source_target_pairs={{0,16},{8,24},{16,0},{24,8},{1,17},{9,25},{17,1},{25,9},{2,18},{10... | collective-permute-start | bytes 393224 | tf_op jit(solution)/shard_map/ppermute | solution.py:225
  241.2 20.8 %collective-permute-start.46 = (bf16[128,512]{1,0:T(8,128)(2,1)S(1)}, bf16[128,512]{1,0:T(8,128)(2,1)S(1)}, u32[]{:S(2)}, u32[]{:S(2)}) collective-permute-start(bf16[128,512]{1,0:T(8,128)(2,1)S(1)} %get-tuple-element.294), channel_id=1, source_target_pairs={{0,8},{8,0},{16,24},{24,16},{1,9},{9,1},{17,25},{25,17},{2,10},{10... | collective-permute-start | bytes 393224 | tf_op jit(solution)/shard_map/ppermute | solution.py:225
  267.0 12.7 %collective-permute-start.48 = (bf16[128,1024]{1,0:T(8,128)(2,1)S(1)}, bf16[128,1024]{1,0:T(8,128)(2,1)S(1)}, u32[]{:S(2)}, u32[]{:S(2)}) collective-permute-start(bf16[128,1024]{1,0:T(8,128)(2,1)S(1)} %get-tuple-element.277), channel_id=1, source_target_pairs={{0,8},{8,0},{16,24},{24,16},{1,9},{9,1},{17,25},{25,17},{2,10},{10... | collective-permute-start | bytes 786440 | tf_op jit(solution)/shard_map/ppermute | solution.py:225
  268.4 11.2 %collective-permute-start.49 = (bf16[256,512]{1,0:T(8,128)(2,1)S(1)}, bf16[256,512]{1,0:T(8,128)(2,1)S(1)}, u32[]{:S(2)}, u32[]{:S(2)}) collective-permute-start(bf16[256,512]{1,0:T(8,128)(2,1)S(1)} %pad_maximum_fusion.24), channel_id=1, source_target_pairs={{0,8},{8,0},{16,24},{24,16},{1,9},{9,1},{17,25},{25,17},{2,10},{10... | collective-permute-start | bytes 786440 | tf_op jit(solution)/shard_map/ppermute | solution.py:225
  269.2 10.4 %collective-permute-start.50 = (bf16[256,512]{1,0:T(8,128)(2,1)S(1)}, bf16[256,512]{1,0:T(8,128)(2,1)S(1)}, u32[]{:S(2)}, u32[]{:S(2)}) collective-permute-start(bf16[256,512]{1,0:T(8,128)(2,1)S(1)} %pad_maximum_fusion.25), channel_id=1, source_target_pairs={{0,16},{8,24},{16,0},{24,8},{1,17},{9,25},{17,1},{25,9},{2,18},{10... | collective-permute-start | bytes 786440 | tf_op jit(solution)/shard_map/ppermute | solution.py:225
  270.8 31.3 %collective-permute-start.53 = (bf16[256,1536]{1,0:T(8,128)(2,1)S(1)}, bf16[256,1536]{1,0:T(8,128)(2,1)S(1)}, u32[]{:S(2)}, u32[]{:S(2)}) collective-permute-start(bf16[256,1536]{1,0:T(8,128)(2,1)S(1)} %add_convert_fusion), channel_id=1, source_target_pairs={{0,0},{2,4},{4,2},{6,6},{1,1},{3,5},{5,3},{7,7},{8,8},{10,12},{12,... | collective-permute-start | bytes 2359304 | tf_op jit(solution)/shard_map/ppermute | solution.py:167
  273.6 33.3 %collective-permute-start.57 = (bf16[512,1024]{1,0:T(8,128)(2,1)S(1)}, bf16[512,1024]{1,0:T(8,128)(2,1)S(1)}, u32[]{:S(2)}, u32[]{:S(2)}) collective-permute-start(bf16[512,1024]{1,0:T(8,128)(2,1)S(1)} %dynamic_slice.167), channel_id=1, source_target_pairs={{0,4},{4,0},{1,5},{5,1},{2,6},{6,2},{3,7},{7,3},{8,12},{12,8},{9,1... | collective-permute-start | bytes 3145736 | tf_op jit(solution)/shard_map/ppermute | solution.py:171
  279.8 22.3 %collective-permute-start.51 = (bf16[256,1024]{1,0:T(8,128)(2,1)S(1)}, bf16[256,1024]{1,0:T(8,128)(2,1)S(1)}, u32[]{:S(2)}, u32[]{:S(2)}) collective-permute-start(bf16[256,1024]{1,0:T(8,128)(2,1)S(1)} %pad_maximum_fusion.18), channel_id=1, source_target_pairs={{0,8},{8,0},{16,24},{24,16},{1,9},{9,1},{17,25},{25,17},{2,10},{10... | collective-permute-start | bytes 1572872 | tf_op jit(solution)/shard_map/ppermute | solution.py:225
  281.5 20.7 %collective-permute-start.52 = (bf16[256,1024]{1,0:T(8,128)(2,1)S(1)}, bf16[256,1024]{1,0:T(8,128)(2,1)S(1)}, u32[]{:S(2)}, u32[]{:S(2)}) collective-permute-start(bf16[256,1024]{1,0:T(8,128)(2,1)S(1)} %pad_maximum_fusion.19), channel_id=1, source_target_pairs={{0,16},{8,24},{16,0},{24,8},{1,17},{9,25},{17,1},{25,9},{2,18},{10... | collective-permute-start | bytes 1572872 | tf_op jit(solution)/shard_map/ppermute | solution.py:225
  285.6 23.1 %collective-permute-start.56 = (bf16[512,1024]{1,0:T(8,128)(2,1)S(1)}, bf16[512,1024]{1,0:T(8,128)(2,1)S(1)}, u32[]{:S(2)}, u32[]{:S(2)}) collective-permute-start(bf16[512,1024]{1,0:T(8,128)(2,1)S(1)} %constant_dynamic-slice_fusion.10), channel_id=1, source_target_pairs={{0,4},{4,0},{1,5},{5,1},{2,6},{6,2},{3,7},{7,3},{8,12},{12,8},{9,1... | collective-permute-start | bytes 3145736 | tf_op jit(solution)/shard_map/ppermute | solution.py:171
  304.5 14.2 %collective-permute-start.60 = (bf16[128,1536]{1,0:T(8,128)(2,1)S(1)}, bf16[128,1536]{1,0:T(8,128)(2,1)S(1)}, u32[]{:S(2)}, u32[]{:S(2)}) collective-permute-start(bf16[128,1536]{1,0:T(8,128)(2,1)S(1)} %constant_dynamic-slice_fusion.7), channel_id=1, source_target_pairs={{0,4},{4,0},{1,5},{5,1},{2,6},{6,2},{3,7},{7,3},{8,12},{12,8},{9,1... | collective-permute-start | bytes 1179656 | tf_op jit(solution)/shard_map/ppermute | solution.py:171
  309.2 10.6 %collective-permute-start.58 = (bf16[128,1024]{1,0:T(8,128)(2,1)S(1)}, bf16[128,1024]{1,0:T(8,128)(2,1)S(1)}, u32[]{:S(2)}, u32[]{:S(2)}) collective-permute-start(bf16[128,1024]{1,0:T(8,128)(2,1)S(1)} %constant_dynamic-slice_fusion.9), channel_id=1, source_target_pairs={{0,4},{4,0},{1,5},{5,1},{2,6},{6,2},{3,7},{7,3},{8,12},{12,8},{9,1... | collective-permute-start | bytes 786440 | tf_op jit(solution)/shard_map/ppermute | solution.py:171
  322.8 25.3 %all-to-all-start = ((bf16[8,128,768]{2,1,0:T(8,128)(2,1)}), bf16[8,128,768]{2,1,0:T(8,128)(2,1)}, u32[]{:S(2)}, u32[]{:S(2)}) async-start(bf16[8,128,768]{2,1,0:T(8,128)(2,1)} %get-tuple-element.205), calls=%async_computation | async-start | bytes 3145728 | tf_op jit(solution)/shard_map/all_to_all | solution.py:604
  327.3 14.8 %collective-permute-start.62 = (bf16[256,1024]{1,0:T(8,128)(2,1)S(1)}, bf16[256,1024]{1,0:T(8,128)(2,1)S(1)}, u32[]{:S(2)}, u32[]{:S(2)}) collective-permute-start(bf16[256,1024]{1,0:T(8,128)(2,1)S(1)} %dynamic-slice_convert_fusion), channel_id=1, source_target_pairs={{0,1},{1,0},{2,3},{3,2},{4,5},{5,4},{6,7},{7,6},{8,9},{9,8},{10,11... | collective-permute-start | bytes 1572872 | tf_op jit(solution)/shard_map/ppermute | solution.py:171
  328.7 26.4 %collective-permute-start.66 = (bf16[256,1024]{1,0:T(8,128)(2,1)S(1)}, bf16[256,1024]{1,0:T(8,128)(2,1)}, u32[]{:S(2)}, u32[]{:S(2)}) collective-permute-start(bf16[256,1024]{1,0:T(8,128)(2,1)S(1)} %dynamic_slice.205), channel_id=1, source_target_pairs={{0,1},{1,0},{2,3},{3,2},{4,5},{5,4},{6,7},{7,6},{8,9},{9,8},{10,11... | collective-permute-start | bytes 1572872 | tf_op jit(solution)/shard_map/ppermute | solution.py:171
  348.2 16.9 %collective-permute-start.63 = (bf16[1024,768]{1,0:T(8,128)(2,1)}, bf16[1024,768]{1,0:T(8,128)(2,1)}, u32[]{:S(2)}, u32[]{:S(2)}) collective-permute-start(bf16[1024,768]{1,0:T(8,128)(2,1)} %bitcast.6.refs_0_), channel_id=1, source_target_pairs={{2,1},{7,6},{10,9},{15,14},{18,17},{23,22},{31,30}} | collective-permute-start | bytes 4718600 | tf_op jit(solution)/shard_map/ppermute | solution.py:610
  350.0 15.1 %collective-permute-start.64 = (bf16[1024,768]{1,0:T(8,128)(2,1)}, bf16[1024,768]{1,0:T(8,128)(2,1)}, u32[]{:S(2)}, u32[]{:S(2)}) collective-permute-start(bf16[1024,768]{1,0:T(8,128)(2,1)} %bitcast.6.refs_0_), channel_id=1, source_target_pairs={{3,1},{4,6},{11,9},{12,14},{19,17},{20,22},{28,30}} | collective-permute-start | bytes 4718600 | tf_op jit(solution)/shard_map/ppermute | solution.py:610
  351.9 32.5 %collective-permute-start.65 = (bf16[1024,768]{1,0:T(8,128)(2,1)}, bf16[1024,768]{1,0:T(8,128)(2,1)}, u32[]{:S(2)}, u32[]{:S(2)}) collective-permute-start(bf16[1024,768]{1,0:T(8,128)(2,1)} %bitcast.6.refs_0_), channel_id=1, source_target_pairs={{0,1},{5,6},{8,9},{13,14},{16,17},{21,22},{29,30}} | collective-permute-start | bytes 4718600 | tf_op jit(solution)/shard_map/ppermute | solution.py:610
  391.7 87.1 %collective-permute-start.75 = (bf16[1024,384]{1,0:T(8,128)(2,1)S(1)}, bf16[1024,384]{1,0:T(8,128)(2,1)S(1)}, u32[]{:S(2)}, u32[]{:S(2)}) collective-permute-start(bf16[1024,384]{1,0:T(8,128)(2,1)S(1)} %get-tuple-element.238), channel_id=1, source_target_pairs={{1,0},{6,5},{9,8},{14,13},{17,16},{22,21},{30,29}} | collective-permute-start | bytes 2359304 | tf_op jit(solution)/shard_map/ppermute | solution.py:620
  393.0 87.4 %collective-permute-start.74 = (bf16[1024,384]{1,0:T(8,128)(2,1)S(1)}, bf16[1024,384]{1,0:T(8,128)(2,1)S(1)}, u32[]{:S(2)}, u32[]{:S(2)}) collective-permute-start(bf16[1024,384]{1,0:T(8,128)(2,1)S(1)} %get-tuple-element.237), channel_id=1, source_target_pairs={{1,3},{6,4},{9,11},{14,12},{17,19},{22,20},{30,28}} | collective-permute-start | bytes 2359304 | tf_op jit(solution)/shard_map/ppermute | solution.py:620
  393.7 86.7 %collective-permute-start.73 = (bf16[1024,384]{1,0:T(8,128)(2,1)S(1)}, bf16[1024,384]{1,0:T(8,128)(2,1)S(1)}, u32[]{:S(2)}, u32[]{:S(2)}) collective-permute-start(bf16[1024,384]{1,0:T(8,128)(2,1)S(1)} %get-tuple-element.236), channel_id=1, source_target_pairs={{1,2},{6,7},{9,10},{14,15},{17,18},{22,23},{30,31}} | collective-permute-start | bytes 2359304 | tf_op jit(solution)/shard_map/ppermute | solution.py:620
  394.5 101.3 %collective-permute-start.78 = (bf16[1024,384]{1,0:T(8,128)(2,1)}, bf16[1024,384]{1,0:T(8,128)(2,1)}, u32[]{:S(2)}, u32[]{:S(2)}) collective-permute-start(bf16[1024,384]{1,0:T(8,128)(2,1)} %get-tuple-element.242), channel_id=1, source_target_pairs={{1,0},{6,5},{9,8},{14,13},{17,16},{22,21},{30,29}} | collective-permute-start | bytes 2359304 | tf_op jit(solution)/shard_map/ppermute | solution.py:620
  395.8 100.0 %collective-permute-start.77 = (bf16[1024,384]{1,0:T(8,128)(2,1)S(1)}, bf16[1024,384]{1,0:T(8,128)(2,1)}, u32[]{:S(2)}, u32[]{:S(2)}) collective-permute-start(bf16[1024,384]{1,0:T(8,128)(2,1)S(1)} %get-tuple-element.241), channel_id=1, source_target_pairs={{1,3},{6,4},{9,11},{14,12},{17,19},{22,20},{30,28}} | collective-permute-start | bytes 2359304 | tf_op jit(solution)/shard_map/ppermute | solution.py:620
  478.9 16.9 %collective-permute-start.76 = (bf16[1024,384]{1,0:T(8,128)(2,1)S(1)}, bf16[1024,384]{1,0:T(8,128)(2,1)}, u32[]{:S(2)}, u32[]{:S(2)}) collective-permute-start(bf16[1024,384]{1,0:T(8,128)(2,1)S(1)} %get-tuple-element.240), channel_id=1, source_target_pairs={{1,2},{6,7},{9,10},{14,15},{17,18},{22,23},{30,31}} | collective-permute-start | bytes 2359304 | tf_op jit(solution)/shard_map/ppermute | solution.py:620
  481.5 17.0 %all-to-all-start.1 = ((bf16[8,128,384]{2,1,0:T(8,128)(2,1)}), bf16[8,128,384]{2,1,0:T(8,128)(2,1)S(1)}, u32[]{:S(2)}, u32[]{:S(2)}) async-start(bf16[8,128,384]{2,1,0:T(8,128)(2,1)} %bitcast.37), calls=%async_computation.1 | async-start | bytes 1572864 | tf_op jit(solution)/shard_map/all_to_all | solution.py:626
  485.0 39.0 %collective-permute-start.71 = (bf16[256,1024]{1,0:T(8,128)(2,1)}, bf16[256,1024]{1,0:T(8,128)(2,1)}, u32[]{:S(2)}, u32[]{:S(2)}) collective-permute-start(bf16[256,1024]{1,0:T(8,128)(2,1)} %add_convert_fusion.1), channel_id=1, source_target_pairs={{0,0},{2,4},{4,2},{6,6},{1,1},{3,5},{5,3},{7,7},{8,8},{10,12},{12,... | collective-permute-start | bytes 1572872 | tf_op jit(solution)/shard_map/ppermute | solution.py:167
  490.4 35.7 %collective-permute-start.72 = (bf16[256,1024]{1,0:T(8,128)(2,1)}, bf16[256,1024]{1,0:T(8,128)(2,1)}, u32[]{:S(2)}, u32[]{:S(2)}) collective-permute-start(bf16[256,1024]{1,0:T(8,128)(2,1)} %fusion.12), channel_id=1, source_target_pairs={{0,0},{2,4},{4,2},{6,6},{1,1},{3,5},{5,3},{7,7},{8,8},{10,12},{12,... | collective-permute-start | bytes 1572872 | tf_op jit(solution)/shard_map/ppermute | solution.py:167
  498.5 30.4 %all-to-all-start.2 = ((bf16[8,128,384]{2,1,0:T(8,128)(2,1)}), bf16[8,128,384]{2,1,0:T(8,128)(2,1)S(1)}, u32[]{:S(2)}, u32[]{:S(2)}) async-start(bf16[8,128,384]{2,1,0:T(8,128)(2,1)} %bitcast.36), calls=%async_computation.2 | async-start | bytes 1572864 | tf_op jit(solution)/shard_map/all_to_all | solution.py:626
  516.2 12.1 %collective-permute-start.79 = (f32[2304]{0:T(1024)S(1)}, f32[2304]{0:T(1024)S(1)}, u32[]{:S(2)}, u32[]{:S(2)}) collective-permute-start(f32[2304]{0:T(1024)S(1)} %add.324), channel_id=1, source_target_pairs={{0,2},{2,0},{1,3},{3,1},{4,6},{6,4},{5,7},{7,5},{8,10},{10,8},{9,1... | collective-permute-start | bytes 27656 | tf_op jit(solution)/shard_map/ppermute | solution.py:314
  (78 other events, 757.2 us)

commit v3 on v2

--- a/solution.py
+++ b/solution.py
@@ -883,14 +883,16 @@
     input_grad = (d_residual + d_input_norm).astype(bf16)
     gain_grad = jnp.concatenate([d_gain_attn, d_gain_mlp, d_gain_heads.reshape(-1)])
     gain_grad = sum_everywhere(gain_grad, [(name, lax.axis_size(name)) for name in ("core", "pl")])
-    pieces, input_grad, block_out, gain_grad = tied(pieces, input_grad, block_out, gain_grad)
+    both = jnp.concatenate([input_grad, block_out], axis=0)
+    pieces, both, gain_grad = tied(pieces, both, gain_grad)
     back = orthogonalize(owns(group, homes), pieces)
     gain_grad = sum_everywhere(gain_grad, [("lo", lax.axis_size("lo"))])
-    back, input_grad, block_out, gain_grad = tied(back, input_grad, block_out, gain_grad)
+    back, both, gain_grad = tied(back, both, gain_grad)
+    back, both = tied(back, swap(both))
     half = len(back) // 2
     received = [from_homes(group, homes, part) for part in (back[:half], back[half:])]
-    input_grad = swap(input_grad).astype(jnp.float32)
-    block_out = swap(block_out).astype(jnp.float32)
+    input_grad = half_of(both, 0).astype(jnp.float32)
+    block_out = half_of(both, 1).astype(jnp.float32)
     received[1], gain_grad = tied(received[1], gain_grad)
     gain_grad = sum_everywhere(gain_grad, [("hi", 2)])
     updated = update([from_columns(part) for part in received], masters, homes)

time: 541 us -> 523 us (0.967)
  starting transfers between devices: 174 us -> 145 us
  waiting for transfers between devices: 219 us -> 237 us
    all_to_all x2, starting transfers between devices: 21.1 us -> 7.24 us  [from_columns(): lax.all_to_all(received.reshape(shape), DP, split_axis=0, concat_axis=0,...]
    ppermute x6, waiting for transfers between devices: 81.6 us -> 92.3 us  [from_homes(): received = received + lax.ppermute(back[step], DP + TENSOR, pairs)]
    ppermute x12 -> x11, starting transfers between devices: 19.8 us -> 9.76 us  [swap(): lax.ppermute(values, ('core', 'hi'), [(0, 0), (1, 2), (2, 1), (3, 3)])]
    all_to_all x2, waiting for transfers between devices: 0.01 us -> 6.11 us  [from_columns(): lax.all_to_all(received.reshape(shape), DP, split_axis=0, concat_axis=0,...]
  transfers between devices with their start and end apart: 83 -> 82, of which waited for: 26 -> 29; matrix products, arithmetic and copies ran while one was open for 11% -> 11% of each run, Pallas kernels for 8% -> 8%
where the time goes in v3:
time: 523 us; the launch traced here: 517 us
  waiting for transfers between devices  237 us (45%)
  starting transfers between devices  145 us (28%)
  Pallas kernels  45.4 us (9%)
  other arithmetic  34.3 us (7%)
  matrix products  30.5 us (6%)
  local copies, waits for them, and re-layouts  22.2 us (4%)
    ppermute x6, waiting for transfers between devices, from_homes(): received = received + lax.ppermute(back[step], DP + TENSOR, pairs)  92.3 us
    ppermute x23, waiting for transfers between devices, to_partner(): return lax.ppermute(values, name, [(0, 1), (1, 0)])  72.4 us
    ppermute x23, starting transfers between devices, to_partner(): return lax.ppermute(values, name, [(0, 1), (1, 0)])  67.5 us
    pallas_call x5, Pallas kernels, in_vmem(): pl.pallas_call(kernel, out_shape=results, in_specs=[pl.BlockSpec(memory_s...  41.1 us
    ppermute x31, waiting for transfers between devices, exchange(): lax.ppermute(values, 'pl', [(index, index ^ stride) for index in range(co...  35.5 us
    ppermute x31, starting transfers between devices, exchange(): lax.ppermute(values, 'pl', [(index, index ^ stride) for index in range(co...  35.3 us
    ppermute x3, waiting for transfers between devices, to_homes(): lax.ppermute(owned, DP + TENSOR, toward_home(group, homes, step))  19 us
    dot_general x4, matrix products, contract_rows(): lax.dot_general(left, right, (((0,), (0,)), ((), ())), preferred_element_...  14.4 us
  transfers between devices with their start and end apart: 82, of which 29 were waited for; matrix products, arithmetic and copies ran while one was open for 11% of the time, Pallas kernels for 8%

profile of v3, /device:TPU:0, one launch (start us, length us, event | category | flops | bytes accessed | tf_op | source)
XLA Modules:
  0.0 517.5 jit_solution(17697708327371241110)
XLA Ops:
  8.3 4.7 collective-permute-start.7
  16.1 1.7 collective-permute-start.2
  17.9 4.6 collective-permute-done.4
  24.4 1.6 collective-permute-start.6
  28.1 6.5 %collective-permute-done.6 = bf16[256,1024]{1,0:T(8,128)(2,1)S(1)} collective-permute-done((bf16[256,1024]{1,0:T(8,128)(2,1)S(1)}, bf16[256,1024]{1,0:T(8,128)(2,1)S(1)}, u32[]{:S(2)}, u32[]{:S(2)}) %collective-permute-start.6) | collective-permute-done | bytes 524320 | tf_op jit(solution)/shard_map/ppermute | solution.py:171
  35.1 19.1 %collective-permute-start.8 = (bf16[512,1024]{1,0:T(8,128)(2,1)S(1)}, bf16[512,1024]{1,0:T(8,128)(2,1)S(1)}, u32[]{:S(2)}, u32[]{:S(2)}) collective-permute-start(bf16[512,1024]{1,0:T(8,128)(2,1)S(1)} %pad_maximum_fusion.8), channel_id=1, source_target_pairs={{0,4},{4,0},{1,5},{5,1},{2,6},{6,2},{3,7},{7,3},{8,12},{12,8},{9,1... | collective-permute-start | bytes 3145736 | tf_op jit(solution)/shard_map/ppermute | solution.py:171
  54.2 1.9 fusion.15
  60.8 4.0 collective-permute-done.9
  67.8 6.9 %shard_map.395 = (bf16[1024,512]{1,0:T(8,128)(2,1)S(1)}, bf16[1024,256]{1,0:T(8,128)(2,1)S(1)}, bf16[1024,256]{1,0:T(8,128)(2,1)S(1)}, f32[1024,768]{1,0:T(8,128)}) custom-call(bf16[1024,1024]{1,0:T(8,128)(2,1)S(1)} %pad_maximum_fusion.1.rows_ref, bf16[1024,1024]{1,0:T(8,128)(2,1)} %copy-done.37, f32[1024,128]{1,0:T(8,128)S(1)} %get-tuple-element.332.cosine_ref, ...), custom_call_target="tpu_custom_call" | custom-call | flops 2147483648 | bytes 10486784 | tf_op jit(solution)/shard_map/pallas_call | solution.py:512
  78.3 9.9 %shard_map.396 = (bf16[1024,512]{1,0:T(8,128)(2,1)S(1)}, f32[4,1024]{1,0:T(4,128)S(1)}) custom-call(bf16[1024,512]{1,0:T(8,128)(2,1)S(1)} %get-tuple-element.160.query_ref, bf16[1024,256]{1,0:T(8,128)(2,1)S(1)} %get-tuple-element.161.key_ref, bf16[1024,256]{1,0:T(8,128)(2,1)S(1)} %get-tuple-element.162.value_ref, s32[1,1024]{1,0:T(1,128)S(1)} %bitcast.32), custom_call_target="tpu_custom_call" | custom-call | flops 2147483648 | bytes 3166208 | tf_op jit(solution)/shard_map/pallas_call | solution.py:512
  88.3 2.0 collective-permute-done.15
  93.3 4.3 collective-permute-start.17
  97.6 2.6 collective-permute-done.17
  100.2 3.3 convert_add_fusion.3
  103.5 2.1 dynamic-slice_convert_fusion.1
  108.3 1.6 collective-permute-start.23
  111.4 8.8 %collective-permute-done.18 = bf16[256,1024]{1,0:T(8,128)(2,1)} collective-permute-done((bf16[256,1024]{1,0:T(8,128)(2,1)}, bf16[256,1024]{1,0:T(8,128)(2,1)}, u32[]{:S(2)}, u32[]{:S(2)}) %collective-permute-start.18) | collective-permute-done | bytes 524320 | tf_op jit(solution)/shard_map/ppermute | solution.py:171
  120.1 1.6 convert_add_fusion.4
  124.2 17.7 %collective-permute-done.22 = bf16[256,1024]{1,0:T(8,128)(2,1)S(1)} collective-permute-done((bf16[256,1024]{1,0:T(8,128)(2,1)S(1)}, bf16[256,1024]{1,0:T(8,128)(2,1)S(1)}, u32[]{:S(2)}, u32[]{:S(2)}) %collective-permute-start.22) | collective-permute-done | bytes 524320 | tf_op jit(solution)/shard_map/ppermute | solution.py:171
  147.4 8.2 %collective-permute-done.29 = bf16[256,768]{0,1:T(8,128)(2,1)S(1)} collective-permute-done((bf16[256,768]{0,1:T(8,128)(2,1)S(1)}, bf16[256,768]{0,1:T(8,128)(2,1)S(1)}, u32[]{:S(2)}, u32[]{:S(2)}) %collective-permute-start.29) | collective-permute-done | bytes 393248 | tf_op jit(solution)/shard_map/ppermute | solution.py:225
  156.4 5.9 %collective-permute-done.26 = bf16[128,1536]{0,1:T(8,128)(2,1)S(1)} collective-permute-done((bf16[128,1536]{0,1:T(8,128)(2,1)S(1)}, bf16[128,1536]{0,1:T(8,128)(2,1)S(1)}, u32[]{:S(2)}, u32[]{:S(2)}) %collective-permute-start.26) | collective-permute-done | bytes 393248 | tf_op jit(solution)/shard_map/ppermute | solution.py:225
  165.1 2.9 collective-permute-done.31
  168.2 3.5 fusion.26
  173.7 3.1 convolution_convert_fusion.5
  176.8 3.5 fusion.2
  180.3 3.6 fusion.5
  190.7 6.0 %convolution_convert_fusion = bf16[1024,1536]{1,0:T(8,128)(2,1)S(1)} fusion(bf16[1024,1024]{1,0:T(8,128)(2,1)} %copy-done.48, bf16[1024,768]{1,0:T(8,128)(2,1)} %copy-done.58, bf16[1024,768]{1,0:T(8,128)(2,1)} %copy-done.57), kind=kOutput, calls=%fused_computation.1 | convolution fusion | flops 3229089792 | bytes 8388608 | tf_op jit(solution)/shard_map/dot_general | solution.py:45
  196.7 1.6 convert_add_fusion.2
  198.7 13.6 %collective-permute-done.33 = bf16[256,1024]{1,0:T(8,128)(2,1)S(1)} collective-permute-done((bf16[256,1024]{1,0:T(8,128)(2,1)S(1)}, bf16[256,1024]{1,0:T(8,128)(2,1)S(1)}, u32[]{:S(2)}, u32[]{:S(2)}) %collective-permute-start.33) | collective-permute-done | bytes 524320 | tf_op jit(solution)/shard_map/ppermute | solution.py:171
  218.8 8.2 %collective-permute-done.34 = bf16[256,1024]{1,0:T(8,128)(2,1)S(1)} collective-permute-done((bf16[256,1024]{1,0:T(8,128)(2,1)S(1)}, bf16[256,1024]{1,0:T(8,128)(2,1)S(1)}, u32[]{:S(2)}, u32[]{:S(2)}) %collective-permute-start.34) | collective-permute-done | bytes 524320 | tf_op jit(solution)/shard_map/ppermute | solution.py:171
  227.1 5.9 %collective-permute-done.36 = bf16[256,768]{1,0:T(8,128)(2,1)S(1)} collective-permute-done((bf16[256,768]{1,0:T(8,128)(2,1)S(1)}, bf16[256,768]{1,0:T(8,128)(2,1)S(1)}, u32[]{:S(2)}, u32[]{:S(2)}) %collective-permute-start.36) | collective-permute-done | bytes 393248 | tf_op jit(solution)/shard_map/ppermute | solution.py:225
  233.5 1.6 collective-permute-start.41
  241.7 20.1 %shard_map.397 = (bf16[1024,1024]{1,0:T(8,128)(2,1)}, f32[2,128]{1,0:T(2,128)S(1)}) custom-call(bf16[1024,1024]{1,0:T(8,128)(2,1)} %pad_maximum_fusion.2.state_ref, bf16[1024,512]{1,0:T(8,128)(2,1)S(1)} %constant_dynamic-update-slice_fusion.10.out_ref, bf16[1024,512]{1,0:T(8,128)(2,1)S(1)} %get-tuple-element.160.query_ref, bf16[1024,256]{1,0:T(8,128)(2,1)S(1)} %copy-done.17, ...), custom_call_target="tpu_custom_call" | custom-call | flops 6442450944 | bytes 11556864 | tf_op jit(solution)/shard_map/pallas_call | solution.py:512
  262.0 4.1 convolution_convert_fusion.2
  271.6 1.8 convolution_convert_fusion.4
  273.6 6.0 %collective-permute-start.57 = (bf16[512,1024]{1,0:T(8,128)(2,1)S(1)}, bf16[512,1024]{1,0:T(8,128)(2,1)S(1)}, u32[]{:S(2)}, u32[]{:S(2)}) collective-permute-start(bf16[512,1024]{1,0:T(8,128)(2,1)S(1)} %dynamic_slice.175), channel_id=1, source_target_pairs={{0,4},{4,0},{1,5},{5,1},{2,6},{6,2},{3,7},{7,3},{8,12},{12,8},{9,1... | collective-permute-start | bytes 3145736 | tf_op jit(solution)/shard_map/ppermute | solution.py:171
  283.0 2.4 convolution_convert_fusion.1
  285.6 16.6 %collective-permute-start.56 = (bf16[512,1024]{1,0:T(8,128)(2,1)S(1)}, bf16[512,1024]{1,0:T(8,128)(2,1)S(1)}, u32[]{:S(2)}, u32[]{:S(2)}) collective-permute-start(bf16[512,1024]{1,0:T(8,128)(2,1)S(1)} %constant_dynamic-slice_fusion.10), channel_id=1, source_target_pairs={{0,4},{4,0},{1,5},{5,1},{2,6},{6,2},{3,7},{7,3},{8,12},{12,8},{9,1... | collective-permute-start | bytes 3145736 | tf_op jit(solution)/shard_map/ppermute | solution.py:171
  307.0 1.7 convert_add_fusion
  309.2 9.5 %collective-permute-start.58 = (bf16[128,1024]{1,0:T(8,128)(2,1)S(1)}, bf16[128,1024]{1,0:T(8,128)(2,1)S(1)}, u32[]{:S(2)}, u32[]{:S(2)}) collective-permute-start(bf16[128,1024]{1,0:T(8,128)(2,1)S(1)} %constant_dynamic-slice_fusion.9), channel_id=1, source_target_pairs={{0,4},{4,0},{1,5},{5,1},{2,6},{6,2},{3,7},{7,3},{8,12},{12,8},{9,1... | collective-permute-start | bytes 786440 | tf_op jit(solution)/shard_map/ppermute | solution.py:171
  320.0 2.9 shard_map.398
  322.9 4.3 all-to-all-start
  328.7 2.0 collective-permute-start.66
  330.7 11.3 %collective-permute-done.62 = bf16[256,1024]{1,0:T(8,128)(2,1)S(1)} collective-permute-done((bf16[256,1024]{1,0:T(8,128)(2,1)S(1)}, bf16[256,1024]{1,0:T(8,128)(2,1)S(1)}, u32[]{:S(2)}, u32[]{:S(2)}) %collective-permute-start.62) | collective-permute-done | bytes 524320 | tf_op jit(solution)/shard_map/ppermute | solution.py:171
  343.5 4.7 all-to-all-done
  348.2 1.8 collective-permute-start.63
  350.0 1.9 collective-permute-start.64
  351.9 2.7 collective-permute-start.65
  354.7 1.7 add_convert_fusion.1
  358.9 2.9 collective-permute-done.68
  362.4 3.1 collective-permute-done.69
  365.4 19.0 %collective-permute-done.65.refs_3_ = bf16[1024,768]{1,0:T(8,128)(2,1)} collective-permute-done((bf16[1024,768]{1,0:T(8,128)(2,1)}, bf16[1024,768]{1,0:T(8,128)(2,1)}, u32[]{:S(2)}, u32[]{:S(2)}) %collective-permute-start.65) | collective-permute-done | bytes 1572896 | tf_op jit(solution)/shard_map/ppermute | solution.py:610
  384.4 3.0 collective-permute-start.70
  387.5 4.3 shard_map.399
  396.5 1.6 collective-permute-start.76
  398.1 81.5 %collective-permute-done.74 = bf16[1024,384]{1,0:T(8,128)(2,1)S(1)} collective-permute-done((bf16[1024,384]{1,0:T(8,128)(2,1)S(1)}, bf16[1024,384]{1,0:T(8,128)(2,1)S(1)}, u32[]{:S(2)}, u32[]{:S(2)}) %collective-permute-start.74) | collective-permute-done | bytes 786464 | tf_op jit(solution)/shard_map/ppermute | solution.py:620
  479.6 1.6 collective-permute-start.75
  482.2 3.5 all-to-all-start.1
  485.8 10.8 %collective-permute-done.77 = bf16[1024,384]{1,0:T(8,128)(2,1)} collective-permute-done((bf16[1024,384]{1,0:T(8,128)(2,1)}, bf16[1024,384]{1,0:T(8,128)(2,1)}, u32[]{:S(2)}, u32[]{:S(2)}) %collective-permute-start.77) | collective-permute-done | bytes 786464 | tf_op jit(solution)/shard_map/ppermute | solution.py:620
  496.6 2.7 add_add_fusion.2
  499.3 3.7 all-to-all-start.2
  503.1 3.0 collective-permute-start.78
  506.0 2.8 slice_convert_fusion.2
  509.4 6.1 %all-to-all-done.2.refs_1_ = bf16[8,128,384]{2,1,0:T(8,128)(2,1)S(1)} async-done(((bf16[8,128,384]{2,1,0:T(8,128)(2,1)}), bf16[8,128,384]{2,1,0:T(8,128)(2,1)S(1)}, u32[]{:S(2)}, u32[]{:S(2)}) %all-to-all-start.2) | async-done | bytes 786464 | tf_op jit(solution)/shard_map/all_to_all | solution.py:626
  (379 shorter events, 97.2 us)
Async XLA Ops:
  5.2 12.6 %collective-permute-start.3 = (bf16[128,512]{1,0:T(8,128)(2,1)S(1)}, bf16[128,512]{1,0:T(8,128)(2,1)S(1)}, u32[]{:S(2)}, u32[]{:S(2)}) collective-permute-start(bf16[128,512]{1,0:T(8,128)(2,1)S(1)} %bitcast.38), channel_id=1, source_target_pairs={{0,4},{4,0},{1,5},{5,1},{2,6},{6,2},{3,7},{7,3},{8,12},{12,8},{9,1... | collective-permute-start | bytes 393224 | tf_op jit(solution)/shard_map/ppermute | solution.py:171
  8.3 17.7 %collective-permute-start.7 = (bf16[128,2304]{0,1:T(8,128)(2,1)S(1)}, bf16[128,2304]{0,1:T(8,128)(2,1)}, u32[]{:S(2)}, u32[]{:S(2)}) collective-permute-start(bf16[128,2304]{0,1:T(8,128)(2,1)S(1)} %pad_maximum_fusion.15), channel_id=1, source_target_pairs={{0,4},{4,0},{1,5},{5,1},{2,6},{6,2},{3,7},{7,3},{8,12},{12,8},{9,1... | collective-permute-start | bytes 1769480 | tf_op jit(solution)/shard_map/ppermute | solution.py:171
  13.0 9.5 %collective-permute-start.4 = (bf16[256,1024]{1,0:T(8,128)(2,1)}, bf16[256,1024]{1,0:T(8,128)(2,1)S(1)}, u32[]{:S(2)}, u32[]{:S(2)}) collective-permute-start(bf16[256,1024]{1,0:T(8,128)(2,1)} %collective-permute-done.1), channel_id=1, source_target_pairs={{0,8},{8,0},{16,24},{24,16},{1,9},{9,1},{17,25},{25,17},{2,10},{10... | collective-permute-start | bytes 1572872 | tf_op jit(solution)/shard_map/ppermute | solution.py:225
  14.6 9.4 %collective-permute-start.5 = (bf16[256,1024]{1,0:T(8,128)(2,1)}, bf16[256,1024]{1,0:T(8,128)(2,1)S(1)}, u32[]{:S(2)}, u32[]{:S(2)}) collective-permute-start(bf16[256,1024]{1,0:T(8,128)(2,1)} %collective-permute-done.1), channel_id=1, source_target_pairs={{0,16},{8,24},{16,0},{24,8},{1,17},{9,25},{17,1},{25,9},{2,18},{10... | collective-permute-start | bytes 1572872 | tf_op jit(solution)/shard_map/ppermute | solution.py:225
  24.4 10.3 %collective-permute-start.6 = (bf16[256,1024]{1,0:T(8,128)(2,1)S(1)}, bf16[256,1024]{1,0:T(8,128)(2,1)S(1)}, u32[]{:S(2)}, u32[]{:S(2)}) collective-permute-start(bf16[256,1024]{1,0:T(8,128)(2,1)S(1)} %fusion.8), channel_id=1, source_target_pairs={{0,1},{1,0},{2,3},{3,2},{4,5},{5,4},{6,7},{7,6},{8,9},{9,8},{10,11... | collective-permute-start | bytes 1572872 | tf_op jit(solution)/shard_map/ppermute | solution.py:171
  27.5 26.7 %collective-permute-start.11 = (s32[1024]{0:T(1024)S(1)}, s32[1024]{0:T(1024)S(1)}, u32[]{:S(2)}, u32[]{:S(2)}) collective-permute-start(s32[1024]{0:T(1024)S(1)} %copy-done.56), channel_id=1, source_target_pairs={{0,0},{2,4},{4,2},{6,6},{1,1},{3,5},{5,3},{7,7},{8,8},{10,12},{12,... | collective-permute-start | bytes 12296 | tf_op jit(solution)/shard_map/ppermute | solution.py:167
  35.1 30.1 %collective-permute-start.8 = (bf16[512,1024]{1,0:T(8,128)(2,1)S(1)}, bf16[512,1024]{1,0:T(8,128)(2,1)S(1)}, u32[]{:S(2)}, u32[]{:S(2)}) collective-permute-start(bf16[512,1024]{1,0:T(8,128)(2,1)S(1)} %pad_maximum_fusion.8), channel_id=1, source_target_pairs={{0,4},{4,0},{1,5},{5,1},{2,6},{6,2},{3,7},{7,3},{8,12},{12,8},{9,1... | collective-permute-start | bytes 3145736 | tf_op jit(solution)/shard_map/ppermute | solution.py:171
  56.5 8.3 %collective-permute-start.9 = (bf16[128,1024]{1,0:T(8,128)(2,1)S(1)}, bf16[128,1024]{1,0:T(8,128)(2,1)S(1)}, u32[]{:S(2)}, u32[]{:S(2)}) collective-permute-start(bf16[128,1024]{1,0:T(8,128)(2,1)S(1)} %slice.115), channel_id=1, source_target_pairs={{0,8},{8,0},{16,24},{24,16},{1,9},{9,1},{17,25},{25,17},{2,10},{10... | collective-permute-start | bytes 786440 | tf_op jit(solution)/shard_map/ppermute | solution.py:225
  57.1 8.0 %collective-permute-start.10 = (bf16[128,1024]{1,0:T(8,128)(2,1)S(1)}, bf16[128,1024]{1,0:T(8,128)(2,1)S(1)}, u32[]{:S(2)}, u32[]{:S(2)}) collective-permute-start(bf16[128,1024]{1,0:T(8,128)(2,1)S(1)} %slice.116), channel_id=1, source_target_pairs={{0,16},{8,24},{16,0},{24,8},{1,17},{9,25},{17,1},{25,9},{2,18},{10... | collective-permute-start | bytes 786440 | tf_op jit(solution)/shard_map/ppermute | solution.py:225
  57.7 17.0 %collective-permute-start.12 = (bf16[256,512]{1,0:T(8,128)(2,1)S(1)}, bf16[256,512]{1,0:T(8,128)(2,1)S(1)}, u32[]{:S(2)}, u32[]{:S(2)}) collective-permute-start(bf16[256,512]{1,0:T(8,128)(2,1)S(1)} %pad_maximum_fusion.24), channel_id=1, source_target_pairs={{0,0},{2,4},{4,2},{6,6},{1,1},{3,5},{5,3},{7,7},{8,8},{10,12},{12,... | collective-permute-start | bytes 786440 | tf_op jit(solution)/shard_map/ppermute | solution.py:167
  59.8 28.4 %collective-permute-start.13 = (bf16[256,2304]{0,1:T(8,128)(2,1)S(1)}, bf16[256,2304]{0,1:T(8,128)(2,1)S(1)}, u32[]{:S(2)}, u32[]{:S(2)}) collective-permute-start(bf16[256,2304]{0,1:T(8,128)(2,1)S(1)} %pad_maximum_fusion.7), channel_id=1, source_target_pairs={{0,0},{2,4},{4,2},{6,6},{1,1},{3,5},{5,3},{7,7},{8,8},{10,12},{12,... | collective-permute-start | bytes 3538952 | tf_op jit(solution)/shard_map/ppermute | solution.py:167
  74.7 13.6 %collective-permute-start.14 = (bf16[256,512]{1,0:T(8,128)(2,1)S(1)}, bf16[256,512]{1,0:T(8,128)(2,1)S(1)}, u32[]{:S(2)}, u32[]{:S(2)}) collective-permute-start(bf16[256,512]{1,0:T(8,128)(2,1)S(1)} %collective-permute-done.12), channel_id=1, source_target_pairs={{0,8},{8,0},{16,24},{24,16},{1,9},{9,1},{17,25},{25,17},{2,10},{10... | collective-permute-start | bytes 786440 | tf_op jit(solution)/shard_map/ppermute | solution.py:225
  76.3 14.0 %collective-permute-start.15 = (bf16[256,512]{1,0:T(8,128)(2,1)S(1)}, bf16[256,512]{1,0:T(8,128)(2,1)S(1)}, u32[]{:S(2)}, u32[]{:S(2)}) collective-permute-start(bf16[256,512]{1,0:T(8,128)(2,1)S(1)} %collective-permute-done.12), channel_id=1, source_target_pairs={{0,16},{8,24},{16,0},{24,8},{1,17},{9,25},{17,1},{25,9},{2,18},{10... | collective-permute-start | bytes 786440 | tf_op jit(solution)/shard_map/ppermute | solution.py:225
  76.8 13.5 %collective-permute-start.16 = (bf16[256,512]{1,0:T(8,128)(2,1)S(1)}, bf16[256,512]{1,0:T(8,128)(2,1)S(1)}, u32[]{:S(2)}, u32[]{:S(2)}) collective-permute-start(bf16[256,512]{1,0:T(8,128)(2,1)S(1)} %collective-permute-done.12), channel_id=1, source_target_pairs={{0,24},{8,16},{16,8},{24,0},{1,25},{9,17},{17,9},{25,1},{2,26},{10... | collective-permute-start | bytes 786440 | tf_op jit(solution)/shard_map/ppermute | solution.py:225
  105.6 14.5 %collective-permute-start.18 = (bf16[256,1024]{1,0:T(8,128)(2,1)}, bf16[256,1024]{1,0:T(8,128)(2,1)}, u32[]{:S(2)}, u32[]{:S(2)}) collective-permute-start(bf16[256,1024]{1,0:T(8,128)(2,1)} %dynamic-slice_convert_fusion.1), channel_id=1, source_target_pairs={{0,1},{1,0},{2,3},{3,2},{4,5},{5,4},{6,7},{7,6},{8,9},{9,8},{10,11... | collective-permute-start | bytes 1572872 | tf_op jit(solution)/shard_map/ppermute | solution.py:171
  108.3 33.7 %collective-permute-start.23 = (bf16[256,1536]{0,1:T(8,128)(2,1)S(1)}, bf16[256,1536]{0,1:T(8,128)(2,1)S(1)}, u32[]{:S(2)}, u32[]{:S(2)}) collective-permute-start(bf16[256,1536]{0,1:T(8,128)(2,1)S(1)} %slice.121), channel_id=1, source_target_pairs={{0,8},{8,0},{16,24},{24,16},{1,9},{9,1},{17,25},{25,17},{2,10},{10... | collective-permute-start | bytes 2359304 | tf_op jit(solution)/shard_map/ppermute | solution.py:225
  109.8 32.2 %collective-permute-start.24 = (bf16[256,1536]{0,1:T(8,128)(2,1)S(1)}, bf16[256,1536]{0,1:T(8,128)(2,1)S(1)}, u32[]{:S(2)}, u32[]{:S(2)}) collective-permute-start(bf16[256,1536]{0,1:T(8,128)(2,1)S(1)} %slice.121), channel_id=1, source_target_pairs={{0,16},{8,24},{16,0},{24,8},{1,17},{9,25},{17,1},{25,9},{2,18},{10... | collective-permute-start | bytes 2359304 | tf_op jit(solution)/shard_map/ppermute | solution.py:225
  122.9 19.1 %collective-permute-start.22 = (bf16[256,1024]{1,0:T(8,128)(2,1)S(1)}, bf16[256,1024]{1,0:T(8,128)(2,1)S(1)}, u32[]{:S(2)}, u32[]{:S(2)}) collective-permute-start(bf16[256,1024]{1,0:T(8,128)(2,1)S(1)} %multiply_convert_fusion.2), channel_id=1, source_target_pairs={{0,1},{1,0},{2,3},{3,2},{4,5},{5,4},{6,7},{7,6},{8,9},{9,8},{10,11... | collective-permute-start | bytes 1572872 | tf_op jit(solution)/shard_map/ppermute | solution.py:171
  123.3 23.7 %collective-permute-start.19 = (bf16[256,1024]{1,0:T(8,128)(2,1)S(1)}, bf16[256,1024]{1,0:T(8,128)(2,1)S(1)}, u32[]{:S(2)}, u32[]{:S(2)}) collective-permute-start(bf16[256,1024]{1,0:T(8,128)(2,1)S(1)} %copy-done.55), channel_id=1, source_target_pairs={{0,0},{2,4},{4,2},{6,6},{1,1},{3,5},{5,3},{7,7},{8,8},{10,12},{12,... | collective-permute-start | bytes 1572872 | tf_op jit(solution)/shard_map/ppermute | solution.py:167
  142.0 13.6 %collective-permute-start.28 = (bf16[256,768]{0,1:T(8,128)(2,1)S(1)}, bf16[256,768]{0,1:T(8,128)(2,1)S(1)}, u32[]{:S(2)}, u32[]{:S(2)}) collective-permute-start(bf16[256,768]{0,1:T(8,128)(2,1)S(1)} %slice.119), channel_id=1, source_target_pairs={{0,8},{8,0},{16,24},{24,16},{1,9},{9,1},{17,25},{25,17},{2,10},{10... | collective-permute-start | bytes 1179656 | tf_op jit(solution)/shard_map/ppermute | solution.py:225
  143.6 12.1 %collective-permute-start.29 = (bf16[256,768]{0,1:T(8,128)(2,1)S(1)}, bf16[256,768]{0,1:T(8,128)(2,1)S(1)}, u32[]{:S(2)}, u32[]{:S(2)}) collective-permute-start(bf16[256,768]{0,1:T(8,128)(2,1)S(1)} %slice.119), channel_id=1, source_target_pairs={{0,16},{8,24},{16,0},{24,8},{1,17},{9,25},{17,1},{25,9},{2,18},{10... | collective-permute-start | bytes 1179656 | tf_op jit(solution)/shard_map/ppermute | solution.py:225
  145.9 16.4 %collective-permute-start.26 = (bf16[128,1536]{0,1:T(8,128)(2,1)S(1)}, bf16[128,1536]{0,1:T(8,128)(2,1)S(1)}, u32[]{:S(2)}, u32[]{:S(2)}) collective-permute-start(bf16[128,1536]{0,1:T(8,128)(2,1)S(1)} %slice.122), channel_id=1, source_target_pairs={{0,8},{8,0},{16,24},{24,16},{1,9},{9,1},{17,25},{25,17},{2,10},{10... | collective-permute-start | bytes 1179656 | tf_op jit(solution)/shard_map/ppermute | solution.py:225
  146.5 17.4 %collective-permute-start.27 = (bf16[128,1536]{0,1:T(8,128)(2,1)S(1)}, bf16[128,1536]{0,1:T(8,128)(2,1)S(1)}, u32[]{:S(2)}, u32[]{:S(2)}) collective-permute-start(bf16[128,1536]{0,1:T(8,128)(2,1)S(1)} %slice.123), channel_id=1, source_target_pairs={{0,16},{8,24},{16,0},{24,8},{1,17},{9,25},{17,1},{25,9},{2,18},{10... | collective-permute-start | bytes 1179656 | tf_op jit(solution)/shard_map/ppermute | solution.py:225
  147.0 21.0 %collective-permute-start.25 = (bf16[512,1024]{1,0:T(8,128)(2,1)S(1)}, bf16[512,1024]{1,0:T(8,128)(2,1)S(1)}, u32[]{:S(2)}, u32[]{:S(2)}) collective-permute-start(bf16[512,1024]{1,0:T(8,128)(2,1)S(1)} %pad_maximum_fusion.10), channel_id=1, source_target_pairs={{0,4},{4,0},{1,5},{5,1},{2,6},{6,2},{3,7},{7,3},{8,12},{12,8},{9,1... | collective-permute-start | bytes 3145736 | tf_op jit(solution)/shard_map/ppermute | solution.py:171
  155.7 9.2 %collective-permute-start.20 = (bf16[256,1024]{1,0:T(8,128)(2,1)S(1)}, bf16[256,1024]{1,0:T(8,128)(2,1)S(1)}, u32[]{:S(2)}, u32[]{:S(2)}) collective-permute-start(bf16[256,1024]{1,0:T(8,128)(2,1)S(1)} %collective-permute-done.19), channel_id=1, source_target_pairs={{0,1},{1,0},{2,3},{3,2},{4,5},{5,4},{6,7},{7,6},{8,9},{9,8},{10,11... | collective-permute-start | bytes 1572872 | tf_op jit(solution)/shard_map/ppermute | solution.py:171
  155.7 9.4 %collective-permute-start.30 = (bf16[128,768]{0,1:T(8,128)(2,1)S(1)}, bf16[128,768]{0,1:T(8,128)(2,1)S(1)}, u32[]{:S(2)}, u32[]{:S(2)}) collective-permute-start(bf16[128,768]{0,1:T(8,128)(2,1)S(1)} %slice.154), channel_id=1, source_target_pairs={{0,8},{8,0},{16,24},{24,16},{1,9},{9,1},{17,25},{25,17},{2,10},{10... | collective-permute-start | bytes 589832 | tf_op jit(solution)/shard_map/ppermute | solution.py:225
  186.3 10.3 %collective-permute-start.32 = (bf16[512,1024]{1,0:T(8,128)(2,1)}, bf16[512,1024]{1,0:T(8,128)(2,1)}, u32[]{:S(2)}, u32[]{:S(2)}) collective-permute-start(bf16[512,1024]{1,0:T(8,128)(2,1)} %dynamic_slice.171), channel_id=1, source_target_pairs={{0,4},{4,0},{1,5},{5,1},{2,6},{6,2},{3,7},{7,3},{8,12},{12,8},{9,1... | collective-permute-start | bytes 3145736 | tf_op jit(solution)/shard_map/ppermute | solution.py:171
  187.6 28.0 %collective-permute-start.37 = (bf16[128,768]{1,0:T(8,128)(2,1)S(1)}, bf16[128,768]{1,0:T(8,128)(2,1)S(1)}, u32[]{:S(2)}, u32[]{:S(2)}) collective-permute-start(bf16[128,768]{1,0:T(8,128)(2,1)S(1)} %get-tuple-element.302), channel_id=1, source_target_pairs={{0,8},{8,0},{16,24},{24,16},{1,9},{9,1},{17,25},{25,17},{2,10},{10... | collective-permute-start | bytes 589832 | tf_op jit(solution)/shard_map/ppermute | solution.py:225
  189.2 26.4 %collective-permute-start.35 = (bf16[128,768]{1,0:T(8,128)(2,1)S(1)}, bf16[128,768]{1,0:T(8,128)(2,1)S(1)}, u32[]{:S(2)}, u32[]{:S(2)}) collective-permute-start(bf16[128,768]{1,0:T(8,128)(2,1)S(1)} %get-tuple-element.303), channel_id=1, source_target_pairs={{0,16},{8,24},{16,0},{24,8},{1,17},{9,25},{17,1},{25,9},{2,18},{10... | collective-permute-start | bytes 589832 | tf_op jit(solution)/shard_map/ppermute | solution.py:225
  198.4 13.8 %collective-permute-start.33 = (bf16[256,1024]{1,0:T(8,128)(2,1)S(1)}, bf16[256,1024]{1,0:T(8,128)(2,1)S(1)}, u32[]{:S(2)}, u32[]{:S(2)}) collective-permute-start(bf16[256,1024]{1,0:T(8,128)(2,1)S(1)} %dynamic_slice.216), channel_id=1, source_target_pairs={{0,1},{1,0},{2,3},{3,2},{4,5},{5,4},{6,7},{7,6},{8,9},{9,8},{10,11... | collective-permute-start | bytes 1572872 | tf_op jit(solution)/shard_map/ppermute | solution.py:171
  214.1 12.9 %collective-permute-start.34 = (bf16[256,1024]{1,0:T(8,128)(2,1)S(1)}, bf16[256,1024]{1,0:T(8,128)(2,1)S(1)}, u32[]{:S(2)}, u32[]{:S(2)}) collective-permute-start(bf16[256,1024]{1,0:T(8,128)(2,1)S(1)} %get-tuple-element.281), channel_id=1, source_target_pairs={{0,1},{1,0},{2,3},{3,2},{4,5},{5,4},{6,7},{7,6},{8,9},{9,8},{10,11... | collective-permute-start | bytes 1572872 | tf_op jit(solution)/shard_map/ppermute | solution.py:171
  214.4 18.9 %collective-permute-start.42 = (bf16[128,1536]{1,0:T(8,128)(2,1)S(1)}, bf16[128,1536]{1,0:T(8,128)(2,1)S(1)}, u32[]{:S(2)}, u32[]{:S(2)}) collective-permute-start(bf16[128,1536]{1,0:T(8,128)(2,1)S(1)} %get-tuple-element.287), channel_id=1, source_target_pairs={{0,8},{8,0},{16,24},{24,16},{1,9},{9,1},{17,25},{25,17},{2,10},{10... | collective-permute-start | bytes 1179656 | tf_op jit(solution)/shard_map/ppermute | solution.py:225
  215.0 18.3 %collective-permute-start.40 = (bf16[128,1536]{1,0:T(8,128)(2,1)S(1)}, bf16[128,1536]{1,0:T(8,128)(2,1)S(1)}, u32[]{:S(2)}, u32[]{:S(2)}) collective-permute-start(bf16[128,1536]{1,0:T(8,128)(2,1)S(1)} %get-tuple-element.288), channel_id=1, source_target_pairs={{0,16},{8,24},{16,0},{24,8},{1,17},{9,25},{17,1},{25,9},{2,18},{10... | collective-permute-start | bytes 1179656 | tf_op jit(solution)/shard_map/ppermute | solution.py:225
  215.8 17.3 %collective-permute-start.36 = (bf16[256,768]{1,0:T(8,128)(2,1)S(1)}, bf16[256,768]{1,0:T(8,128)(2,1)S(1)}, u32[]{:S(2)}, u32[]{:S(2)}) collective-permute-start(bf16[256,768]{1,0:T(8,128)(2,1)S(1)} %pad_maximum_fusion.21), channel_id=1, source_target_pairs={{0,8},{8,0},{16,24},{24,16},{1,9},{9,1},{17,25},{25,17},{2,10},{10... | collective-permute-start | bytes 1179656 | tf_op jit(solution)/shard_map/ppermute | solution.py:225
  217.3 15.9 %collective-permute-start.38 = (bf16[256,768]{1,0:T(8,128)(2,1)S(1)}, bf16[256,768]{1,0:T(8,128)(2,1)S(1)}, u32[]{:S(2)}, u32[]{:S(2)}) collective-permute-start(bf16[256,768]{1,0:T(8,128)(2,1)S(1)} %pad_maximum_fusion.22), channel_id=1, source_target_pairs={{0,16},{8,24},{16,0},{24,8},{1,17},{9,25},{17,1},{25,9},{2,18},{10... | collective-permute-start | bytes 1179656 | tf_op jit(solution)/shard_map/ppermute | solution.py:225
  233.5 28.3 %collective-permute-start.41 = (bf16[256,1536]{1,0:T(8,128)(2,1)S(1)}, bf16[256,1536]{1,0:T(8,128)(2,1)S(1)}, u32[]{:S(2)}, u32[]{:S(2)}) collective-permute-start(bf16[256,1536]{1,0:T(8,128)(2,1)S(1)} %pad_maximum_fusion.13), channel_id=1, source_target_pairs={{0,8},{8,0},{16,24},{24,16},{1,9},{9,1},{17,25},{25,17},{2,10},{10... | collective-permute-start | bytes 2359304 | tf_op jit(solution)/shard_map/ppermute | solution.py:225
  235.2 26.7 %collective-permute-start.43 = (bf16[256,1536]{1,0:T(8,128)(2,1)S(1)}, bf16[256,1536]{1,0:T(8,128)(2,1)S(1)}, u32[]{:S(2)}, u32[]{:S(2)}) collective-permute-start(bf16[256,1536]{1,0:T(8,128)(2,1)S(1)} %pad_maximum_fusion.14), channel_id=1, source_target_pairs={{0,16},{8,24},{16,0},{24,8},{1,17},{9,25},{17,1},{25,9},{2,18},{10... | collective-permute-start | bytes 2359304 | tf_op jit(solution)/shard_map/ppermute | solution.py:225
  236.0 25.9 %collective-permute-start.44 = (bf16[256,768]{1,0:T(8,128)(2,1)S(1)}, bf16[256,768]{1,0:T(8,128)(2,1)S(1)}, u32[]{:S(2)}, u32[]{:S(2)}) collective-permute-start(bf16[256,768]{1,0:T(8,128)(2,1)S(1)} %add_convert_fusion.3), channel_id=1, source_target_pairs={{0,0},{2,4},{4,2},{6,6},{1,1},{3,5},{5,3},{7,7},{8,8},{10,12},{12,... | collective-permute-start | bytes 1179656 | tf_op jit(solution)/shard_map/ppermute | solution.py:167
  239.7 22.3 %collective-permute-start.45 = (bf16[128,512]{1,0:T(8,128)(2,1)S(1)}, bf16[128,512]{1,0:T(8,128)(2,1)S(1)}, u32[]{:S(2)}, u32[]{:S(2)}) collective-permute-start(bf16[128,512]{1,0:T(8,128)(2,1)S(1)} %get-tuple-element.311), channel_id=1, source_target_pairs={{0,16},{8,24},{16,0},{24,8},{1,17},{9,25},{17,1},{25,9},{2,18},{10... | collective-permute-start | bytes 393224 | tf_op jit(solution)/shard_map/ppermute | solution.py:225
  241.2 20.8 %collective-permute-start.46 = (bf16[128,512]{1,0:T(8,128)(2,1)S(1)}, bf16[128,512]{1,0:T(8,128)(2,1)S(1)}, u32[]{:S(2)}, u32[]{:S(2)}) collective-permute-start(bf16[128,512]{1,0:T(8,128)(2,1)S(1)} %get-tuple-element.310), channel_id=1, source_target_pairs={{0,8},{8,0},{16,24},{24,16},{1,9},{9,1},{17,25},{25,17},{2,10},{10... | collective-permute-start | bytes 393224 | tf_op jit(solution)/shard_map/ppermute | solution.py:225
  267.0 12.7 %collective-permute-start.48 = (bf16[128,1024]{1,0:T(8,128)(2,1)S(1)}, bf16[128,1024]{1,0:T(8,128)(2,1)S(1)}, u32[]{:S(2)}, u32[]{:S(2)}) collective-permute-start(bf16[128,1024]{1,0:T(8,128)(2,1)S(1)} %get-tuple-element.291), channel_id=1, source_target_pairs={{0,8},{8,0},{16,24},{24,16},{1,9},{9,1},{17,25},{25,17},{2,10},{10... | collective-permute-start | bytes 786440 | tf_op jit(solution)/shard_map/ppermute | solution.py:225
  268.3 11.3 %collective-permute-start.49 = (bf16[256,512]{1,0:T(8,128)(2,1)S(1)}, bf16[256,512]{1,0:T(8,128)(2,1)S(1)}, u32[]{:S(2)}, u32[]{:S(2)}) collective-permute-start(bf16[256,512]{1,0:T(8,128)(2,1)S(1)} %pad_maximum_fusion.25), channel_id=1, source_target_pairs={{0,8},{8,0},{16,24},{24,16},{1,9},{9,1},{17,25},{25,17},{2,10},{10... | collective-permute-start | bytes 786440 | tf_op jit(solution)/shard_map/ppermute | solution.py:225
  269.3 10.4 %collective-permute-start.50 = (bf16[256,512]{1,0:T(8,128)(2,1)S(1)}, bf16[256,512]{1,0:T(8,128)(2,1)S(1)}, u32[]{:S(2)}, u32[]{:S(2)}) collective-permute-start(bf16[256,512]{1,0:T(8,128)(2,1)S(1)} %pad_maximum_fusion.26), channel_id=1, source_target_pairs={{0,16},{8,24},{16,0},{24,8},{1,17},{9,25},{17,1},{25,9},{2,18},{10... | collective-permute-start | bytes 786440 | tf_op jit(solution)/shard_map/ppermute | solution.py:225
  270.8 31.3 %collective-permute-start.53 = (bf16[256,1536]{1,0:T(8,128)(2,1)S(1)}, bf16[256,1536]{1,0:T(8,128)(2,1)S(1)}, u32[]{:S(2)}, u32[]{:S(2)}) collective-permute-start(bf16[256,1536]{1,0:T(8,128)(2,1)S(1)} %add_convert_fusion), channel_id=1, source_target_pairs={{0,0},{2,4},{4,2},{6,6},{1,1},{3,5},{5,3},{7,7},{8,8},{10,12},{12,... | collective-permute-start | bytes 2359304 | tf_op jit(solution)/shard_map/ppermute | solution.py:167
  273.6 33.3 %collective-permute-start.57 = (bf16[512,1024]{1,0:T(8,128)(2,1)S(1)}, bf16[512,1024]{1,0:T(8,128)(2,1)S(1)}, u32[]{:S(2)}, u32[]{:S(2)}) collective-permute-start(bf16[512,1024]{1,0:T(8,128)(2,1)S(1)} %dynamic_slice.175), channel_id=1, source_target_pairs={{0,4},{4,0},{1,5},{5,1},{2,6},{6,2},{3,7},{7,3},{8,12},{12,8},{9,1... | collective-permute-start | bytes 3145736 | tf_op jit(solution)/shard_map/ppermute | solution.py:171
  279.8 22.3 %collective-permute-start.51 = (bf16[256,1024]{1,0:T(8,128)(2,1)S(1)}, bf16[256,1024]{1,0:T(8,128)(2,1)S(1)}, u32[]{:S(2)}, u32[]{:S(2)}) collective-permute-start(bf16[256,1024]{1,0:T(8,128)(2,1)S(1)} %pad_maximum_fusion.19), channel_id=1, source_target_pairs={{0,8},{8,0},{16,24},{24,16},{1,9},{9,1},{17,25},{25,17},{2,10},{10... | collective-permute-start | bytes 1572872 | tf_op jit(solution)/shard_map/ppermute | solution.py:225
  281.5 20.7 %collective-permute-start.52 = (bf16[256,1024]{1,0:T(8,128)(2,1)S(1)}, bf16[256,1024]{1,0:T(8,128)(2,1)S(1)}, u32[]{:S(2)}, u32[]{:S(2)}) collective-permute-start(bf16[256,1024]{1,0:T(8,128)(2,1)S(1)} %pad_maximum_fusion.20), channel_id=1, source_target_pairs={{0,16},{8,24},{16,0},{24,8},{1,17},{9,25},{17,1},{25,9},{2,18},{10... | collective-permute-start | bytes 1572872 | tf_op jit(solution)/shard_map/ppermute | solution.py:225
  285.6 23.1 %collective-permute-start.56 = (bf16[512,1024]{1,0:T(8,128)(2,1)S(1)}, bf16[512,1024]{1,0:T(8,128)(2,1)S(1)}, u32[]{:S(2)}, u32[]{:S(2)}) collective-permute-start(bf16[512,1024]{1,0:T(8,128)(2,1)S(1)} %constant_dynamic-slice_fusion.10), channel_id=1, source_target_pairs={{0,4},{4,0},{1,5},{5,1},{2,6},{6,2},{3,7},{7,3},{8,12},{12,8},{9,1... | collective-permute-start | bytes 3145736 | tf_op jit(solution)/shard_map/ppermute | solution.py:171
  304.5 14.2 %collective-permute-start.60 = (bf16[128,1536]{1,0:T(8,128)(2,1)S(1)}, bf16[128,1536]{1,0:T(8,128)(2,1)S(1)}, u32[]{:S(2)}, u32[]{:S(2)}) collective-permute-start(bf16[128,1536]{1,0:T(8,128)(2,1)S(1)} %constant_dynamic-slice_fusion.7), channel_id=1, source_target_pairs={{0,4},{4,0},{1,5},{5,1},{2,6},{6,2},{3,7},{7,3},{8,12},{12,8},{9,1... | collective-permute-start | bytes 1179656 | tf_op jit(solution)/shard_map/ppermute | solution.py:171
  309.2 10.6 %collective-permute-start.58 = (bf16[128,1024]{1,0:T(8,128)(2,1)S(1)}, bf16[128,1024]{1,0:T(8,128)(2,1)S(1)}, u32[]{:S(2)}, u32[]{:S(2)}) collective-permute-start(bf16[128,1024]{1,0:T(8,128)(2,1)S(1)} %constant_dynamic-slice_fusion.9), channel_id=1, source_target_pairs={{0,4},{4,0},{1,5},{5,1},{2,6},{6,2},{3,7},{7,3},{8,12},{12,8},{9,1... | collective-permute-start | bytes 786440 | tf_op jit(solution)/shard_map/ppermute | solution.py:171
  322.9 25.3 %all-to-all-start = ((bf16[8,128,768]{2,1,0:T(8,128)(2,1)}), bf16[8,128,768]{2,1,0:T(8,128)(2,1)}, u32[]{:S(2)}, u32[]{:S(2)}) async-start(bf16[8,128,768]{2,1,0:T(8,128)(2,1)} %get-tuple-element.212), calls=%async_computation | async-start | bytes 3145728 | tf_op jit(solution)/shard_map/all_to_all | solution.py:604
  327.3 14.8 %collective-permute-start.62 = (bf16[256,1024]{1,0:T(8,128)(2,1)S(1)}, bf16[256,1024]{1,0:T(8,128)(2,1)S(1)}, u32[]{:S(2)}, u32[]{:S(2)}) collective-permute-start(bf16[256,1024]{1,0:T(8,128)(2,1)S(1)} %dynamic-slice_convert_fusion), channel_id=1, source_target_pairs={{0,1},{1,0},{2,3},{3,2},{4,5},{5,4},{6,7},{7,6},{8,9},{9,8},{10,11... | collective-permute-start | bytes 1572872 | tf_op jit(solution)/shard_map/ppermute | solution.py:171
  328.7 25.9 %collective-permute-start.66 = (bf16[256,1024]{1,0:T(8,128)(2,1)S(1)}, bf16[256,1024]{1,0:T(8,128)(2,1)}, u32[]{:S(2)}, u32[]{:S(2)}) collective-permute-start(bf16[256,1024]{1,0:T(8,128)(2,1)S(1)} %dynamic_slice.215), channel_id=1, source_target_pairs={{0,1},{1,0},{2,3},{3,2},{4,5},{5,4},{6,7},{7,6},{8,9},{9,8},{10,11... | collective-permute-start | bytes 1572872 | tf_op jit(solution)/shard_map/ppermute | solution.py:171
  348.2 17.2 %collective-permute-start.63 = (bf16[1024,768]{1,0:T(8,128)(2,1)}, bf16[1024,768]{1,0:T(8,128)(2,1)}, u32[]{:S(2)}, u32[]{:S(2)}) collective-permute-start(bf16[1024,768]{1,0:T(8,128)(2,1)} %bitcast.6.refs_0_), channel_id=1, source_target_pairs={{2,1},{7,6},{10,9},{15,14},{18,17},{23,22},{31,30}} | collective-permute-start | bytes 4718600 | tf_op jit(solution)/shard_map/ppermute | solution.py:610
  350.0 15.4 %collective-permute-start.64 = (bf16[1024,768]{1,0:T(8,128)(2,1)}, bf16[1024,768]{1,0:T(8,128)(2,1)}, u32[]{:S(2)}, u32[]{:S(2)}) collective-permute-start(bf16[1024,768]{1,0:T(8,128)(2,1)} %bitcast.6.refs_0_), channel_id=1, source_target_pairs={{3,1},{4,6},{11,9},{12,14},{19,17},{20,22},{28,30}} | collective-permute-start | bytes 4718600 | tf_op jit(solution)/shard_map/ppermute | solution.py:610
  351.9 32.5 %collective-permute-start.65 = (bf16[1024,768]{1,0:T(8,128)(2,1)}, bf16[1024,768]{1,0:T(8,128)(2,1)}, u32[]{:S(2)}, u32[]{:S(2)}) collective-permute-start(bf16[1024,768]{1,0:T(8,128)(2,1)} %bitcast.6.refs_0_), channel_id=1, source_target_pairs={{0,1},{5,6},{8,9},{13,14},{16,17},{21,22},{29,30}} | collective-permute-start | bytes 4718600 | tf_op jit(solution)/shard_map/ppermute | solution.py:610
  392.5 87.1 %collective-permute-start.74 = (bf16[1024,384]{1,0:T(8,128)(2,1)S(1)}, bf16[1024,384]{1,0:T(8,128)(2,1)S(1)}, u32[]{:S(2)}, u32[]{:S(2)}) collective-permute-start(bf16[1024,384]{1,0:T(8,128)(2,1)S(1)} %get-tuple-element.252), channel_id=1, source_target_pairs={{1,0},{6,5},{9,8},{14,13},{17,16},{22,21},{30,29}} | collective-permute-start | bytes 2359304 | tf_op jit(solution)/shard_map/ppermute | solution.py:620
  393.8 87.4 %collective-permute-start.73 = (bf16[1024,384]{1,0:T(8,128)(2,1)S(1)}, bf16[1024,384]{1,0:T(8,128)(2,1)S(1)}, u32[]{:S(2)}, u32[]{:S(2)}) collective-permute-start(bf16[1024,384]{1,0:T(8,128)(2,1)S(1)} %get-tuple-element.251), channel_id=1, source_target_pairs={{1,3},{6,4},{9,11},{14,12},{17,19},{22,20},{30,28}} | collective-permute-start | bytes 2359304 | tf_op jit(solution)/shard_map/ppermute | solution.py:620
  394.5 86.7 %collective-permute-start.72 = (bf16[1024,384]{1,0:T(8,128)(2,1)S(1)}, bf16[1024,384]{1,0:T(8,128)(2,1)S(1)}, u32[]{:S(2)}, u32[]{:S(2)}) collective-permute-start(bf16[1024,384]{1,0:T(8,128)(2,1)S(1)} %get-tuple-element.250), channel_id=1, source_target_pairs={{1,2},{6,7},{9,10},{14,15},{17,18},{22,23},{30,31}} | collective-permute-start | bytes 2359304 | tf_op jit(solution)/shard_map/ppermute | solution.py:620
  395.2 101.4 %collective-permute-start.77 = (bf16[1024,384]{1,0:T(8,128)(2,1)}, bf16[1024,384]{1,0:T(8,128)(2,1)}, u32[]{:S(2)}, u32[]{:S(2)}) collective-permute-start(bf16[1024,384]{1,0:T(8,128)(2,1)} %get-tuple-element.256), channel_id=1, source_target_pairs={{1,0},{6,5},{9,8},{14,13},{17,16},{22,21},{30,29}} | collective-permute-start | bytes 2359304 | tf_op jit(solution)/shard_map/ppermute | solution.py:620
  396.5 100.1 %collective-permute-start.76 = (bf16[1024,384]{1,0:T(8,128)(2,1)S(1)}, bf16[1024,384]{1,0:T(8,128)(2,1)}, u32[]{:S(2)}, u32[]{:S(2)}) collective-permute-start(bf16[1024,384]{1,0:T(8,128)(2,1)S(1)} %get-tuple-element.255), channel_id=1, source_target_pairs={{1,3},{6,4},{9,11},{14,12},{17,19},{22,20},{30,28}} | collective-permute-start | bytes 2359304 | tf_op jit(solution)/shard_map/ppermute | solution.py:620
  479.6 17.0 %collective-permute-start.75 = (bf16[1024,384]{1,0:T(8,128)(2,1)S(1)}, bf16[1024,384]{1,0:T(8,128)(2,1)}, u32[]{:S(2)}, u32[]{:S(2)}) collective-permute-start(bf16[1024,384]{1,0:T(8,128)(2,1)S(1)} %get-tuple-element.254), channel_id=1, source_target_pairs={{1,2},{6,7},{9,10},{14,15},{17,18},{22,23},{30,31}} | collective-permute-start | bytes 2359304 | tf_op jit(solution)/shard_map/ppermute | solution.py:620
  482.2 17.0 %all-to-all-start.1 = ((bf16[8,128,384]{2,1,0:T(8,128)(2,1)}), bf16[8,128,384]{2,1,0:T(8,128)(2,1)S(1)}, u32[]{:S(2)}, u32[]{:S(2)}) async-start(bf16[8,128,384]{2,1,0:T(8,128)(2,1)} %bitcast.37), calls=%async_computation.1 | async-start | bytes 1572864 | tf_op jit(solution)/shard_map/all_to_all | solution.py:626
  499.3 16.2 %all-to-all-start.2 = ((bf16[8,128,384]{2,1,0:T(8,128)(2,1)}), bf16[8,128,384]{2,1,0:T(8,128)(2,1)S(1)}, u32[]{:S(2)}, u32[]{:S(2)}) async-start(bf16[8,128,384]{2,1,0:T(8,128)(2,1)} %bitcast.36), calls=%async_computation.2 | async-start | bytes 1572864 | tf_op jit(solution)/shard_map/all_to_all | solution.py:626
  (78 other events, 691.5 us)

commit v4 on v3

--- a/solution.py
+++ b/solution.py
@@ -759,7 +759,7 @@
     heads_near = gather_plane_near(heads_held)
     out_pair = both_cores(out_local)
     mlp_pair = both_cores(mlp_local)
-    hidden_in, out_pair, heads_near = tied(hidden_in, out_pair, heads_near)
+    hidden_in, positions, out_pair, heads_near = tied(hidden_in, positions, out_pair, heads_near)
     heads_full = gather_plane_far(heads_near)
     out_held = swap(out_pair)
     gain_attn = gains[:MODEL_WIDTH]

time: 523 us -> 516 us (0.987)
  waiting for transfers between devices: 237 us -> 231 us
where the time goes in v4:
time: 516 us; the launch traced here: 511 us
  waiting for transfers between devices  231 us (45%)
  starting transfers between devices  145 us (28%)
  Pallas kernels  45.4 us (9%)
  other arithmetic  34.3 us (7%)
  matrix products  30.5 us (6%)
  local copies, waits for them, and re-layouts  22.2 us (4%)
    ppermute x6, waiting for transfers between devices, from_homes(): received = received + lax.ppermute(back[step], DP + TENSOR, pairs)  92.3 us
    ppermute x23, waiting for transfers between devices, to_partner(): return lax.ppermute(values, name, [(0, 1), (1, 0)])  69.7 us
    ppermute x23, starting transfers between devices, to_partner(): return lax.ppermute(values, name, [(0, 1), (1, 0)])  66.5 us
    pallas_call x5, Pallas kernels, in_vmem(): pl.pallas_call(kernel, out_shape=results, in_specs=[pl.BlockSpec(memory_s...  41.1 us
    ppermute x31, starting transfers between devices, exchange(): lax.ppermute(values, 'pl', [(index, index ^ stride) for index in range(co...  36.7 us
    ppermute x31, waiting for transfers between devices, exchange(): lax.ppermute(values, 'pl', [(index, index ^ stride) for index in range(co...  31.5 us
    ppermute x3, waiting for transfers between devices, to_homes(): lax.ppermute(owned, DP + TENSOR, toward_home(group, homes, step))  19 us
    dot_general x4, matrix products, contract_rows(): lax.dot_general(left, right, (((0,), (0,)), ((), ())), preferred_element_...  14.4 us
  transfers between devices with their start and end apart: 82, of which 29 were waited for; matrix products, arithmetic and copies ran while one was open for 11% of the time, Pallas kernels for 8%

profile of v4, /device:TPU:0, one launch (start us, length us, event | category | flops | bytes accessed | tf_op | source)
XLA Modules:
  0.0 510.6 jit_solution(11080098671535982513)
XLA Ops:
  8.3 4.7 collective-permute-start.8
  16.1 1.7 collective-permute-start.2
  18.6 3.9 collective-permute-done.5
  24.4 1.6 collective-permute-start.7
  28.1 1.6 collective-permute-start.11
  31.7 2.9 collective-permute-done.7
  35.0 20.4 %collective-permute-start.9 = (bf16[512,1024]{1,0:T(8,128)(2,1)S(1)}, bf16[512,1024]{1,0:T(8,128)(2,1)S(1)}, u32[]{:S(2)}, u32[]{:S(2)}) collective-permute-start(bf16[512,1024]{1,0:T(8,128)(2,1)S(1)} %pad_maximum_fusion.8), channel_id=1, source_target_pairs={{0,4},{4,0},{1,5},{5,1},{2,6},{6,2},{3,7},{7,3},{8,12},{12,8},{9,1... | collective-permute-start | bytes 3145736 | tf_op jit(solution)/shard_map/ppermute | solution.py:171
  55.5 1.9 fusion.15
  61.5 6.9 %shard_map.395 = (bf16[1024,512]{1,0:T(8,128)(2,1)S(1)}, bf16[1024,256]{1,0:T(8,128)(2,1)S(1)}, bf16[1024,256]{1,0:T(8,128)(2,1)S(1)}, f32[1024,768]{1,0:T(8,128)}) custom-call(bf16[1024,1024]{1,0:T(8,128)(2,1)S(1)} %pad_maximum_fusion.1.rows_ref, bf16[1024,1024]{1,0:T(8,128)(2,1)} %copy-done.37, f32[1024,128]{1,0:T(8,128)S(1)} %get-tuple-element.334.cosine_ref, ...), custom_call_target="tpu_custom_call" | custom-call | flops 2147483648 | bytes 10486784 | tf_op jit(solution)/shard_map/pallas_call | solution.py:512
  71.9 9.9 %shard_map.396 = (bf16[1024,512]{1,0:T(8,128)(2,1)S(1)}, f32[4,1024]{1,0:T(4,128)S(1)}) custom-call(bf16[1024,512]{1,0:T(8,128)(2,1)S(1)} %get-tuple-element.162.query_ref, bf16[1024,256]{1,0:T(8,128)(2,1)S(1)} %get-tuple-element.163.key_ref, bf16[1024,256]{1,0:T(8,128)(2,1)S(1)} %get-tuple-element.164.value_ref, s32[1,1024]{1,0:T(1,128)S(1)} %bitcast.32), custom_call_target="tpu_custom_call" | custom-call | flops 2147483648 | bytes 3166208 | tf_op jit(solution)/shard_map/pallas_call | solution.py:512
  82.0 1.8 collective-permute-done.15
  86.9 5.1 collective-permute-start.17
  92.0 2.6 collective-permute-done.17
  94.6 3.3 convert_add_fusion.3
  97.9 2.1 dynamic-slice_convert_fusion.1
  104.9 9.7 %collective-permute-done.18 = bf16[256,1024]{1,0:T(8,128)(2,1)} collective-permute-done((bf16[256,1024]{1,0:T(8,128)(2,1)}, bf16[256,1024]{1,0:T(8,128)(2,1)}, u32[]{:S(2)}, u32[]{:S(2)}) %collective-permute-start.18) | collective-permute-done | bytes 524320 | tf_op jit(solution)/shard_map/ppermute | solution.py:171
  114.5 1.6 convert_add_fusion.4
  118.6 17.7 %collective-permute-done.22 = bf16[256,1024]{1,0:T(8,128)(2,1)S(1)} collective-permute-done((bf16[256,1024]{1,0:T(8,128)(2,1)S(1)}, bf16[256,1024]{1,0:T(8,128)(2,1)S(1)}, u32[]{:S(2)}, u32[]{:S(2)}) %collective-permute-start.22) | collective-permute-done | bytes 524320 | tf_op jit(solution)/shard_map/ppermute | solution.py:171
  141.8 7.7 %collective-permute-done.29 = bf16[256,768]{0,1:T(8,128)(2,1)S(1)} collective-permute-done((bf16[256,768]{0,1:T(8,128)(2,1)S(1)}, bf16[256,768]{0,1:T(8,128)(2,1)S(1)}, u32[]{:S(2)}, u32[]{:S(2)}) %collective-permute-start.29) | collective-permute-done | bytes 393248 | tf_op jit(solution)/shard_map/ppermute | solution.py:225
  150.8 5.9 %collective-permute-done.26 = bf16[128,1536]{0,1:T(8,128)(2,1)S(1)} collective-permute-done((bf16[128,1536]{0,1:T(8,128)(2,1)S(1)}, bf16[128,1536]{0,1:T(8,128)(2,1)S(1)}, u32[]{:S(2)}, u32[]{:S(2)}) %collective-permute-start.26) | collective-permute-done | bytes 393248 | tf_op jit(solution)/shard_map/ppermute | solution.py:225
  159.0 3.4 collective-permute-done.31
  162.5 3.5 fusion.26
  168.1 3.1 convolution_convert_fusion.5
  171.2 3.5 fusion.2
  174.7 3.6 fusion.5
  184.5 6.0 %convolution_convert_fusion = bf16[1024,1536]{1,0:T(8,128)(2,1)S(1)} fusion(bf16[1024,1024]{1,0:T(8,128)(2,1)} %copy-done.48, bf16[1024,768]{1,0:T(8,128)(2,1)} %copy-done.58, bf16[1024,768]{1,0:T(8,128)(2,1)} %copy-done.57), kind=kOutput, calls=%fused_computation.1 | convolution fusion | flops 3229089792 | bytes 8388608 | tf_op jit(solution)/shard_map/dot_general | solution.py:45
  190.6 1.6 convert_add_fusion.2
  192.5 13.6 %collective-permute-done.33 = bf16[256,1024]{1,0:T(8,128)(2,1)S(1)} collective-permute-done((bf16[256,1024]{1,0:T(8,128)(2,1)S(1)}, bf16[256,1024]{1,0:T(8,128)(2,1)S(1)}, u32[]{:S(2)}, u32[]{:S(2)}) %collective-permute-start.33) | collective-permute-done | bytes 524320 | tf_op jit(solution)/shard_map/ppermute | solution.py:171
  212.7 8.2 %collective-permute-done.34 = bf16[256,1024]{1,0:T(8,128)(2,1)S(1)} collective-permute-done((bf16[256,1024]{1,0:T(8,128)(2,1)S(1)}, bf16[256,1024]{1,0:T(8,128)(2,1)S(1)}, u32[]{:S(2)}, u32[]{:S(2)}) %collective-permute-start.34) | collective-permute-done | bytes 524320 | tf_op jit(solution)/shard_map/ppermute | solution.py:171
  221.0 5.9 %collective-permute-done.36 = bf16[256,768]{1,0:T(8,128)(2,1)S(1)} collective-permute-done((bf16[256,768]{1,0:T(8,128)(2,1)S(1)}, bf16[256,768]{1,0:T(8,128)(2,1)S(1)}, u32[]{:S(2)}, u32[]{:S(2)}) %collective-permute-start.36) | collective-permute-done | bytes 393248 | tf_op jit(solution)/shard_map/ppermute | solution.py:225
  227.4 1.6 collective-permute-start.41
  235.6 20.1 %shard_map.397 = (bf16[1024,1024]{1,0:T(8,128)(2,1)}, f32[2,128]{1,0:T(2,128)S(1)}) custom-call(bf16[1024,1024]{1,0:T(8,128)(2,1)} %pad_maximum_fusion.2.state_ref, bf16[1024,512]{1,0:T(8,128)(2,1)S(1)} %constant_dynamic-update-slice_fusion.10.out_ref, bf16[1024,512]{1,0:T(8,128)(2,1)S(1)} %get-tuple-element.162.query_ref, bf16[1024,256]{1,0:T(8,128)(2,1)S(1)} %copy-done.17, ...), custom_call_target="tpu_custom_call" | custom-call | flops 6442450944 | bytes 11556864 | tf_op jit(solution)/shard_map/pallas_call | solution.py:512
  255.8 4.1 convolution_convert_fusion.2
  265.4 1.8 convolution_convert_fusion.4
  267.5 5.1 collective-permute-start.57
  273.8 1.8 collective-permute-start.51
  275.8 2.3 collective-permute-start.52
  278.9 2.4 convolution_convert_fusion.1
  281.4 13.7 %collective-permute-start.56 = (bf16[512,1024]{1,0:T(8,128)(2,1)S(1)}, bf16[512,1024]{1,0:T(8,128)(2,1)S(1)}, u32[]{:S(2)}, u32[]{:S(2)}) collective-permute-start(bf16[512,1024]{1,0:T(8,128)(2,1)S(1)} %constant_dynamic-slice_fusion.10), channel_id=1, source_target_pairs={{0,4},{4,0},{1,5},{5,1},{2,6},{6,2},{3,7},{7,3},{8,12},{12,8},{9,1... | collective-permute-start | bytes 3145736 | tf_op jit(solution)/shard_map/ppermute | solution.py:171
  299.9 1.7 convert_add_fusion
  302.2 10.2 %collective-permute-start.58 = (bf16[128,1024]{1,0:T(8,128)(2,1)S(1)}, bf16[128,1024]{1,0:T(8,128)(2,1)S(1)}, u32[]{:S(2)}, u32[]{:S(2)}) collective-permute-start(bf16[128,1024]{1,0:T(8,128)(2,1)S(1)} %constant_dynamic-slice_fusion.9), channel_id=1, source_target_pairs={{0,4},{4,0},{1,5},{5,1},{2,6},{6,2},{3,7},{7,3},{8,12},{12,8},{9,1... | collective-permute-start | bytes 786440 | tf_op jit(solution)/shard_map/ppermute | solution.py:171
  313.7 2.9 shard_map.398
  316.6 4.3 all-to-all-start
  322.4 2.0 collective-permute-start.66
  324.4 11.3 %collective-permute-done.62 = bf16[256,1024]{1,0:T(8,128)(2,1)S(1)} collective-permute-done((bf16[256,1024]{1,0:T(8,128)(2,1)S(1)}, bf16[256,1024]{1,0:T(8,128)(2,1)S(1)}, u32[]{:S(2)}, u32[]{:S(2)}) %collective-permute-start.62) | collective-permute-done | bytes 524320 | tf_op jit(solution)/shard_map/ppermute | solution.py:171
  337.2 4.7 all-to-all-done
  341.9 1.8 collective-permute-start.63
  343.7 1.9 collective-permute-start.64
  345.6 2.7 collective-permute-start.65
  348.4 1.7 add_convert_fusion.1
  352.6 2.9 collective-permute-done.68
  356.1 3.1 collective-permute-done.69
  359.1 19.0 %collective-permute-done.65.refs_3_ = bf16[1024,768]{1,0:T(8,128)(2,1)} collective-permute-done((bf16[1024,768]{1,0:T(8,128)(2,1)}, bf16[1024,768]{1,0:T(8,128)(2,1)}, u32[]{:S(2)}, u32[]{:S(2)}) %collective-permute-start.65) | collective-permute-done | bytes 1572896 | tf_op jit(solution)/shard_map/ppermute | solution.py:610
  378.1 2.5 collective-permute-start.70
  380.6 4.3 shard_map.399
  389.7 1.6 collective-permute-start.76
  391.2 81.5 %collective-permute-done.74 = bf16[1024,384]{1,0:T(8,128)(2,1)S(1)} collective-permute-done((bf16[1024,384]{1,0:T(8,128)(2,1)S(1)}, bf16[1024,384]{1,0:T(8,128)(2,1)S(1)}, u32[]{:S(2)}, u32[]{:S(2)}) %collective-permute-start.74) | collective-permute-done | bytes 786464 | tf_op jit(solution)/shard_map/ppermute | solution.py:620
  475.4 3.5 all-to-all-start.1
  478.9 10.8 %collective-permute-done.77 = bf16[1024,384]{1,0:T(8,128)(2,1)} collective-permute-done((bf16[1024,384]{1,0:T(8,128)(2,1)}, bf16[1024,384]{1,0:T(8,128)(2,1)}, u32[]{:S(2)}, u32[]{:S(2)}) %collective-permute-start.77) | collective-permute-done | bytes 786464 | tf_op jit(solution)/shard_map/ppermute | solution.py:620
  489.7 2.7 add_add_fusion.2
  492.5 3.7 all-to-all-start.2
  496.2 3.0 collective-permute-start.78
  499.2 2.8 slice_convert_fusion.2
  502.6 6.1 %all-to-all-done.2.refs_1_ = bf16[8,128,384]{2,1,0:T(8,128)(2,1)S(1)} async-done(((bf16[8,128,384]{2,1,0:T(8,128)(2,1)}), bf16[8,128,384]{2,1,0:T(8,128)(2,1)S(1)}, u32[]{:S(2)}, u32[]{:S(2)}) %all-to-all-start.2) | async-done | bytes 786464 | tf_op jit(solution)/shard_map/all_to_all | solution.py:626
  (379 shorter events, 96.9 us)
Async XLA Ops:
  5.2 12.7 %collective-permute-start.4 = (bf16[128,512]{1,0:T(8,128)(2,1)S(1)}, bf16[128,512]{1,0:T(8,128)(2,1)S(1)}, u32[]{:S(2)}, u32[]{:S(2)}) collective-permute-start(bf16[128,512]{1,0:T(8,128)(2,1)S(1)} %bitcast.38), channel_id=1, source_target_pairs={{0,4},{4,0},{1,5},{5,1},{2,6},{6,2},{3,7},{7,3},{8,12},{12,8},{9,1... | collective-permute-start | bytes 393224 | tf_op jit(solution)/shard_map/ppermute | solution.py:171
  8.3 17.7 %collective-permute-start.8 = (bf16[128,2304]{0,1:T(8,128)(2,1)S(1)}, bf16[128,2304]{0,1:T(8,128)(2,1)}, u32[]{:S(2)}, u32[]{:S(2)}) collective-permute-start(bf16[128,2304]{0,1:T(8,128)(2,1)S(1)} %pad_maximum_fusion.15), channel_id=1, source_target_pairs={{0,4},{4,0},{1,5},{5,1},{2,6},{6,2},{3,7},{7,3},{8,12},{12,8},{9,1... | collective-permute-start | bytes 1769480 | tf_op jit(solution)/shard_map/ppermute | solution.py:171
  13.0 9.5 %collective-permute-start.5 = (bf16[256,1024]{1,0:T(8,128)(2,1)}, bf16[256,1024]{1,0:T(8,128)(2,1)S(1)}, u32[]{:S(2)}, u32[]{:S(2)}) collective-permute-start(bf16[256,1024]{1,0:T(8,128)(2,1)} %collective-permute-done.1), channel_id=1, source_target_pairs={{0,8},{8,0},{16,24},{24,16},{1,9},{9,1},{17,25},{25,17},{2,10},{10... | collective-permute-start | bytes 1572872 | tf_op jit(solution)/shard_map/ppermute | solution.py:225
  14.6 9.4 %collective-permute-start.6 = (bf16[256,1024]{1,0:T(8,128)(2,1)}, bf16[256,1024]{1,0:T(8,128)(2,1)S(1)}, u32[]{:S(2)}, u32[]{:S(2)}) collective-permute-start(bf16[256,1024]{1,0:T(8,128)(2,1)} %collective-permute-done.1), channel_id=1, source_target_pairs={{0,16},{8,24},{16,0},{24,8},{1,17},{9,25},{17,1},{25,9},{2,18},{10... | collective-permute-start | bytes 1572872 | tf_op jit(solution)/shard_map/ppermute | solution.py:225
  24.4 10.2 %collective-permute-start.7 = (bf16[256,1024]{1,0:T(8,128)(2,1)S(1)}, bf16[256,1024]{1,0:T(8,128)(2,1)S(1)}, u32[]{:S(2)}, u32[]{:S(2)}) collective-permute-start(bf16[256,1024]{1,0:T(8,128)(2,1)S(1)} %fusion.8), channel_id=1, source_target_pairs={{0,1},{1,0},{2,3},{3,2},{4,5},{5,4},{6,7},{7,6},{8,9},{9,8},{10,11... | collective-permute-start | bytes 1572872 | tf_op jit(solution)/shard_map/ppermute | solution.py:171
  27.5 31.2 %collective-permute-start.10 = (bf16[128,1024]{1,0:T(8,128)(2,1)S(1)}, bf16[128,1024]{1,0:T(8,128)(2,1)S(1)}, u32[]{:S(2)}, u32[]{:S(2)}) collective-permute-start(bf16[128,1024]{1,0:T(8,128)(2,1)S(1)} %slice.115), channel_id=1, source_target_pairs={{0,8},{8,0},{16,24},{24,16},{1,9},{9,1},{17,25},{25,17},{2,10},{10... | collective-permute-start | bytes 786440 | tf_op jit(solution)/shard_map/ppermute | solution.py:225
  28.1 30.6 %collective-permute-start.11 = (bf16[128,1024]{1,0:T(8,128)(2,1)S(1)}, bf16[128,1024]{1,0:T(8,128)(2,1)S(1)}, u32[]{:S(2)}, u32[]{:S(2)}) collective-permute-start(bf16[128,1024]{1,0:T(8,128)(2,1)S(1)} %slice.116), channel_id=1, source_target_pairs={{0,16},{8,24},{16,0},{24,8},{1,17},{9,25},{17,1},{25,9},{2,18},{10... | collective-permute-start | bytes 786440 | tf_op jit(solution)/shard_map/ppermute | solution.py:225
  29.7 38.7 %collective-permute-start.12 = (bf16[256,512]{1,0:T(8,128)(2,1)S(1)}, bf16[256,512]{1,0:T(8,128)(2,1)S(1)}, u32[]{:S(2)}, u32[]{:S(2)}) collective-permute-start(bf16[256,512]{1,0:T(8,128)(2,1)S(1)} %pad_maximum_fusion.24), channel_id=1, source_target_pairs={{0,0},{2,4},{4,2},{6,6},{1,1},{3,5},{5,3},{7,7},{8,8},{10,12},{12,... | collective-permute-start | bytes 786440 | tf_op jit(solution)/shard_map/ppermute | solution.py:167
  35.0 23.8 %collective-permute-start.9 = (bf16[512,1024]{1,0:T(8,128)(2,1)S(1)}, bf16[512,1024]{1,0:T(8,128)(2,1)S(1)}, u32[]{:S(2)}, u32[]{:S(2)}) collective-permute-start(bf16[512,1024]{1,0:T(8,128)(2,1)S(1)} %pad_maximum_fusion.8), channel_id=1, source_target_pairs={{0,4},{4,0},{1,5},{5,1},{2,6},{6,2},{3,7},{7,3},{8,12},{12,8},{9,1... | collective-permute-start | bytes 3145736 | tf_op jit(solution)/shard_map/ppermute | solution.py:171
  57.8 24.1 %collective-permute-start.13 = (bf16[256,2304]{0,1:T(8,128)(2,1)S(1)}, bf16[256,2304]{0,1:T(8,128)(2,1)S(1)}, u32[]{:S(2)}, u32[]{:S(2)}) collective-permute-start(bf16[256,2304]{0,1:T(8,128)(2,1)S(1)} %pad_maximum_fusion.7), channel_id=1, source_target_pairs={{0,0},{2,4},{4,2},{6,6},{1,1},{3,5},{5,3},{7,7},{8,8},{10,12},{12,... | collective-permute-start | bytes 3538952 | tf_op jit(solution)/shard_map/ppermute | solution.py:167
  68.3 13.6 %collective-permute-start.14 = (bf16[256,512]{1,0:T(8,128)(2,1)S(1)}, bf16[256,512]{1,0:T(8,128)(2,1)S(1)}, u32[]{:S(2)}, u32[]{:S(2)}) collective-permute-start(bf16[256,512]{1,0:T(8,128)(2,1)S(1)} %collective-permute-done.12), channel_id=1, source_target_pairs={{0,8},{8,0},{16,24},{24,16},{1,9},{9,1},{17,25},{25,17},{2,10},{10... | collective-permute-start | bytes 786440 | tf_op jit(solution)/shard_map/ppermute | solution.py:225
  69.9 13.8 %collective-permute-start.15 = (bf16[256,512]{1,0:T(8,128)(2,1)S(1)}, bf16[256,512]{1,0:T(8,128)(2,1)S(1)}, u32[]{:S(2)}, u32[]{:S(2)}) collective-permute-start(bf16[256,512]{1,0:T(8,128)(2,1)S(1)} %collective-permute-done.12), channel_id=1, source_target_pairs={{0,16},{8,24},{16,0},{24,8},{1,17},{9,25},{17,1},{25,9},{2,18},{10... | collective-permute-start | bytes 786440 | tf_op jit(solution)/shard_map/ppermute | solution.py:225
  71.4 12.5 %collective-permute-start.16 = (bf16[256,512]{1,0:T(8,128)(2,1)S(1)}, bf16[256,512]{1,0:T(8,128)(2,1)S(1)}, u32[]{:S(2)}, u32[]{:S(2)}) collective-permute-start(bf16[256,512]{1,0:T(8,128)(2,1)S(1)} %collective-permute-done.12), channel_id=1, source_target_pairs={{0,24},{8,16},{16,8},{24,0},{1,25},{9,17},{17,9},{25,1},{2,26},{10... | collective-permute-start | bytes 786440 | tf_op jit(solution)/shard_map/ppermute | solution.py:225
  100.0 14.5 %collective-permute-start.18 = (bf16[256,1024]{1,0:T(8,128)(2,1)}, bf16[256,1024]{1,0:T(8,128)(2,1)}, u32[]{:S(2)}, u32[]{:S(2)}) collective-permute-start(bf16[256,1024]{1,0:T(8,128)(2,1)} %dynamic-slice_convert_fusion.1), channel_id=1, source_target_pairs={{0,1},{1,0},{2,3},{3,2},{4,5},{5,4},{6,7},{7,6},{8,9},{9,8},{10,11... | collective-permute-start | bytes 1572872 | tf_op jit(solution)/shard_map/ppermute | solution.py:171
  102.7 33.8 %collective-permute-start.23 = (bf16[256,1536]{0,1:T(8,128)(2,1)S(1)}, bf16[256,1536]{0,1:T(8,128)(2,1)S(1)}, u32[]{:S(2)}, u32[]{:S(2)}) collective-permute-start(bf16[256,1536]{0,1:T(8,128)(2,1)S(1)} %slice.121), channel_id=1, source_target_pairs={{0,8},{8,0},{16,24},{24,16},{1,9},{9,1},{17,25},{25,17},{2,10},{10... | collective-permute-start | bytes 2359304 | tf_op jit(solution)/shard_map/ppermute | solution.py:225
  103.3 33.1 %collective-permute-start.24 = (bf16[256,1536]{0,1:T(8,128)(2,1)S(1)}, bf16[256,1536]{0,1:T(8,128)(2,1)S(1)}, u32[]{:S(2)}, u32[]{:S(2)}) collective-permute-start(bf16[256,1536]{0,1:T(8,128)(2,1)S(1)} %slice.121), channel_id=1, source_target_pairs={{0,16},{8,24},{16,0},{24,8},{1,17},{9,25},{17,1},{25,9},{2,18},{10... | collective-permute-start | bytes 2359304 | tf_op jit(solution)/shard_map/ppermute | solution.py:225
  117.3 19.1 %collective-permute-start.22 = (bf16[256,1024]{1,0:T(8,128)(2,1)S(1)}, bf16[256,1024]{1,0:T(8,128)(2,1)S(1)}, u32[]{:S(2)}, u32[]{:S(2)}) collective-permute-start(bf16[256,1024]{1,0:T(8,128)(2,1)S(1)} %multiply_convert_fusion.2), channel_id=1, source_target_pairs={{0,1},{1,0},{2,3},{3,2},{4,5},{5,4},{6,7},{7,6},{8,9},{9,8},{10,11... | collective-permute-start | bytes 1572872 | tf_op jit(solution)/shard_map/ppermute | solution.py:171
  117.7 23.7 %collective-permute-start.19 = (bf16[256,1024]{1,0:T(8,128)(2,1)S(1)}, bf16[256,1024]{1,0:T(8,128)(2,1)S(1)}, u32[]{:S(2)}, u32[]{:S(2)}) collective-permute-start(bf16[256,1024]{1,0:T(8,128)(2,1)S(1)} %copy-done.55), channel_id=1, source_target_pairs={{0,0},{2,4},{4,2},{6,6},{1,1},{3,5},{5,3},{7,7},{8,8},{10,12},{12,... | collective-permute-start | bytes 1572872 | tf_op jit(solution)/shard_map/ppermute | solution.py:167
  136.4 13.1 %collective-permute-start.28 = (bf16[256,768]{0,1:T(8,128)(2,1)S(1)}, bf16[256,768]{0,1:T(8,128)(2,1)S(1)}, u32[]{:S(2)}, u32[]{:S(2)}) collective-permute-start(bf16[256,768]{0,1:T(8,128)(2,1)S(1)} %slice.119), channel_id=1, source_target_pairs={{0,8},{8,0},{16,24},{24,16},{1,9},{9,1},{17,25},{25,17},{2,10},{10... | collective-permute-start | bytes 1179656 | tf_op jit(solution)/shard_map/ppermute | solution.py:225
  137.5 12.1 %collective-permute-start.29 = (bf16[256,768]{0,1:T(8,128)(2,1)S(1)}, bf16[256,768]{0,1:T(8,128)(2,1)S(1)}, u32[]{:S(2)}, u32[]{:S(2)}) collective-permute-start(bf16[256,768]{0,1:T(8,128)(2,1)S(1)} %slice.119), channel_id=1, source_target_pairs={{0,16},{8,24},{16,0},{24,8},{1,17},{9,25},{17,1},{25,9},{2,18},{10... | collective-permute-start | bytes 1179656 | tf_op jit(solution)/shard_map/ppermute | solution.py:225
  139.8 16.9 %collective-permute-start.26 = (bf16[128,1536]{0,1:T(8,128)(2,1)S(1)}, bf16[128,1536]{0,1:T(8,128)(2,1)S(1)}, u32[]{:S(2)}, u32[]{:S(2)}) collective-permute-start(bf16[128,1536]{0,1:T(8,128)(2,1)S(1)} %slice.122), channel_id=1, source_target_pairs={{0,8},{8,0},{16,24},{24,16},{1,9},{9,1},{17,25},{25,17},{2,10},{10... | collective-permute-start | bytes 1179656 | tf_op jit(solution)/shard_map/ppermute | solution.py:225
  140.4 17.4 %collective-permute-start.27 = (bf16[128,1536]{0,1:T(8,128)(2,1)S(1)}, bf16[128,1536]{0,1:T(8,128)(2,1)S(1)}, u32[]{:S(2)}, u32[]{:S(2)}) collective-permute-start(bf16[128,1536]{0,1:T(8,128)(2,1)S(1)} %slice.123), channel_id=1, source_target_pairs={{0,16},{8,24},{16,0},{24,8},{1,17},{9,25},{17,1},{25,9},{2,18},{10... | collective-permute-start | bytes 1179656 | tf_op jit(solution)/shard_map/ppermute | solution.py:225
  141.4 21.0 %collective-permute-start.25 = (bf16[512,1024]{1,0:T(8,128)(2,1)S(1)}, bf16[512,1024]{1,0:T(8,128)(2,1)S(1)}, u32[]{:S(2)}, u32[]{:S(2)}) collective-permute-start(bf16[512,1024]{1,0:T(8,128)(2,1)S(1)} %pad_maximum_fusion.10), channel_id=1, source_target_pairs={{0,4},{4,0},{1,5},{5,1},{2,6},{6,2},{3,7},{7,3},{8,12},{12,8},{9,1... | collective-permute-start | bytes 3145736 | tf_op jit(solution)/shard_map/ppermute | solution.py:171
  149.5 9.2 %collective-permute-start.20 = (bf16[256,1024]{1,0:T(8,128)(2,1)S(1)}, bf16[256,1024]{1,0:T(8,128)(2,1)S(1)}, u32[]{:S(2)}, u32[]{:S(2)}) collective-permute-start(bf16[256,1024]{1,0:T(8,128)(2,1)S(1)} %collective-permute-done.19), channel_id=1, source_target_pairs={{0,1},{1,0},{2,3},{3,2},{4,5},{5,4},{6,7},{7,6},{8,9},{9,8},{10,11... | collective-permute-start | bytes 1572872 | tf_op jit(solution)/shard_map/ppermute | solution.py:171
  149.5 9.4 %collective-permute-start.30 = (bf16[128,768]{0,1:T(8,128)(2,1)S(1)}, bf16[128,768]{0,1:T(8,128)(2,1)S(1)}, u32[]{:S(2)}, u32[]{:S(2)}) collective-permute-start(bf16[128,768]{0,1:T(8,128)(2,1)S(1)} %slice.154), channel_id=1, source_target_pairs={{0,8},{8,0},{16,24},{24,16},{1,9},{9,1},{17,25},{25,17},{2,10},{10... | collective-permute-start | bytes 589832 | tf_op jit(solution)/shard_map/ppermute | solution.py:225
  158.8 8.2 %collective-permute-start.21 = (bf16[512,1024]{1,0:T(8,128)(2,1)S(1)}, bf16[512,1024]{1,0:T(8,128)(2,1)S(1)}, u32[]{:S(2)}, u32[]{:S(2)}) collective-permute-start(bf16[512,1024]{1,0:T(8,128)(2,1)S(1)} %pad_maximum_fusion.9), channel_id=1, source_target_pairs={{0,4},{4,0},{1,5},{5,1},{2,6},{6,2},{3,7},{7,3},{8,12},{12,8},{9,1... | collective-permute-start | bytes 3145736 | tf_op jit(solution)/shard_map/ppermute | solution.py:171
  180.7 9.8 %collective-permute-start.32 = (bf16[512,1024]{1,0:T(8,128)(2,1)}, bf16[512,1024]{1,0:T(8,128)(2,1)}, u32[]{:S(2)}, u32[]{:S(2)}) collective-permute-start(bf16[512,1024]{1,0:T(8,128)(2,1)} %dynamic_slice.171), channel_id=1, source_target_pairs={{0,4},{4,0},{1,5},{5,1},{2,6},{6,2},{3,7},{7,3},{8,12},{12,8},{9,1... | collective-permute-start | bytes 3145736 | tf_op jit(solution)/shard_map/ppermute | solution.py:171
  182.0 27.9 %collective-permute-start.37 = (bf16[128,768]{1,0:T(8,128)(2,1)S(1)}, bf16[128,768]{1,0:T(8,128)(2,1)S(1)}, u32[]{:S(2)}, u32[]{:S(2)}) collective-permute-start(bf16[128,768]{1,0:T(8,128)(2,1)S(1)} %get-tuple-element.304), channel_id=1, source_target_pairs={{0,8},{8,0},{16,24},{24,16},{1,9},{9,1},{17,25},{25,17},{2,10},{10... | collective-permute-start | bytes 589832 | tf_op jit(solution)/shard_map/ppermute | solution.py:225
  183.0 26.8 %collective-permute-start.35 = (bf16[128,768]{1,0:T(8,128)(2,1)S(1)}, bf16[128,768]{1,0:T(8,128)(2,1)S(1)}, u32[]{:S(2)}, u32[]{:S(2)}) collective-permute-start(bf16[128,768]{1,0:T(8,128)(2,1)S(1)} %get-tuple-element.305), channel_id=1, source_target_pairs={{0,16},{8,24},{16,0},{24,8},{1,17},{9,25},{17,1},{25,9},{2,18},{10... | collective-permute-start | bytes 589832 | tf_op jit(solution)/shard_map/ppermute | solution.py:225
  192.3 13.8 %collective-permute-start.33 = (bf16[256,1024]{1,0:T(8,128)(2,1)S(1)}, bf16[256,1024]{1,0:T(8,128)(2,1)S(1)}, u32[]{:S(2)}, u32[]{:S(2)}) collective-permute-start(bf16[256,1024]{1,0:T(8,128)(2,1)S(1)} %dynamic_slice.216), channel_id=1, source_target_pairs={{0,1},{1,0},{2,3},{3,2},{4,5},{5,4},{6,7},{7,6},{8,9},{9,8},{10,11... | collective-permute-start | bytes 1572872 | tf_op jit(solution)/shard_map/ppermute | solution.py:171
  207.9 12.9 %collective-permute-start.34 = (bf16[256,1024]{1,0:T(8,128)(2,1)S(1)}, bf16[256,1024]{1,0:T(8,128)(2,1)S(1)}, u32[]{:S(2)}, u32[]{:S(2)}) collective-permute-start(bf16[256,1024]{1,0:T(8,128)(2,1)S(1)} %get-tuple-element.283), channel_id=1, source_target_pairs={{0,1},{1,0},{2,3},{3,2},{4,5},{5,4},{6,7},{7,6},{8,9},{9,8},{10,11... | collective-permute-start | bytes 1572872 | tf_op jit(solution)/shard_map/ppermute | solution.py:171
  208.2 18.9 %collective-permute-start.42 = (bf16[128,1536]{1,0:T(8,128)(2,1)S(1)}, bf16[128,1536]{1,0:T(8,128)(2,1)S(1)}, u32[]{:S(2)}, u32[]{:S(2)}) collective-permute-start(bf16[128,1536]{1,0:T(8,128)(2,1)S(1)} %get-tuple-element.289), channel_id=1, source_target_pairs={{0,8},{8,0},{16,24},{24,16},{1,9},{9,1},{17,25},{25,17},{2,10},{10... | collective-permute-start | bytes 1179656 | tf_op jit(solution)/shard_map/ppermute | solution.py:225
  208.8 18.3 %collective-permute-start.40 = (bf16[128,1536]{1,0:T(8,128)(2,1)S(1)}, bf16[128,1536]{1,0:T(8,128)(2,1)S(1)}, u32[]{:S(2)}, u32[]{:S(2)}) collective-permute-start(bf16[128,1536]{1,0:T(8,128)(2,1)S(1)} %get-tuple-element.290), channel_id=1, source_target_pairs={{0,16},{8,24},{16,0},{24,8},{1,17},{9,25},{17,1},{25,9},{2,18},{10... | collective-permute-start | bytes 1179656 | tf_op jit(solution)/shard_map/ppermute | solution.py:225
  210.0 16.9 %collective-permute-start.36 = (bf16[256,768]{1,0:T(8,128)(2,1)S(1)}, bf16[256,768]{1,0:T(8,128)(2,1)S(1)}, u32[]{:S(2)}, u32[]{:S(2)}) collective-permute-start(bf16[256,768]{1,0:T(8,128)(2,1)S(1)} %pad_maximum_fusion.21), channel_id=1, source_target_pairs={{0,8},{8,0},{16,24},{24,16},{1,9},{9,1},{17,25},{25,17},{2,10},{10... | collective-permute-start | bytes 1179656 | tf_op jit(solution)/shard_map/ppermute | solution.py:225
  211.2 15.9 %collective-permute-start.38 = (bf16[256,768]{1,0:T(8,128)(2,1)S(1)}, bf16[256,768]{1,0:T(8,128)(2,1)S(1)}, u32[]{:S(2)}, u32[]{:S(2)}) collective-permute-start(bf16[256,768]{1,0:T(8,128)(2,1)S(1)} %pad_maximum_fusion.22), channel_id=1, source_target_pairs={{0,16},{8,24},{16,0},{24,8},{1,17},{9,25},{17,1},{25,9},{2,18},{10... | collective-permute-start | bytes 1179656 | tf_op jit(solution)/shard_map/ppermute | solution.py:225
  227.4 28.3 %collective-permute-start.41 = (bf16[256,1536]{1,0:T(8,128)(2,1)S(1)}, bf16[256,1536]{1,0:T(8,128)(2,1)S(1)}, u32[]{:S(2)}, u32[]{:S(2)}) collective-permute-start(bf16[256,1536]{1,0:T(8,128)(2,1)S(1)} %pad_maximum_fusion.13), channel_id=1, source_target_pairs={{0,8},{8,0},{16,24},{24,16},{1,9},{9,1},{17,25},{25,17},{2,10},{10... | collective-permute-start | bytes 2359304 | tf_op jit(solution)/shard_map/ppermute | solution.py:225
  229.0 26.7 %collective-permute-start.43 = (bf16[256,1536]{1,0:T(8,128)(2,1)S(1)}, bf16[256,1536]{1,0:T(8,128)(2,1)S(1)}, u32[]{:S(2)}, u32[]{:S(2)}) collective-permute-start(bf16[256,1536]{1,0:T(8,128)(2,1)S(1)} %pad_maximum_fusion.14), channel_id=1, source_target_pairs={{0,16},{8,24},{16,0},{24,8},{1,17},{9,25},{17,1},{25,9},{2,18},{10... | collective-permute-start | bytes 2359304 | tf_op jit(solution)/shard_map/ppermute | solution.py:225
  229.9 25.8 %collective-permute-start.44 = (bf16[256,768]{1,0:T(8,128)(2,1)S(1)}, bf16[256,768]{1,0:T(8,128)(2,1)S(1)}, u32[]{:S(2)}, u32[]{:S(2)}) collective-permute-start(bf16[256,768]{1,0:T(8,128)(2,1)S(1)} %add_convert_fusion.3), channel_id=1, source_target_pairs={{0,0},{2,4},{4,2},{6,6},{1,1},{3,5},{5,3},{7,7},{8,8},{10,12},{12,... | collective-permute-start | bytes 1179656 | tf_op jit(solution)/shard_map/ppermute | solution.py:167
  233.6 22.2 %collective-permute-start.45 = (bf16[128,512]{1,0:T(8,128)(2,1)S(1)}, bf16[128,512]{1,0:T(8,128)(2,1)S(1)}, u32[]{:S(2)}, u32[]{:S(2)}) collective-permute-start(bf16[128,512]{1,0:T(8,128)(2,1)S(1)} %get-tuple-element.313), channel_id=1, source_target_pairs={{0,16},{8,24},{16,0},{24,8},{1,17},{9,25},{17,1},{25,9},{2,18},{10... | collective-permute-start | bytes 393224 | tf_op jit(solution)/shard_map/ppermute | solution.py:225
  235.0 20.7 %collective-permute-start.46 = (bf16[128,512]{1,0:T(8,128)(2,1)S(1)}, bf16[128,512]{1,0:T(8,128)(2,1)S(1)}, u32[]{:S(2)}, u32[]{:S(2)}) collective-permute-start(bf16[128,512]{1,0:T(8,128)(2,1)S(1)} %get-tuple-element.312), channel_id=1, source_target_pairs={{0,8},{8,0},{16,24},{24,16},{1,9},{9,1},{17,25},{25,17},{2,10},{10... | collective-permute-start | bytes 393224 | tf_op jit(solution)/shard_map/ppermute | solution.py:225
  261.1 11.5 %collective-permute-start.48 = (bf16[128,1024]{1,0:T(8,128)(2,1)S(1)}, bf16[128,1024]{1,0:T(8,128)(2,1)S(1)}, u32[]{:S(2)}, u32[]{:S(2)}) collective-permute-start(bf16[128,1024]{1,0:T(8,128)(2,1)S(1)} %get-tuple-element.293), channel_id=1, source_target_pairs={{0,8},{8,0},{16,24},{24,16},{1,9},{9,1},{17,25},{25,17},{2,10},{10... | collective-permute-start | bytes 786440 | tf_op jit(solution)/shard_map/ppermute | solution.py:225
  262.3 11.4 %collective-permute-start.49 = (bf16[256,512]{1,0:T(8,128)(2,1)S(1)}, bf16[256,512]{1,0:T(8,128)(2,1)S(1)}, u32[]{:S(2)}, u32[]{:S(2)}) collective-permute-start(bf16[256,512]{1,0:T(8,128)(2,1)S(1)} %pad_maximum_fusion.25), channel_id=1, source_target_pairs={{0,8},{8,0},{16,24},{24,16},{1,9},{9,1},{17,25},{25,17},{2,10},{10... | collective-permute-start | bytes 786440 | tf_op jit(solution)/shard_map/ppermute | solution.py:225
  263.4 10.3 %collective-permute-start.50 = (bf16[256,512]{1,0:T(8,128)(2,1)S(1)}, bf16[256,512]{1,0:T(8,128)(2,1)S(1)}, u32[]{:S(2)}, u32[]{:S(2)}) collective-permute-start(bf16[256,512]{1,0:T(8,128)(2,1)S(1)} %pad_maximum_fusion.26), channel_id=1, source_target_pairs={{0,16},{8,24},{16,0},{24,8},{1,17},{9,25},{17,1},{25,9},{2,18},{10... | collective-permute-start | bytes 786440 | tf_op jit(solution)/shard_map/ppermute | solution.py:225
  264.7 30.5 %collective-permute-start.53 = (bf16[256,1536]{1,0:T(8,128)(2,1)S(1)}, bf16[256,1536]{1,0:T(8,128)(2,1)S(1)}, u32[]{:S(2)}, u32[]{:S(2)}) collective-permute-start(bf16[256,1536]{1,0:T(8,128)(2,1)S(1)} %add_convert_fusion), channel_id=1, source_target_pairs={{0,0},{2,4},{4,2},{6,6},{1,1},{3,5},{5,3},{7,7},{8,8},{10,12},{12,... | collective-permute-start | bytes 2359304 | tf_op jit(solution)/shard_map/ppermute | solution.py:167
  267.5 32.5 %collective-permute-start.57 = (bf16[512,1024]{1,0:T(8,128)(2,1)S(1)}, bf16[512,1024]{1,0:T(8,128)(2,1)S(1)}, u32[]{:S(2)}, u32[]{:S(2)}) collective-permute-start(bf16[512,1024]{1,0:T(8,128)(2,1)S(1)} %dynamic_slice.175), channel_id=1, source_target_pairs={{0,4},{4,0},{1,5},{5,1},{2,6},{6,2},{3,7},{7,3},{8,12},{12,8},{9,1... | collective-permute-start | bytes 3145736 | tf_op jit(solution)/shard_map/ppermute | solution.py:171
  273.8 21.3 %collective-permute-start.51 = (bf16[256,1024]{1,0:T(8,128)(2,1)S(1)}, bf16[256,1024]{1,0:T(8,128)(2,1)S(1)}, u32[]{:S(2)}, u32[]{:S(2)}) collective-permute-start(bf16[256,1024]{1,0:T(8,128)(2,1)S(1)} %pad_maximum_fusion.19), channel_id=1, source_target_pairs={{0,8},{8,0},{16,24},{24,16},{1,9},{9,1},{17,25},{25,17},{2,10},{10... | collective-permute-start | bytes 1572872 | tf_op jit(solution)/shard_map/ppermute | solution.py:225
  275.8 19.4 %collective-permute-start.52 = (bf16[256,1024]{1,0:T(8,128)(2,1)S(1)}, bf16[256,1024]{1,0:T(8,128)(2,1)S(1)}, u32[]{:S(2)}, u32[]{:S(2)}) collective-permute-start(bf16[256,1024]{1,0:T(8,128)(2,1)S(1)} %pad_maximum_fusion.20), channel_id=1, source_target_pairs={{0,16},{8,24},{16,0},{24,8},{1,17},{9,25},{17,1},{25,9},{2,18},{10... | collective-permute-start | bytes 1572872 | tf_op jit(solution)/shard_map/ppermute | solution.py:225
  281.4 20.2 %collective-permute-start.56 = (bf16[512,1024]{1,0:T(8,128)(2,1)S(1)}, bf16[512,1024]{1,0:T(8,128)(2,1)S(1)}, u32[]{:S(2)}, u32[]{:S(2)}) collective-permute-start(bf16[512,1024]{1,0:T(8,128)(2,1)S(1)} %constant_dynamic-slice_fusion.10), channel_id=1, source_target_pairs={{0,4},{4,0},{1,5},{5,1},{2,6},{6,2},{3,7},{7,3},{8,12},{12,8},{9,1... | collective-permute-start | bytes 3145736 | tf_op jit(solution)/shard_map/ppermute | solution.py:171
  297.5 14.9 %collective-permute-start.60 = (bf16[128,1536]{1,0:T(8,128)(2,1)S(1)}, bf16[128,1536]{1,0:T(8,128)(2,1)S(1)}, u32[]{:S(2)}, u32[]{:S(2)}) collective-permute-start(bf16[128,1536]{1,0:T(8,128)(2,1)S(1)} %constant_dynamic-slice_fusion.7), channel_id=1, source_target_pairs={{0,4},{4,0},{1,5},{5,1},{2,6},{6,2},{3,7},{7,3},{8,12},{12,8},{9,1... | collective-permute-start | bytes 1179656 | tf_op jit(solution)/shard_map/ppermute | solution.py:171
  302.2 11.3 %collective-permute-start.58 = (bf16[128,1024]{1,0:T(8,128)(2,1)S(1)}, bf16[128,1024]{1,0:T(8,128)(2,1)S(1)}, u32[]{:S(2)}, u32[]{:S(2)}) collective-permute-start(bf16[128,1024]{1,0:T(8,128)(2,1)S(1)} %constant_dynamic-slice_fusion.9), channel_id=1, source_target_pairs={{0,4},{4,0},{1,5},{5,1},{2,6},{6,2},{3,7},{7,3},{8,12},{12,8},{9,1... | collective-permute-start | bytes 786440 | tf_op jit(solution)/shard_map/ppermute | solution.py:171
  316.6 25.3 %all-to-all-start = ((bf16[8,128,768]{2,1,0:T(8,128)(2,1)}), bf16[8,128,768]{2,1,0:T(8,128)(2,1)}, u32[]{:S(2)}, u32[]{:S(2)}) async-start(bf16[8,128,768]{2,1,0:T(8,128)(2,1)} %get-tuple-element.214), calls=%async_computation | async-start | bytes 3145728 | tf_op jit(solution)/shard_map/all_to_all | solution.py:604
  321.0 14.8 %collective-permute-start.62 = (bf16[256,1024]{1,0:T(8,128)(2,1)S(1)}, bf16[256,1024]{1,0:T(8,128)(2,1)S(1)}, u32[]{:S(2)}, u32[]{:S(2)}) collective-permute-start(bf16[256,1024]{1,0:T(8,128)(2,1)S(1)} %dynamic-slice_convert_fusion), channel_id=1, source_target_pairs={{0,1},{1,0},{2,3},{3,2},{4,5},{5,4},{6,7},{7,6},{8,9},{9,8},{10,11... | collective-permute-start | bytes 1572872 | tf_op jit(solution)/shard_map/ppermute | solution.py:171
  322.4 25.9 %collective-permute-start.66 = (bf16[256,1024]{1,0:T(8,128)(2,1)S(1)}, bf16[256,1024]{1,0:T(8,128)(2,1)}, u32[]{:S(2)}, u32[]{:S(2)}) collective-permute-start(bf16[256,1024]{1,0:T(8,128)(2,1)S(1)} %dynamic_slice.215), channel_id=1, source_target_pairs={{0,1},{1,0},{2,3},{3,2},{4,5},{5,4},{6,7},{7,6},{8,9},{9,8},{10,11... | collective-permute-start | bytes 1572872 | tf_op jit(solution)/shard_map/ppermute | solution.py:171
  341.9 17.2 %collective-permute-start.63 = (bf16[1024,768]{1,0:T(8,128)(2,1)}, bf16[1024,768]{1,0:T(8,128)(2,1)}, u32[]{:S(2)}, u32[]{:S(2)}) collective-permute-start(bf16[1024,768]{1,0:T(8,128)(2,1)} %bitcast.6.refs_0_), channel_id=1, source_target_pairs={{2,1},{7,6},{10,9},{15,14},{18,17},{23,22},{31,30}} | collective-permute-start | bytes 4718600 | tf_op jit(solution)/shard_map/ppermute | solution.py:610
  343.7 15.4 %collective-permute-start.64 = (bf16[1024,768]{1,0:T(8,128)(2,1)}, bf16[1024,768]{1,0:T(8,128)(2,1)}, u32[]{:S(2)}, u32[]{:S(2)}) collective-permute-start(bf16[1024,768]{1,0:T(8,128)(2,1)} %bitcast.6.refs_0_), channel_id=1, source_target_pairs={{3,1},{4,6},{11,9},{12,14},{19,17},{20,22},{28,30}} | collective-permute-start | bytes 4718600 | tf_op jit(solution)/shard_map/ppermute | solution.py:610
  345.6 32.5 %collective-permute-start.65 = (bf16[1024,768]{1,0:T(8,128)(2,1)}, bf16[1024,768]{1,0:T(8,128)(2,1)}, u32[]{:S(2)}, u32[]{:S(2)}) collective-permute-start(bf16[1024,768]{1,0:T(8,128)(2,1)} %bitcast.6.refs_0_), channel_id=1, source_target_pairs={{0,1},{5,6},{8,9},{13,14},{16,17},{21,22},{29,30}} | collective-permute-start | bytes 4718600 | tf_op jit(solution)/shard_map/ppermute | solution.py:610
  385.6 87.1 %collective-permute-start.74 = (bf16[1024,384]{1,0:T(8,128)(2,1)S(1)}, bf16[1024,384]{1,0:T(8,128)(2,1)S(1)}, u32[]{:S(2)}, u32[]{:S(2)}) collective-permute-start(bf16[1024,384]{1,0:T(8,128)(2,1)S(1)} %get-tuple-element.254), channel_id=1, source_target_pairs={{1,0},{6,5},{9,8},{14,13},{17,16},{22,21},{30,29}} | collective-permute-start | bytes 2359304 | tf_op jit(solution)/shard_map/ppermute | solution.py:620
  386.9 87.4 %collective-permute-start.73 = (bf16[1024,384]{1,0:T(8,128)(2,1)S(1)}, bf16[1024,384]{1,0:T(8,128)(2,1)S(1)}, u32[]{:S(2)}, u32[]{:S(2)}) collective-permute-start(bf16[1024,384]{1,0:T(8,128)(2,1)S(1)} %get-tuple-element.253), channel_id=1, source_target_pairs={{1,3},{6,4},{9,11},{14,12},{17,19},{22,20},{30,28}} | collective-permute-start | bytes 2359304 | tf_op jit(solution)/shard_map/ppermute | solution.py:620
  387.6 86.7 %collective-permute-start.72 = (bf16[1024,384]{1,0:T(8,128)(2,1)S(1)}, bf16[1024,384]{1,0:T(8,128)(2,1)S(1)}, u32[]{:S(2)}, u32[]{:S(2)}) collective-permute-start(bf16[1024,384]{1,0:T(8,128)(2,1)S(1)} %get-tuple-element.252), channel_id=1, source_target_pairs={{1,2},{6,7},{9,10},{14,15},{17,18},{22,23},{30,31}} | collective-permute-start | bytes 2359304 | tf_op jit(solution)/shard_map/ppermute | solution.py:620
  388.4 101.4 %collective-permute-start.77 = (bf16[1024,384]{1,0:T(8,128)(2,1)}, bf16[1024,384]{1,0:T(8,128)(2,1)}, u32[]{:S(2)}, u32[]{:S(2)}) collective-permute-start(bf16[1024,384]{1,0:T(8,128)(2,1)} %get-tuple-element.258), channel_id=1, source_target_pairs={{1,0},{6,5},{9,8},{14,13},{17,16},{22,21},{30,29}} | collective-permute-start | bytes 2359304 | tf_op jit(solution)/shard_map/ppermute | solution.py:620
  389.7 100.1 %collective-permute-start.76 = (bf16[1024,384]{1,0:T(8,128)(2,1)S(1)}, bf16[1024,384]{1,0:T(8,128)(2,1)}, u32[]{:S(2)}, u32[]{:S(2)}) collective-permute-start(bf16[1024,384]{1,0:T(8,128)(2,1)S(1)} %get-tuple-element.257), channel_id=1, source_target_pairs={{1,3},{6,4},{9,11},{14,12},{17,19},{22,20},{30,28}} | collective-permute-start | bytes 2359304 | tf_op jit(solution)/shard_map/ppermute | solution.py:620
  472.8 17.0 %collective-permute-start.75 = (bf16[1024,384]{1,0:T(8,128)(2,1)S(1)}, bf16[1024,384]{1,0:T(8,128)(2,1)}, u32[]{:S(2)}, u32[]{:S(2)}) collective-permute-start(bf16[1024,384]{1,0:T(8,128)(2,1)S(1)} %get-tuple-element.256), channel_id=1, source_target_pairs={{1,2},{6,7},{9,10},{14,15},{17,18},{22,23},{30,31}} | collective-permute-start | bytes 2359304 | tf_op jit(solution)/shard_map/ppermute | solution.py:620
  475.4 17.0 %all-to-all-start.1 = ((bf16[8,128,384]{2,1,0:T(8,128)(2,1)}), bf16[8,128,384]{2,1,0:T(8,128)(2,1)S(1)}, u32[]{:S(2)}, u32[]{:S(2)}) async-start(bf16[8,128,384]{2,1,0:T(8,128)(2,1)} %bitcast.37), calls=%async_computation.1 | async-start | bytes 1572864 | tf_op jit(solution)/shard_map/all_to_all | solution.py:626
  492.5 16.2 %all-to-all-start.2 = ((bf16[8,128,384]{2,1,0:T(8,128)(2,1)}), bf16[8,128,384]{2,1,0:T(8,128)(2,1)S(1)}, u32[]{:S(2)}, u32[]{:S(2)}) async-start(bf16[8,128,384]{2,1,0:T(8,128)(2,1)} %bitcast.36), calls=%async_computation.2 | async-start | bytes 1572864 | tf_op jit(solution)/shard_map/all_to_all | solution.py:626
  (78 other events, 698.2 us)
